TPU v7x, 32 devices: a whole 2x2x4 slice. The times are simulated.
32 devices in a mesh: replica: 4 (over x, core), shard: 8 (over z, y).
Axes of the slice: x: 2, y: 2, z: 4, core: 2. Of those that a mesh axis runs over, the one named last changes fastest.
Arguments:
- tokens: bfloat16 [4096, 768], P(('replica', 'shard')), may hold values from -6 to 6
- lengths: int32 [32, 4], P(('replica', 'shard')), may hold values from 0 to 128, as said below
- qkv_weight: bfloat16 [768, 2304], P('shard'), may hold values from -0.21875 to 0.21875
- qv_bias: bfloat16 [1536], P('shard'), may hold values from -3 to 3
- out_weight: bfloat16 [768, 768], P('shard'), may hold values from -0.875 to 0.875
- out_bias: bfloat16 [768], P('shard'), may hold values from -2 to 2
- first_gain: bfloat16 [768], P('shard'), may hold values from 0.5 to 1.5
- first_shift: bfloat16 [768], P('shard'), may hold values from -2 to 2
- up_weight: bfloat16 [768, 3072], P('shard'), may hold values from -0.21875 to 0.21875
- up_bias: bfloat16 [3072], P('shard'), may hold values from -3 to 3
- down_weight: bfloat16 [3072, 768], P('shard'), may hold values from -0.109375 to 0.109375
- down_bias: bfloat16 [768], P('shard'), may hold values from -2 to 2
- second_gain: bfloat16 [768], P('shard'), may hold values from 0.5 to 1.5
- second_shift: bfloat16 [768], P('shard'), may hold values from -2 to 2
- cotangent: bfloat16 [4096, 768], P(('replica', 'shard')), may hold values from -6 to 6
Outputs:
- layer_out: bfloat16 [4096, 768], P(('replica', 'shard'))
- grad_tokens: bfloat16 [4096, 768], P(('replica', 'shard'))
- d_qkv_weight: float32 [768, 2304], P('shard')
- d_qv_bias: float32 [1536], P('shard')
- d_out_weight: float32 [768, 768], P('shard')
- d_out_bias: float32 [768], P('shard')
- d_first_gain: float32 [768], P('shard')
- d_first_shift: float32 [768], P('shard')
- d_up_weight: float32 [768, 3072], P('shard')
- d_up_bias: float32 [3072], P('shard')
- d_down_weight: float32 [3072, 768], P('shard')
- d_down_bias: float32 [768], P('shard')
- d_second_gain: float32 [768], P('shard')
- d_second_shift: float32 [768], P('shard')
Inputs may be any that keep to these rules, and one draw needn't show every extreme that they name: Row b holds the lengths of the 4 sequences packed in order into token block b; a row sums to at most 128, and the slots after its sum are padding. Zero lengths occur. In every draw some row is one sequence of 128 tokens followed by empty ones.
All inputs are finite; a program needn't handle non-finite values.
Results may differ from a plain program's by a relative error of at most 0.018.
Values may be sent and summed in bfloat16 or wider, within the bound.
No kernel may reach another device: no remote copies, remote signals or barrier semaphores. Data moves between devices by JAX's collectives and lax.ppermute only.
A program may use at most 128 MiB of HBM per device.

v0:
```python
from functools import partial

import jax
import jax.numpy as jnp
from jax import lax
from jax.sharding import PartitionSpec as P

HEADS = 12


EPSILON = 1e-05
NEG_FILL = -1e30


def layout(length_row, row_count):
    bounds = jnp.cumsum(length_row)
    places = jnp.arange(row_count, dtype=jnp.int32)
    segment = jnp.sum((places[:, None] >= bounds[None, :]).astype(jnp.int32), axis=1)
    usable = places < bounds[-1]
    segment_id = jnp.where(usable, segment, length_row.shape[0] + places)
    return (segment_id, usable)


def matmul(left_side, right_side):
    return jnp.dot(left_side, right_side, preferred_element_type=jnp.float32)


def matmul_tn(left_side, right_side):
    return lax.dot_general(
        left_side, right_side, (((0,), (0,)), ((), ())), preferred_element_type=jnp.float32
    )


def matmul_nt(left_side, right_side):
    return lax.dot_general(
        left_side, right_side, (((1,), (1,)), ((), ())), preferred_element_type=jnp.float32
    )


def normalize(residual, norm_gain, norm_shift):
    center = residual - jnp.mean(residual, axis=1, keepdims=True)
    inverse = lax.rsqrt(jnp.mean(center * center, axis=1, keepdims=True) + EPSILON)
    normed = center * inverse
    return (normed * norm_gain + norm_shift, normed, inverse)


def normalize_back(grad_out, normed, inverse, norm_gain):
    scaled = grad_out * norm_gain
    grad_in = inverse * (
        scaled
        - jnp.mean(scaled, axis=1, keepdims=True)
        - normed * jnp.mean(scaled * normed, axis=1, keepdims=True)
    )
    return (grad_in, jnp.sum(grad_out * normed, axis=0), jnp.sum(grad_out, axis=0))


def split_heads(tensor):
    return tensor.reshape((tensor.shape[0], HEADS, tensor.shape[1] // HEADS))


def masked_scores(queries, key_rows, same_segment):
    scale_factor = (queries.shape[1] // HEADS) ** (-0.5)
    scores = (
        jnp.einsum(
            "qhd,khd->hqk",
            split_heads(queries),
            split_heads(key_rows),
            preferred_element_type=jnp.float32,
        )
        * scale_factor
    )
    return jnp.where(same_segment[None], scores, NEG_FILL)


def attend(queries, key_rows, values, same_segment):
    masked = masked_scores(queries, key_rows, same_segment)
    highest = jnp.max(masked, axis=2, keepdims=True)
    weights = jnp.exp(masked - highest)
    total = jnp.sum(weights, axis=2, keepdims=True)
    log_total = highest + jnp.log(total)
    attn_probs = (weights / total).astype(jnp.bfloat16)
    context = jnp.einsum(
        "hqk,khd->qhd", attn_probs, split_heads(values), preferred_element_type=jnp.float32
    )
    return (context.reshape(queries.shape).astype(jnp.bfloat16), log_total)


def attend_back(grad_context, queries, key_rows, values, same_segment, log_total):
    scale_factor = (queries.shape[1] // HEADS) ** (-0.5)
    masked = masked_scores(queries, key_rows, same_segment)
    attn_probs = jnp.exp(masked - log_total)
    probs_low = attn_probs.astype(jnp.bfloat16)
    grad_heads = split_heads(grad_context)
    grad_probs = jnp.einsum(
        "qhd,khd->hqk", grad_heads, split_heads(values), preferred_element_type=jnp.float32
    )
    grad_values = jnp.einsum(
        "hqk,qhd->khd", probs_low, grad_heads, preferred_element_type=jnp.float32
    )
    inner = jnp.sum(attn_probs * grad_probs, axis=2, keepdims=True)
    grad_scores = (attn_probs * (grad_probs - inner)).astype(jnp.bfloat16)
    grad_queries = (
        jnp.einsum(
            "hqk,khd->qhd", grad_scores, split_heads(key_rows), preferred_element_type=jnp.float32
        )
        * scale_factor
    )
    grad_keys = (
        jnp.einsum(
            "hqk,qhd->khd", grad_scores, split_heads(queries), preferred_element_type=jnp.float32
        )
        * scale_factor
    )
    shape_flat = queries.shape
    return (
        grad_queries.reshape(shape_flat).astype(jnp.bfloat16),
        grad_keys.reshape(shape_flat).astype(jnp.bfloat16),
        grad_values.reshape(shape_flat).astype(jnp.bfloat16),
    )


def on_device(
    tokens,
    lengths,
    qkv_weight,
    qv_bias,
    out_weight,
    out_bias,
    first_gain,
    first_shift,
    up_weight,
    up_bias,
    down_weight,
    down_bias,
    second_gain,
    second_shift,
    cotangent,
):
    model_width = tokens.shape[1]
    segment_id, usable = layout(lengths[0], tokens.shape[0])
    same_segment = segment_id[:, None] == segment_id[None, :]
    keep_rows = usable.astype(jnp.float32)[:, None]
    w_qkv, b_qv, w_out, b_out, gain_one, shift_one = (
        lax.all_gather(qkv_weight, "shard", axis=0, tiled=True),
        lax.all_gather(qv_bias, "shard", axis=0, tiled=True),
        lax.all_gather(out_weight, "shard", axis=0, tiled=True),
        lax.all_gather(out_bias, "shard", axis=0, tiled=True),
        lax.all_gather(first_gain, "shard", axis=0, tiled=True),
        lax.all_gather(first_shift, "shard", axis=0, tiled=True),
    )
    projected = matmul(tokens, w_qkv)
    bias_full = b_qv.astype(jnp.float32)
    queries = (projected[:, :model_width] + bias_full[:model_width]).astype(jnp.bfloat16)
    key_rows = projected[:, model_width : 2 * model_width].astype(jnp.bfloat16)
    values = (projected[:, 2 * model_width :] + bias_full[model_width:]).astype(jnp.bfloat16)
    context, log_total = attend(queries, key_rows, values, same_segment)
    attn_out = matmul(context, w_out) + b_out.astype(jnp.float32)
    gain_first = gain_one.astype(jnp.float32)
    hidden, normed_one, inverse_one = normalize(
        tokens.astype(jnp.float32) + attn_out, gain_first, shift_one.astype(jnp.float32)
    )
    hidden_low = hidden.astype(jnp.bfloat16)
    w_up, b_up, w_down, b_down, gain_two, shift_two = (
        lax.all_gather(up_weight, "shard", axis=0, tiled=True),
        lax.all_gather(up_bias, "shard", axis=0, tiled=True),
        lax.all_gather(down_weight, "shard", axis=0, tiled=True),
        lax.all_gather(down_bias, "shard", axis=0, tiled=True),
        lax.all_gather(second_gain, "shard", axis=0, tiled=True),
        lax.all_gather(second_shift, "shard", axis=0, tiled=True),
    )
    pre_act = matmul(hidden_low, w_up) + b_up.astype(jnp.float32)
    activated = jax.nn.gelu(pre_act, approximate=False).astype(jnp.bfloat16)
    branch = matmul(activated, w_down) + b_down.astype(jnp.float32)
    gain_second = gain_two.astype(jnp.float32)
    output_full, normed_two, inverse_two = normalize(
        hidden + branch, gain_second, shift_two.astype(jnp.float32)
    )
    layer_out = (output_full * keep_rows).astype(jnp.bfloat16)
    grad_out = cotangent.astype(jnp.float32) * keep_rows
    grad_second, grad_gain_two, grad_shift_two = normalize_back(
        grad_out, normed_two, inverse_two, gain_second
    )
    back_up, back_down = (w_up, w_down)
    grad_branch = grad_second.astype(jnp.bfloat16)
    grad_w_down = matmul_tn(activated, grad_branch)
    grad_b_down = jnp.sum(grad_branch.astype(jnp.float32), axis=0)
    grad_act = matmul_nt(grad_branch, back_down)
    gelu_value, gelu_pull = jax.vjp(partial(jax.nn.gelu, approximate=False), pre_act)
    grad_pre = gelu_pull(grad_act)[0].astype(jnp.bfloat16)
    grad_w_up = matmul_tn(hidden_low, grad_pre)
    grad_b_up = jnp.sum(grad_pre.astype(jnp.float32), axis=0)
    grad_hidden = grad_second + matmul_nt(grad_pre, back_up)
    ffn_shares = (
        lax.psum_scatter(
            grad_w_up.astype(jnp.bfloat16), "shard", scatter_dimension=0, tiled=True
        ).astype(jnp.float32),
        lax.psum_scatter(
            grad_b_up.astype(jnp.bfloat16), "shard", scatter_dimension=0, tiled=True
        ).astype(jnp.float32),
        lax.psum_scatter(
            grad_w_down.astype(jnp.bfloat16), "shard", scatter_dimension=0, tiled=True
        ).astype(jnp.float32),
        lax.psum_scatter(
            grad_b_down.astype(jnp.bfloat16), "shard", scatter_dimension=0, tiled=True
        ).astype(jnp.float32),
        lax.psum_scatter(
            grad_gain_two.astype(jnp.bfloat16), "shard", scatter_dimension=0, tiled=True
        ).astype(jnp.float32),
        lax.psum_scatter(
            grad_shift_two.astype(jnp.bfloat16), "shard", scatter_dimension=0, tiled=True
        ).astype(jnp.float32),
    )
    grad_first, grad_gain_one, grad_shift_one = normalize_back(
        grad_hidden, normed_one, inverse_one, gain_first
    )
    back_qkv, back_out = (w_qkv, w_out)
    grad_attn = grad_first.astype(jnp.bfloat16)
    grad_w_out = matmul_tn(context, grad_attn)
    grad_b_out = jnp.sum(grad_attn.astype(jnp.float32), axis=0)
    grad_context = matmul_nt(grad_attn, back_out).astype(jnp.bfloat16)
    grad_queries, grad_keys, grad_values = attend_back(
        grad_context, queries, key_rows, values, same_segment, log_total
    )
    grad_proj = jnp.concatenate([grad_queries, grad_keys, grad_values], axis=1)
    grad_w_qkv = matmul_tn(tokens, grad_proj)
    grad_b_qv = jnp.concatenate(
        [
            jnp.sum(grad_queries.astype(jnp.float32), axis=0),
            jnp.sum(grad_values.astype(jnp.float32), axis=0),
        ]
    )
    grad_tokens = (grad_first + matmul_nt(grad_proj, back_qkv)).astype(jnp.bfloat16)
    attn_shares = (
        lax.psum_scatter(
            grad_w_qkv.astype(jnp.bfloat16), "shard", scatter_dimension=0, tiled=True
        ).astype(jnp.float32),
        lax.psum_scatter(
            grad_b_qv.astype(jnp.bfloat16), "shard", scatter_dimension=0, tiled=True
        ).astype(jnp.float32),
        lax.psum_scatter(
            grad_w_out.astype(jnp.bfloat16), "shard", scatter_dimension=0, tiled=True
        ).astype(jnp.float32),
        lax.psum_scatter(
            grad_b_out.astype(jnp.bfloat16), "shard", scatter_dimension=0, tiled=True
        ).astype(jnp.float32),
        lax.psum_scatter(
            grad_gain_one.astype(jnp.bfloat16), "shard", scatter_dimension=0, tiled=True
        ).astype(jnp.float32),
        lax.psum_scatter(
            grad_shift_one.astype(jnp.bfloat16), "shard", scatter_dimension=0, tiled=True
        ).astype(jnp.float32),
    )
    totals = (
        lax.psum(ffn_shares[0].astype(jnp.bfloat16), "replica").astype(jnp.float32),
        lax.psum(ffn_shares[1].astype(jnp.bfloat16), "replica").astype(jnp.float32),
        lax.psum(ffn_shares[2].astype(jnp.bfloat16), "replica").astype(jnp.float32),
        lax.psum(ffn_shares[3].astype(jnp.bfloat16), "replica").astype(jnp.float32),
        lax.psum(ffn_shares[4].astype(jnp.bfloat16), "replica").astype(jnp.float32),
        lax.psum(ffn_shares[5].astype(jnp.bfloat16), "replica").astype(jnp.float32),
        lax.psum(attn_shares[0].astype(jnp.bfloat16), "replica").astype(jnp.float32),
        lax.psum(attn_shares[1].astype(jnp.bfloat16), "replica").astype(jnp.float32),
        lax.psum(attn_shares[2].astype(jnp.bfloat16), "replica").astype(jnp.float32),
        lax.psum(attn_shares[3].astype(jnp.bfloat16), "replica").astype(jnp.float32),
        lax.psum(attn_shares[4].astype(jnp.bfloat16), "replica").astype(jnp.float32),
        lax.psum(attn_shares[5].astype(jnp.bfloat16), "replica").astype(jnp.float32),
    )
    return (
        layer_out,
        grad_tokens,
        totals[6],
        totals[7],
        totals[8],
        totals[9],
        totals[10],
        totals[11],
        totals[0],
        totals[1],
        totals[2],
        totals[3],
        totals[4],
        totals[5],
    )


def solution(mesh):
    placed = (
        P(("replica", "shard"), None),
        P(("replica", "shard"), None),
        P("shard", None),
        P("shard"),
        P("shard", None),
        P("shard"),
        P("shard"),
        P("shard"),
        P("shard", None),
        P("shard"),
        P("shard", None),
        P("shard"),
        P("shard"),
        P("shard"),
        P(("replica", "shard"), None),
    )
    return jax.shard_map(
        on_device,
        mesh=mesh,
        in_specs=placed,
        out_specs=(
            P(("replica", "shard"), None),
            P(("replica", "shard"), None),
            P("shard", None),
            P("shard"),
            P("shard", None),
            P("shard"),
            P("shard"),
            P("shard"),
            P("shard", None),
            P("shard"),
            P("shard", None),
            P("shard"),
            P("shard"),
            P("shard"),
        ),
        check_vma=False,
    )
```

profile of v0, /device:TPU:1, one launch (start us, length us, event | category | flops | bytes accessed | tf_op | source)
XLA Modules:
  0.0 716.0 jit_solution(8241709807723992071)
XLA Ops:
  14.3 31.4 %all-reduce.16 = (bf16[1536]{0:T(1024)(128)(2,1)S(1)}, bf16[768]{0:T(1024)(128)(2,1)S(1)}, bf16[768]{0:T(1024)(128)(2,1)S(1)}, bf16[768]{0:T(1024)(128)(2,1)S(1)...) all-reduce(bf16[1536]{0:T(1024)(128)(2,1)S(1)} %dynamic-update-slic, ...), channel_id=1, replica_groups=mesh['replica'=4,'shard'=8] {'shard'}, use_global_device_ids=true, to_apply=%add | all-reduce | flops 5376 | bytes 21504
  45.7 23.2 %all-gather = bf16[8,1,384]{2,1,0:T(2,128)(2,1)S(1)} all-gather(bf16[1,1,384]{2,1,0:T(2,128)(2,1)S(1)} %reshape.200), channel_id=1, replica_groups=mesh['replica'=4,'shard'=8] {'shard'}, dimensions={0}, use_global_device_ids=true | all-gather | bytes 6912 | tf_op jit(solution)/shard_map/all_gather | solution.py:165
  70.5 6.8 all-gather.6.cloned.1.call-done
  77.3 2.6 fusion.43
  81.3 37.5 %all-gather.8.cloned.1.call-done = bf16[768,768]{1,0:T(8,128)(2,1)} async-done(((bf16[96,768]{1,0:T(8,128)(2,1)}), bf16[768,768]{1,0:T(8,128)(2,1)}) %all-gather.8.cloned.1.call-update) | async-done | bytes 1179664 | tf_op jit(solution)/shard_map/all_gather | solution.py:146
  118.8 1.7 fusion.38
  120.8 79.2 %all-gather.10.cloned.1.call-done = bf16[768,3072]{1,0:T(8,128)(2,1)} async-done(((bf16[96,3072]{1,0:T(8,128)(2,1)}), bf16[768,3072]{1,0:T(8,128)(2,1)}) %all-gather.10.cloned.1.call-update) | async-done | bytes 4718608 | tf_op jit(solution)/shard_map/all_gather | solution.py:164
  200.0 8.4 %multiply_convert_fusion = (bf16[128,3072]{1,0:T(8,128)(2,1)S(1)}, f32[128,3072]{1,0:T(8,128)}, f32[128,3072]{1,0:T(8,128)}) fusion(f32[3072]{0:T(1024)S(1)} %bitcast.70, bf16[768,3072]{1,0:T(8,128)(2,1)} %all-gather.10.cloned.1.call-done, f32[128,768]{1,0:T(8,128)S(1)} %get-tuple-element.120, f32[768]{0:T(1024)S(1)} %convert_element_type.235, ...), kind=kOutput, calls=%fused_computation.8 | convolution fusion | flops 630423552 | bytes 9063424 | tf_op jit(solution)/shard_map/dot_general | solution.py:25
  208.4 71.7 %all-gather.12.cloned.1.call-done = bf16[3072,768]{1,0:T(8,128)(2,1)} async-done(((bf16[384,768]{1,0:T(8,128)(2,1)}), bf16[3072,768]{1,0:T(8,128)(2,1)}) %all-gather.12.cloned.1.call-update) | async-done | bytes 4718608 | tf_op jit(solution)/shard_map/all_gather | solution.py:166
  280.1 3.4 fusion.39
  285.4 2.5 fusion.42
  287.9 2.4 multiply_reduce_fusion.2
  290.2 1.5 convert_reduce_fusion.1
  291.8 1.2 convolution_convert_fusion.5
  293.0 1.7 copy.64
  294.7 2.0 fusion.40
  296.7 1.4 multiply_reduce_fusion
  299.1 2.8 fusion
  301.9 5.8 copy.73
  308.7 1.5 convolution_convert_fusion.3
  310.3 3.6 convolution_convert_fusion.1
  314.0 3.6 convolution_convert_fusion
  317.8 68.1 %reduce-scatter.13.cloned.1.call-done = bf16[96,2304]{1,0:T(8,128)(2,1)} async-done(((bf16[768,2304]{1,0:T(8,128)(2,1)}), bf16[96,2304]{1,0:T(8,128)(2,1)}) %reduce-scatter.13.cloned.1.call-update) | async-done | bytes 442384
  385.9 2.1 copy.74
  388.0 64.0 %reduce-scatter.7.cloned.1.call-done = bf16[96,768]{1,0:T(8,128)(2,1)} async-done(((bf16[768,768]{1,0:T(8,128)(2,1)}), bf16[96,768]{1,0:T(8,128)(2,1)}) %reduce-scatter.7.cloned.1.call-update) | async-done | bytes 147472 | tf_op jit(solution)/shard_map/reduce_scatter | solution.py:240
  452.0 99.4 %reduce-scatter.9.cloned.1.call-done = bf16[96,3072]{1,0:T(8,128)(2,1)} async-done(((bf16[768,3072]{1,0:T(8,128)(2,1)}), bf16[96,3072]{1,0:T(8,128)(2,1)}) %reduce-scatter.9.cloned.1.call-update) | async-done | bytes 589840 | tf_op jit(solution)/shard_map/reduce_scatter | solution.py:194
  551.5 98.7 %reduce-scatter.11.cloned.1.call-done = bf16[384,768]{1,0:T(8,128)(2,1)} async-done(((bf16[3072,768]{1,0:T(8,128)(2,1)}), bf16[384,768]{1,0:T(8,128)(2,1)}) %reduce-scatter.11.cloned.1.call-update) | async-done | bytes 589840 | tf_op jit(solution)/shard_map/reduce_scatter | solution.py:200
  652.6 28.9 %all-reduce.15 = (bf16[768]{0:T(1024)(128)(2,1)S(1)}, bf16[1536]{0:T(1024)(128)(2,1)S(1)}, bf16[768]{0:T(1024)(128)(2,1)S(1)}, bf16[768]{0:T(1024)(128)(2,1)S(1)...) all-reduce(bf16[768]{0:T(1024)(128)(2,1)S(1)} %dynamic-update-slice, ...), channel_id=1, replica_groups=mesh['replica'=4,'shard'=8] {'shard'}, use_global_device_ids=true, to_apply=%add.6 | all-reduce | flops 9984 | bytes 39936
  682.2 12.9 %all-reduce.17 = (bf16[192]{0:T(256)(128)(2,1)S(1)}, bf16[96]{0:T(256)(128)(2,1)S(1)}, bf16[96]{0:T(256)(128)(2,1)S(1)}, bf16[96]{0:T(256)(128)(2,1)S(1)}, bf16[...) all-reduce(bf16[192]{0:T(256)(128)(2,1)S(1)} %dynamic-slice.8, ...), channel_id=1, replica_groups=mesh['replica'=4,'shard'=8] {'replica'}, use_global_device_ids=true, to_apply=%region_18.19 | all-reduce | flops 1152 | bytes 4608 | tf_op jit(solution)/shard_map/psum | solution.py:261
  700.2 4.0 fusion.12
  704.2 2.3 copy.68
  707.2 1.1 convert_element_type.275
  (203 shorter events, 20.4 us)
Async XLA Ops:
  7.3 6.7 copy-start.48
  7.3 70.0 %copy-start.4 = (bf16[128,768]{1,0:T(8,128)(2,1)S(1)}, bf16[128,768]{1,0:T(8,128)(2,1)}, u32[]{:S(2)}) copy-start(bf16[128,768]{1,0:T(8,128)(2,1)} %param.15) | copy-start | bytes 589828
  7.3 70.0 %all-gather.6.cloned.1.call-start = ((), (), s32[]{:S(2)}) async-start(), calls=%async_computation.4 | async-start | bytes 3981312 | tf_op jit(solution)/shard_map/all_gather | solution.py:144
  8.0 110.8 %all-gather.8.cloned.1.call-start = ((), (), s32[]{:S(2)}) async-start(), calls=%async_computation.5 | async-start | bytes 1327104 | tf_op jit(solution)/shard_map/all_gather | solution.py:146
  8.8 191.2 %all-gather.10.cloned.1.call-start = ((), (), s32[]{:S(2)}) async-start(), calls=%async_computation.6 | async-start | bytes 5308416 | tf_op jit(solution)/shard_map/all_gather | solution.py:164
  9.5 270.6 %all-gather.12.cloned.1.call-start = ((), (), s32[]{:S(2)}) async-start(), calls=%async_computation.7 | async-start | bytes 5308416 | tf_op jit(solution)/shard_map/all_gather | solution.py:166
  10.1 375.9 %reduce-scatter.13.cloned.1.call-start = ((), (), s32[]{:S(2)}) async-start(), calls=%async_computation.11 | async-start | bytes 3981312
  45.7 238.8 %copy-start.20 = (f32[768]{0:T(1024)}, f32[768]{0:T(1024)S(1)}, u32[]{:S(2)}) copy-start(f32[768]{0:T(1024)S(1)} %convert_element_type.240) | copy-start | bytes 9220
  69.6 214.9 %copy-start.36 = (f32[128]{0:T(128)}, f32[128]{0:T(128)S(1)}, u32[]{:S(2)}) copy-start(f32[128]{0:T(128)S(1)} %compare_convert_fusion) | copy-start | bytes 1540
  81.3 127.0 %copy-start.13 = (bf16[12,64,128]{2,1,0:T(8,128)(2,1)}, bf16[12,64,128]{2,1,0:T(8,128)(2,1)S(1)}, u32[]{:S(2)}) copy-start(bf16[12,64,128]{2,1,0:T(8,128)(2,1)S(1)} %convolution_convert_fusion.6) | copy-start | bytes 589828
  120.6 167.2 %copy-start.22 = (f32[128]{0:T(128)}, f32[128]{0:T(128)S(1)}, u32[]{:S(2)}) copy-start(f32[128]{0:T(128)S(1)} %broadcast_multiply_fusion.5) | copy-start | bytes 1540
  120.8 167.0 %copy-start.25 = (f32[128]{0:T(128)}, f32[128]{0:T(128)S(1)}, u32[]{:S(2)}) copy-start(f32[128]{0:T(128)S(1)} %add_rsqrt_fusion.1) | copy-start | bytes 1540
  307.8 144.2 %reduce-scatter.7.cloned.1.call-start = ((), (), s32[]{:S(2)}) async-start(), calls=%async_computation.8 | async-start | bytes 1327104 | tf_op jit(solution)/shard_map/reduce_scatter | solution.py:240
  310.2 241.3 %reduce-scatter.9.cloned.1.call-start = ((), (), s32[]{:S(2)}) async-start(), calls=%async_computation.9 | async-start | bytes 5308416 | tf_op jit(solution)/shard_map/reduce_scatter | solution.py:194
  313.9 336.2 %reduce-scatter.11.cloned.1.call-start = ((), (), s32[]{:S(2)}) async-start(), calls=%async_computation.10 | async-start | bytes 5308416 | tf_op jit(solution)/shard_map/reduce_scatter | solution.py:200
  317.6 334.5 %copy-start.49 = (bf16[96]{0:T(256)(128)(2,1)S(1)}, bf16[96]{0:T(256)(128)(2,1)}, u32[]{:S(2)}) copy-start(bf16[96]{0:T(256)(128)(2,1)} %param.28) | copy-start | bytes 580
  317.6 334.8 %copy-start.24 = (bf16[12,64]{1,0:T(8,128)(2,1)S(1)}, bf16[12,64]{1,0:T(8,128)(2,1)}, u32[]{:S(2)}) copy-start(bf16[12,64]{1,0:T(8,128)(2,1)} %get-tuple-element.125) | copy-start | bytes 4612
  317.6 334.9 %copy-start.29 = (bf16[768]{0:T(1024)(128)(2,1)S(1)}, bf16[768]{0:T(1024)(128)(2,1)}, u32[]{:S(2)}) copy-start(bf16[768]{0:T(1024)(128)(2,1)} %get-tuple-element.72) | copy-start | bytes 4612
  317.7 334.9 %copy-start.30 = (bf16[768]{0:T(1024)(128)(2,1)S(1)}, bf16[768]{0:T(1024)(128)(2,1)}, u32[]{:S(2)}) copy-start(bf16[768]{0:T(1024)(128)(2,1)} %get-tuple-element.77) | copy-start | bytes 4612
  317.7 334.9 %copy-start.31 = (bf16[768]{0:T(1024)(128)(2,1)S(1)}, bf16[768]{0:T(1024)(128)(2,1)}, u32[]{:S(2)}) copy-start(bf16[768]{0:T(1024)(128)(2,1)} %get-tuple-element.105) | copy-start | bytes 4612
  317.7 334.9 %copy-start.32 = (bf16[768]{0:T(1024)(128)(2,1)S(1)}, bf16[768]{0:T(1024)(128)(2,1)}, u32[]{:S(2)}) copy-start(bf16[768]{0:T(1024)(128)(2,1)} %get-tuple-element.70) | copy-start | bytes 4612
  317.7 334.9 %copy-start.33 = (bf16[768]{0:T(1024)(128)(2,1)S(1)}, bf16[768]{0:T(1024)(128)(2,1)}, u32[]{:S(2)}) copy-start(bf16[768]{0:T(1024)(128)(2,1)} %get-tuple-element.75) | copy-start | bytes 4612
  317.7 334.9 %copy-start.34 = (bf16[768]{0:T(1024)(128)(2,1)S(1)}, bf16[768]{0:T(1024)(128)(2,1)}, u32[]{:S(2)}) copy-start(bf16[768]{0:T(1024)(128)(2,1)} %get-tuple-element.107) | copy-start | bytes 4612
  317.7 334.9 %copy-start.35 = (bf16[3072]{0:T(1024)(128)(2,1)S(1)}, bf16[3072]{0:T(1024)(128)(2,1)}, u32[]{:S(2)}) copy-start(bf16[3072]{0:T(1024)(128)(2,1)} %get-tuple-element.131) | copy-start | bytes 18436
  317.7 381.6 %copy-start.21 = (f32[768]{0:T(1024)S(1)}, f32[768]{0:T(1024)}, u32[]{:S(2)}) copy-start(f32[768]{0:T(1024)} %copy-done.20) | copy-start | bytes 9220
  317.7 381.6 %copy-start.28 = (f32[128]{0:T(128)S(1)}, f32[128]{0:T(128)}, u32[]{:S(2)}) copy-start(f32[128]{0:T(128)} %copy-done.27) | copy-start | bytes 1540
  317.7 381.6 %copy-start.37 = (f32[128]{0:T(128)S(1)}, f32[128]{0:T(128)}, u32[]{:S(2)}) copy-start(f32[128]{0:T(128)} %copy-done.36) | copy-start | bytes 1540
  317.7 381.6 %copy-start.39 = (f32[128]{0:T(128)S(1)}, f32[128]{0:T(128)}, u32[]{:S(2)}) copy-start(f32[128]{0:T(128)} %copy-done.38) | copy-start | bytes 1540
  317.8 386.4 %all-reduce.21.cloned.1.call-start = ((), (), s32[]{:S(2)}) async-start(), calls=%async_computation.12 | async-start | bytes 3833856 | tf_op jit(solution)/shard_map/psum | solution.py:260
  388.0 312.2 %copy-start.8 = (bf16[12,64,128]{2,1,0:T(8,128)(2,1)S(1)}, bf16[12,64,128]{2,1,0:T(8,128)(2,1)}, u32[]{:S(2)}) copy-start(bf16[12,64,128]{2,1,0:T(8,128)(2,1)} %copy-done.7) | copy-start | bytes 589828
  388.0 312.2 %copy-start.10 = (bf16[12,64,128]{2,1,0:T(8,128)(2,1)S(1)}, bf16[12,64,128]{2,1,0:T(8,128)(2,1)}, u32[]{:S(2)}) copy-start(bf16[12,64,128]{2,1,0:T(8,128)(2,1)} %copy-done.9) | copy-start | bytes 589828
  388.0 312.2 %copy-start.12 = (bf16[12,64,128]{2,1,0:T(8,128)(2,1)S(1)}, bf16[12,64,128]{2,1,0:T(8,128)(2,1)}, u32[]{:S(2)}) copy-start(bf16[12,64,128]{2,1,0:T(8,128)(2,1)} %copy-done.11) | copy-start | bytes 589828
  (31 other events, 107.7 us)
Sparse Core Ops, SparseCore 0:
  10.3 66.9 all-gather.5
  79.5 39.3 all-gather.7
  121.0 78.9 all-gather.9
  202.0 78.0 all-gather.11
  307.9 77.9 reduce-scatter.12
  389.8 62.2 reduce-scatter.6
  455.7 95.7 reduce-scatter.8
  555.1 94.9 reduce-scatter.10
  653.4 49.2 all-reduce.20
where the time goes:
time: 718 us; the launch traced here: 716 us
  waiting for transfers between devices  528 us (74%)
  blocking collectives  96.5 us (13%)
  matrix products  42.4 us (6%)
  between operations  17.8 us (2%)
  local copies, waits for them, and re-layouts  16.9 us (2%)
  other arithmetic  13.6 us (2%)
    reduce_scatter x1, waiting for transfers between devices, on_device(): lax.psum_scatter(grad_w_up.astype(jnp.bfloat16), 'shard', scatter_dimensi...  99.4 us
    reduce_scatter x1, waiting for transfers between devices, on_device(): lax.psum_scatter(grad_w_down.astype(jnp.bfloat16), 'shard', scatter_dimen...  98.7 us
    all_gather x1, waiting for transfers between devices, on_device(): lax.all_gather(up_weight, 'shard', axis=0, tiled=True)  79.2 us
    all_gather x1, waiting for transfers between devices, on_device(): lax.all_gather(down_weight, 'shard', axis=0, tiled=True)  71.7 us
    unnamed x10, waiting for transfers between devices  70.8 us
    reduce_scatter x1, waiting for transfers between devices, on_device(): lax.psum_scatter(grad_w_out.astype(jnp.bfloat16), 'shard', scatter_dimens...  64 us
    unnamed x2, blocking collectives  60.4 us
    all_gather x1, waiting for transfers between devices, on_device(): lax.all_gather(out_weight, 'shard', axis=0, tiled=True)  37.5 us
  transfers between devices with their start and end apart: 9, of which 8 were waited for; matrix products, arithmetic and copies ran while one was open for 5% of the time, Pallas kernels for 0%

commit v1 on v0

--- a/solution.py
+++ b/solution.py
@@ -3,6 +3,8 @@
 import jax
 import jax.numpy as jnp
 from jax import lax
+from jax.experimental import pallas as pl
+from jax.experimental.pallas import tpu as pltpu
 from jax.sharding import PartitionSpec as P
 
 HEADS = 12
@@ -119,7 +121,209 @@
     )
 
 
+AXES = ("replica", "shard")
+REPLICAS = 4
+SHARDS = 8
+
+
+def swap_pairs(dx, dcore, dz, dy):
+    pairs = []
+    for replica in range(REPLICAS):
+        for shard in range(SHARDS):
+            to_replica = replica ^ (dx * 2 + dcore)
+            to_shard = shard ^ (dz * 2 + dy)
+            pairs.append((replica * SHARDS + shard, to_replica * SHARDS + to_shard))
+    return pairs
+
+
+def swap_x(value):
+    return lax.ppermute(value, AXES, swap_pairs(1, 0, 0, 0))
+
+
+def swap_core(value):
+    return lax.ppermute(value, AXES, swap_pairs(0, 1, 0, 0))
+
+
+def swap_y(value):
+    return lax.ppermute(value, AXES, swap_pairs(0, 0, 0, 1))
+
+
+def swap_z(value, distance):
+    return lax.ppermute(value, AXES, swap_pairs(0, 0, distance, 0))
+
+
+def after(value, *others):
+    return lax.optimization_barrier((value,) + others)[0]
+
+
+def place_kernel(block_at, half, replica_shard, *refs):
+    parts, whole, semaphores = refs[:-2], refs[-2], refs[-1]
+    replica, shard = replica_shard[0], replica_shard[1]
+    copies = []
+    for core in range(2):
+        for which in range(2):
+            part = parts[core * 2 + which]
+            for first in range(2):
+                for second in range(2):
+                    for z in range(4):
+                        x, y = (first, second) if which == 0 else (second, first)
+                        to_replica = replica ^ (x * 2 + core)
+                        to_shard = shard ^ (z * 2 + y)
+                        copy = pltpu.make_async_copy(
+                            part.at[first, second, z],
+                            block_at(whole, to_replica, to_shard, which * half, half),
+                            semaphores.at[len(copies)],
+                        )
+                        copy.start()
+                        copies.append(copy)
+    for copy in copies:
+        copy.wait()
+
+
+def split_kernel(block_at, half, replica_shard, whole, *refs):
+    parts, semaphores = refs[:-1], refs[-1]
+    replica, shard = replica_shard[0], replica_shard[1]
+    copies = []
+    for core in (1, 0):
+        for which in range(2):
+            part = parts[core * 2 + which]
+            for first in range(2):
+                for second in range(2):
+                    for z in range(4):
+                        x, y = (first, second) if which == 0 else (second, first)
+                        to_replica = replica ^ (x * 2 + core)
+                        to_shard = shard ^ (z * 2 + y)
+                        copy = pltpu.make_async_copy(
+                            block_at(whole, to_replica, to_shard, which * half, half),
+                            part.at[first, second, z],
+                            semaphores.at[len(copies)],
+                        )
+                        copy.start()
+                        copies.append(copy)
+    for copy in copies:
+        copy.wait()
+
+
+def block_columns(whole, replica, shard, start, half):
+    width = whole.shape[1] // REPLICAS
+    height = whole.shape[0] // SHARDS
+    return whole.at[
+        pl.ds(pl.multiple_of(shard * height + start, 16), half),
+        pl.ds(pl.multiple_of(replica * width, 128), width),
+    ]
+
+
+def block_rows(whole, replica, shard, start, half):
+    height = whole.shape[0] // (SHARDS * REPLICAS)
+    return whole.at[
+        pl.ds(pl.multiple_of((shard * REPLICAS + replica) * height + start, 16), half), :
+    ]
+
+
+def place(parts, shape, block_at, position):
+    half = parts[0].shape[3]
+    return pl.pallas_call(
+        partial(place_kernel, block_at, half),
+        out_shape=jax.ShapeDtypeStruct(shape, parts[0].dtype),
+        in_specs=[pl.BlockSpec(memory_space=pltpu.SMEM)]
+        + [pl.BlockSpec(memory_space=pl.ANY)] * 4,
+        out_specs=pl.BlockSpec(memory_space=pltpu.VMEM),
+        compiler_params=pltpu.CompilerParams(vmem_limit_bytes=16 * 2**20),
+        scratch_shapes=[pltpu.SemaphoreType.DMA((64,))],
+        name="place",
+    )(position, *parts)
+
+
+def split(whole, half, width, block_at, position):
+    shape = jax.ShapeDtypeStruct((2, 2, 4, half, width), whole.dtype)
+    return pl.pallas_call(
+        partial(split_kernel, block_at, half),
+        out_shape=[shape] * 4,
+        in_specs=[
+            pl.BlockSpec(memory_space=pltpu.SMEM),
+            pl.BlockSpec(memory_space=pltpu.VMEM),
+        ],
+        out_specs=[pl.BlockSpec(memory_space=pl.ANY)] * 4,
+        compiler_params=pltpu.CompilerParams(vmem_limit_bytes=16 * 2**20),
+        scratch_shapes=[pltpu.SemaphoreType.DMA((64,))],
+        name="split",
+    )(position, whole)
+
+
+def gather_z(piece):
+    received = [swap_z(piece, distance) for distance in (1, 2, 3)]
+    half = piece.shape[0] // 2
+    return [
+        jnp.stack([entry[which * half : (which + 1) * half] for entry in [piece] + received])
+        for which in range(2)
+    ]
+
+
+def gather_xy(halves):
+    y_first, x_first = halves
+    y_pair = jnp.stack([y_first, swap_y(y_first)])
+    x_pair = jnp.stack([x_first, swap_x(x_first)])
+    y_all = jnp.stack([y_pair, swap_x(y_pair)])
+    x_all = jnp.stack([x_pair, swap_y(x_pair)])
+    return (y_all, x_all)
+
+
+def gather_core(pair):
+    y_all, x_all = pair
+    return (y_all, x_all, swap_core(y_all), swap_core(x_all))
+
+
+def plus(left_side, right_side):
+    return (left_side.astype(jnp.float32) + right_side.astype(jnp.float32)).astype(jnp.bfloat16)
+
+
+def reduce_chunk(parts):
+    mine_x, mine_y, other_x, other_y = parts
+    sum_x = plus(mine_x, swap_core(other_x))
+    sum_y = plus(mine_y, swap_core(other_y))
+    sum_x = plus(sum_x[0], swap_x(sum_x[1]))
+    sum_y = plus(sum_y[0], swap_y(sum_y[1]))
+    sum_x = plus(sum_x[0], swap_y(sum_x[1]))
+    sum_y = plus(sum_y[0], swap_x(sum_y[1]))
+    both = jnp.concatenate([sum_x, sum_y], axis=1)
+    total = both[0].astype(jnp.float32)
+    for distance in (1, 2, 3):
+        total = total + swap_z(both[distance], distance).astype(jnp.float32)
+    return total.astype(jnp.bfloat16)
+
+
+def spread(quarter, x, core):
+    other = swap_x(quarter)
+    pair = jnp.stack([jnp.where(x == 0, quarter, other), jnp.where(x == 0, other, quarter)])
+    far = swap_core(pair)
+    return jnp.stack(
+        [jnp.where(core == 0, pair, far), jnp.where(core == 0, far, pair)], axis=1
+    ).reshape((REPLICAS,) + quarter.shape)
+
+
+def small_gather(vector, z, y):
+    block = vector[None]
+    other = swap_y(block)
+    block = jnp.concatenate([jnp.where(y == 0, block, other), jnp.where(y == 0, other, block)])
+    for distance in (1, 2):
+        other = swap_z(block, distance)
+        low_side = (z & distance) == 0
+        block = jnp.concatenate(
+            [jnp.where(low_side, block, other), jnp.where(low_side, other, block)]
+        )
+    return block
+
+
+def small_sum(vector):
+    vector = vector + swap_core(vector)
+    vector = vector + swap_x(vector)
+    vector = vector + swap_y(vector)
+    vector = vector + swap_z(vector, 1)
+    return vector + swap_z(vector, 2)
+
+
 def on_device(
+    mesh_shape,
     tokens,
     lengths,
     qkv_weight,
@@ -137,16 +341,51 @@
     cotangent,
 ):
     model_width = tokens.shape[1]
+    replica = lax.axis_index("replica").astype(jnp.int32)
+    shard = lax.axis_index("shard").astype(jnp.int32)
+    x, core, z, y = replica // 2, replica % 2, shard // 2, shard % 2
+    direct = mesh_shape["replica"] == REPLICAS and mesh_shape["shard"] == SHARDS
+    position = jnp.stack([replica, shard])
     segment_id, usable = layout(lengths[0], tokens.shape[0])
     same_segment = segment_id[:, None] == segment_id[None, :]
     keep_rows = usable.astype(jnp.float32)[:, None]
-    w_qkv, b_qv, w_out, b_out, gain_one, shift_one = (
-        lax.all_gather(qkv_weight, "shard", axis=0, tiled=True),
-        lax.all_gather(qv_bias, "shard", axis=0, tiled=True),
-        lax.all_gather(out_weight, "shard", axis=0, tiled=True),
-        lax.all_gather(out_bias, "shard", axis=0, tiled=True),
-        lax.all_gather(first_gain, "shard", axis=0, tiled=True),
-        lax.all_gather(first_shift, "shard", axis=0, tiled=True),
+    small = (qv_bias, out_bias, first_gain, first_shift, up_bias, down_bias, second_gain, second_shift)
+    sizes = [entry.shape[0] for entry in small]
+    if direct:
+        packed = small_gather(jnp.concatenate(small), z, y)
+        quarter_attn = lax.switch(
+            replica,
+            [lambda at=at: qkv_weight[:, at * 768 : (at + 1) * 768] for at in range(3)]
+            + [lambda: out_weight],
+        )
+        quarter_up = lax.dynamic_slice_in_dim(up_weight, replica * 768, 768, axis=1)
+        quarter_down = lax.dynamic_slice_in_dim(down_weight, replica * 96, 96, axis=0)
+        z_attn = gather_z(quarter_attn)
+        quarter_up = after(quarter_up, *z_attn)
+        xy_attn = gather_xy(z_attn)
+        z_up = gather_z(quarter_up)
+        quarter_down = after(quarter_down, *z_up)
+        z_up = [after(entry, *xy_attn) for entry in z_up]
+        core_attn = gather_core(xy_attn)
+        z_down = gather_z(quarter_down)
+        xy_up = gather_xy(z_up)
+        z_down = [after(entry, *xy_up) for entry in z_down]
+        core_up = gather_core(xy_up)
+        xy_down = gather_xy(z_down)
+        core_down = gather_core(xy_down)
+        w_attn = place(core_attn, (768, 3072), block_columns, position)
+        w_qkv, w_out = w_attn[:, : 3 * model_width], w_attn[:, 3 * model_width :]
+        w_up = place(core_up, (768, 3072), block_columns, position)
+        w_down = place(core_down, (3072, 768), block_rows, position)
+    else:
+        packed = lax.all_gather(jnp.concatenate(small), "shard", axis=0)
+        w_qkv, w_out, w_up, w_down = (
+            lax.all_gather(entry, "shard", axis=0, tiled=True)
+            for entry in (qkv_weight, out_weight, up_weight, down_weight)
+        )
+    ends = [sum(sizes[:count]) for count in range(len(sizes) + 1)]
+    b_qv, b_out, gain_one, shift_one, b_up, b_down, gain_two, shift_two = (
+        packed[:, ends[at] : ends[at + 1]].reshape(-1) for at in range(len(sizes))
     )
     projected = matmul(tokens, w_qkv)
     bias_full = b_qv.astype(jnp.float32)
@@ -160,14 +399,6 @@
         tokens.astype(jnp.float32) + attn_out, gain_first, shift_one.astype(jnp.float32)
     )
     hidden_low = hidden.astype(jnp.bfloat16)
-    w_up, b_up, w_down, b_down, gain_two, shift_two = (
-        lax.all_gather(up_weight, "shard", axis=0, tiled=True),
-        lax.all_gather(up_bias, "shard", axis=0, tiled=True),
-        lax.all_gather(down_weight, "shard", axis=0, tiled=True),
-        lax.all_gather(down_bias, "shard", axis=0, tiled=True),
-        lax.all_gather(second_gain, "shard", axis=0, tiled=True),
-        lax.all_gather(second_shift, "shard", axis=0, tiled=True),
-    )
     pre_act = matmul(hidden_low, w_up) + b_up.astype(jnp.float32)
     activated = jax.nn.gelu(pre_act, approximate=False).astype(jnp.bfloat16)
     branch = matmul(activated, w_down) + b_down.astype(jnp.float32)
@@ -180,105 +411,90 @@
     grad_second, grad_gain_two, grad_shift_two = normalize_back(
         grad_out, normed_two, inverse_two, gain_second
     )
-    back_up, back_down = (w_up, w_down)
     grad_branch = grad_second.astype(jnp.bfloat16)
-    grad_w_down = matmul_tn(activated, grad_branch)
+    grad_w_down = matmul_tn(activated, grad_branch).astype(jnp.bfloat16)
+    if direct:
+        parts_down = split(grad_w_down, 48, 768, block_rows, position)
+        reduced_down = reduce_chunk(parts_down)
     grad_b_down = jnp.sum(grad_branch.astype(jnp.float32), axis=0)
-    grad_act = matmul_nt(grad_branch, back_down)
+    grad_act = matmul_nt(grad_branch, w_down)
     gelu_value, gelu_pull = jax.vjp(partial(jax.nn.gelu, approximate=False), pre_act)
     grad_pre = gelu_pull(grad_act)[0].astype(jnp.bfloat16)
-    grad_w_up = matmul_tn(hidden_low, grad_pre)
+    grad_w_up = matmul_tn(hidden_low, grad_pre).astype(jnp.bfloat16)
+    if direct:
+        parts_up = split(grad_w_up, 48, 768, block_columns, position)
+        reduced_up = reduce_chunk(parts_up)
     grad_b_up = jnp.sum(grad_pre.astype(jnp.float32), axis=0)
-    grad_hidden = grad_second + matmul_nt(grad_pre, back_up)
-    ffn_shares = (
-        lax.psum_scatter(
-            grad_w_up.astype(jnp.bfloat16), "shard", scatter_dimension=0, tiled=True
-        ).astype(jnp.float32),
-        lax.psum_scatter(
-            grad_b_up.astype(jnp.bfloat16), "shard", scatter_dimension=0, tiled=True
-        ).astype(jnp.float32),
-        lax.psum_scatter(
-            grad_w_down.astype(jnp.bfloat16), "shard", scatter_dimension=0, tiled=True
-        ).astype(jnp.float32),
-        lax.psum_scatter(
-            grad_b_down.astype(jnp.bfloat16), "shard", scatter_dimension=0, tiled=True
-        ).astype(jnp.float32),
-        lax.psum_scatter(
-            grad_gain_two.astype(jnp.bfloat16), "shard", scatter_dimension=0, tiled=True
-        ).astype(jnp.float32),
-        lax.psum_scatter(
-            grad_shift_two.astype(jnp.bfloat16), "shard", scatter_dimension=0, tiled=True
-        ).astype(jnp.float32),
-    )
+    grad_hidden = grad_second + matmul_nt(grad_pre, w_up)
     grad_first, grad_gain_one, grad_shift_one = normalize_back(
         grad_hidden, normed_one, inverse_one, gain_first
     )
-    back_qkv, back_out = (w_qkv, w_out)
     grad_attn = grad_first.astype(jnp.bfloat16)
-    grad_w_out = matmul_tn(context, grad_attn)
+    grad_w_out = matmul_tn(context, grad_attn).astype(jnp.bfloat16)
     grad_b_out = jnp.sum(grad_attn.astype(jnp.float32), axis=0)
-    grad_context = matmul_nt(grad_attn, back_out).astype(jnp.bfloat16)
+    grad_context = matmul_nt(grad_attn, w_out).astype(jnp.bfloat16)
     grad_queries, grad_keys, grad_values = attend_back(
         grad_context, queries, key_rows, values, same_segment, log_total
     )
     grad_proj = jnp.concatenate([grad_queries, grad_keys, grad_values], axis=1)
-    grad_w_qkv = matmul_tn(tokens, grad_proj)
+    grad_w_qkv = matmul_tn(tokens, grad_proj).astype(jnp.bfloat16)
     grad_b_qv = jnp.concatenate(
         [
             jnp.sum(grad_queries.astype(jnp.float32), axis=0),
             jnp.sum(grad_values.astype(jnp.float32), axis=0),
         ]
     )
-    grad_tokens = (grad_first + matmul_nt(grad_proj, back_qkv)).astype(jnp.bfloat16)
-    attn_shares = (
-        lax.psum_scatter(
-            grad_w_qkv.astype(jnp.bfloat16), "shard", scatter_dimension=0, tiled=True
-        ).astype(jnp.float32),
-        lax.psum_scatter(
-            grad_b_qv.astype(jnp.bfloat16), "shard", scatter_dimension=0, tiled=True
-        ).astype(jnp.float32),
-        lax.psum_scatter(
-            grad_w_out.astype(jnp.bfloat16), "shard", scatter_dimension=0, tiled=True
-        ).astype(jnp.float32),
-        lax.psum_scatter(
-            grad_b_out.astype(jnp.bfloat16), "shard", scatter_dimension=0, tiled=True
-        ).astype(jnp.float32),
-        lax.psum_scatter(
-            grad_gain_one.astype(jnp.bfloat16), "shard", scatter_dimension=0, tiled=True
-        ).astype(jnp.float32),
-        lax.psum_scatter(
-            grad_shift_one.astype(jnp.bfloat16), "shard", scatter_dimension=0, tiled=True
-        ).astype(jnp.float32),
-    )
-    totals = (
-        lax.psum(ffn_shares[0].astype(jnp.bfloat16), "replica").astype(jnp.float32),
-        lax.psum(ffn_shares[1].astype(jnp.bfloat16), "replica").astype(jnp.float32),
-        lax.psum(ffn_shares[2].astype(jnp.bfloat16), "replica").astype(jnp.float32),
-        lax.psum(ffn_shares[3].astype(jnp.bfloat16), "replica").astype(jnp.float32),
-        lax.psum(ffn_shares[4].astype(jnp.bfloat16), "replica").astype(jnp.float32),
-        lax.psum(ffn_shares[5].astype(jnp.bfloat16), "replica").astype(jnp.float32),
-        lax.psum(attn_shares[0].astype(jnp.bfloat16), "replica").astype(jnp.float32),
-        lax.psum(attn_shares[1].astype(jnp.bfloat16), "replica").astype(jnp.float32),
-        lax.psum(attn_shares[2].astype(jnp.bfloat16), "replica").astype(jnp.float32),
-        lax.psum(attn_shares[3].astype(jnp.bfloat16), "replica").astype(jnp.float32),
-        lax.psum(attn_shares[4].astype(jnp.bfloat16), "replica").astype(jnp.float32),
-        lax.psum(attn_shares[5].astype(jnp.bfloat16), "replica").astype(jnp.float32),
-    )
+    grad_tokens = (grad_first + matmul_nt(grad_proj, w_qkv)).astype(jnp.bfloat16)
+    small_grads = (
+        grad_b_qv,
+        grad_b_out,
+        grad_gain_one,
+        grad_shift_one,
+        grad_b_up,
+        grad_b_down,
+        grad_gain_two,
+        grad_shift_two,
+    )
+    shards = mesh_shape["shard"]
+    packed_grads = jnp.concatenate([entry.reshape(shards, -1) for entry in small_grads], axis=1)
+    if direct:
+        parts_attn = split(
+            jnp.concatenate([grad_w_qkv, grad_w_out], axis=1), 48, 768, block_columns, position
+        )
+        reduced_attn = reduce_chunk(parts_attn)
+        small_total = lax.dynamic_index_in_dim(small_sum(packed_grads), shard, 0, False)
+        d_down = spread(reduced_down, x, core).reshape(-1, 768).astype(jnp.float32)
+        up_quarters = spread(reduced_up, x, core).astype(jnp.float32)
+        d_up = jnp.concatenate([up_quarters[at] for at in range(REPLICAS)], axis=1)
+        attn_quarters = spread(reduced_attn, x, core).astype(jnp.float32)
+        d_qkv = jnp.concatenate([attn_quarters[at] for at in range(3)], axis=1)
+        d_out = attn_quarters[3]
+    else:
+        d_down, d_up, d_qkv, d_out = (
+            lax.psum(
+                lax.psum_scatter(entry, "shard", scatter_dimension=0, tiled=True), "replica"
+            ).astype(jnp.float32)
+            for entry in (grad_w_down, grad_w_up, grad_w_qkv, grad_w_out)
+        )
+        small_total = lax.psum(
+            lax.psum_scatter(packed_grads, "shard", scatter_dimension=0, tiled=True), "replica"
+        ).reshape(-1)
+    small_outs = [small_total[ends[at] : ends[at + 1]] for at in range(len(sizes))]
     return (
         layer_out,
         grad_tokens,
-        totals[6],
-        totals[7],
-        totals[8],
-        totals[9],
-        totals[10],
-        totals[11],
-        totals[0],
-        totals[1],
-        totals[2],
-        totals[3],
-        totals[4],
-        totals[5],
+        d_qkv,
+        small_outs[0],
+        d_out,
+        small_outs[1],
+        small_outs[2],
+        small_outs[3],
+        d_up,
+        small_outs[4],
+        d_down,
+        small_outs[5],
+        small_outs[6],
+        small_outs[7],
     )
 
 
@@ -301,7 +517,7 @@
         P(("replica", "shard"), None),
     )
     return jax.shard_map(
-        on_device,
+        partial(on_device, dict(mesh.shape)),
         mesh=mesh,
         in_specs=placed,
         out_specs=(

time: 718 us -> 283 us (0.39)
  waiting for transfers between devices: 528 us -> 92.1 us
  blocking collectives: 96.5 us -> 0 us
  starting transfers between devices: 0.58 us -> 90.2 us
  Pallas kernels: 0 us -> 27.9 us
  matrix products: 42.4 us -> 22.8 us
  between operations: 17.8 us -> 2.26 us
  other arithmetic: 13.6 us -> 23.3 us
    reduce_scatter x3 -> x0, waiting for transfers between devices: 262 us -> none  [the longest x1 99.4 us: on_device(): lax.psum_scatter(grad_w_up.astype(jnp.bfloat16), 'shard', scatter_dimensi...]
    all_gather x4 -> x0, waiting for transfers between devices: 195 us -> none  [the longest x1 79.2 us: on_device(): lax.all_gather(up_weight, 'shard', axis=0, tiled=True)]
    ppermute x0 -> x68, waiting for transfers between devices: none -> 92.1 us  [the longest x16 37.6 us: swap_x(): return lax.ppermute(value, AXES, swap_pairs(1, 0, 0, 0))]
    ppermute x0 -> x68, starting transfers between devices: none -> 90.2 us  [the longest x22 32.3 us: swap_z(): return lax.ppermute(value, AXES, swap_pairs(0, 0, distance, 0))]
    unnamed x10 -> x0, waiting for transfers between devices: 70.8 us -> none
    unnamed x2 -> x0, blocking collectives: 60.4 us -> none
    pallas_call x0 -> x6, Pallas kernels: none -> 27.9 us  [the longest x3 14.5 us: place(): pl.pallas_call(partial(place_kernel, block_at, half), out_shape=jax.Shape...]
    all_gather x1 -> x0, blocking collectives: 23.2 us -> none  [on_device(): lax.all_gather(up_bias, 'shard', axis=0, tiled=True)]
  transfers between devices with their start and end apart: 9 -> 68, of which waited for: 8 -> 20; matrix products, arithmetic and copies ran while one was open for 5% -> 17% of each run, Pallas kernels for 0% -> 7%
where the time goes in v1:
time: 283 us; the launch traced here: 282 us
  waiting for transfers between devices  92.1 us (33%)
  starting transfers between devices  90.2 us (32%)
  Pallas kernels  27.9 us (10%)
  local copies, waits for them, and re-layouts  23.3 us (8%)
  other arithmetic  23.3 us (8%)
  matrix products  22.8 us (8%)
    ppermute x16, waiting for transfers between devices, swap_x(): return lax.ppermute(value, AXES, swap_pairs(1, 0, 0, 0))  37.6 us
    ppermute x22, starting transfers between devices, swap_z(): return lax.ppermute(value, AXES, swap_pairs(0, 0, distance, 0))  32.3 us
    ppermute x16, starting transfers between devices, swap_core(): return lax.ppermute(value, AXES, swap_pairs(0, 1, 0, 0))  30.5 us
    ppermute x22, waiting for transfers between devices, swap_z(): return lax.ppermute(value, AXES, swap_pairs(0, 0, distance, 0))  28.1 us
    ppermute x14, waiting for transfers between devices, swap_y(): return lax.ppermute(value, AXES, swap_pairs(0, 0, 0, 1))  26.3 us
    pallas_call x3, Pallas kernels, place(): pl.pallas_call(partial(place_kernel, block_at, half), out_shape=jax.Shape...  14.5 us
    ppermute x14, starting transfers between devices, swap_y(): return lax.ppermute(value, AXES, swap_pairs(0, 0, 0, 1))  13.8 us
    ppermute x16, starting transfers between devices, swap_x(): return lax.ppermute(value, AXES, swap_pairs(1, 0, 0, 0))  13.5 us
  transfers between devices with their start and end apart: 68, of which 20 were waited for; matrix products, arithmetic and copies ran while one was open for 17% of the time, Pallas kernels for 7%

profile of v1, /device:TPU:1, one launch (start us, length us, event | category | flops | bytes accessed | tf_op | source)
XLA Modules:
  0.0 281.8 jit_solution(1909975838152092336)
XLA Ops:
  2.7 4.2 %collective-permute-start.2 = (bf16[96,768]{1,0:T(8,128)(2,1)S(1)}, bf16[96,768]{1,0:T(8,128)(2,1)S(1)}, u32[]{:S(2)}, u32[]{:S(2)}) collective-permute-start(bf16[96,768]{1,0:T(8,128)(2,1)S(1)} %get-tuple-element.62), channel_id=1, source_target_pairs={{0,6},{1,7},{2,4},{3,5},{4,2},{5,3},{6,0},{7,1},{8,14},{9,15},{10,... | collective-permute-start | bytes 442376 | tf_op jit(solution)/shard_map/ppermute | solution.py:152
  22.1 2.5 collective-permute-start.14
  32.1 6.3 %collective-permute-done.13 = bf16[96,768]{1,0:T(8,128)(2,1)S(1)} collective-permute-done((bf16[96,768]{1,0:T(8,128)(2,1)S(1)}, bf16[96,768]{1,0:T(8,128)(2,1)S(1)}, u32[]{:S(2)}, u32[]{:S(2)}) %collective-permute-start.13) | collective-permute-done | bytes 147488 | tf_op jit(solution)/shard_map/ppermute | solution.py:152
  38.6 4.2 %collective-permute-done.6 = bf16[2,4,48,768]{3,2,1,0:T(8,128)(2,1)S(1)} collective-permute-done((bf16[2,4,48,768]{3,2,1,0:T(8,128)(2,1)S(1)}, bf16[2,4,48,768]{3,2,1,0:T(8,128)(2,1)S(1)}, u32[]{:S(2)}, u32[]{:S(2)}) %collective-permute-start.6) | collective-permute-done | bytes 589856 | tf_op jit(solution)/shard_map/ppermute | solution.py:148
  46.0 2.9 %collective-permute-start.22 = (bf16[96,768]{1,0:T(8,128)(2,1)}, bf16[96,768]{1,0:T(8,128)(2,1)S(1)}, u32[]{:S(2)}, u32[]{:S(2)}) collective-permute-start(bf16[96,768]{1,0:T(8,128)(2,1)} %constant_dynamic-slice_fusion), channel_id=1, source_target_pairs={{0,4},{1,5},{2,6},{3,7},{4,0},{5,1},{6,2},{7,3},{8,12},{9,13},{10,... | collective-permute-start | bytes 442376 | tf_op jit(solution)/shard_map/ppermute | solution.py:152
  48.9 2.9 %collective-permute-start.21 = (bf16[96,768]{1,0:T(8,128)(2,1)}, bf16[96,768]{1,0:T(8,128)(2,1)S(1)}, u32[]{:S(2)}, u32[]{:S(2)}) collective-permute-start(bf16[96,768]{1,0:T(8,128)(2,1)} %constant_dynamic-slice_fusion), channel_id=1, source_target_pairs={{0,2},{1,3},{2,0},{3,1},{4,6},{5,7},{6,4},{7,5},{8,10},{9,11},{10,... | collective-permute-start | bytes 442376 | tf_op jit(solution)/shard_map/ppermute | solution.py:152
  53.4 4.2 %collective-permute-done.17 = bf16[4,48,768]{2,1,0:T(8,128)(2,1)S(1)} collective-permute-done((bf16[4,48,768]{2,1,0:T(8,128)(2,1)S(1)}, bf16[4,48,768]{2,1,0:T(8,128)(2,1)S(1)}, u32[]{:S(2)}, u32[]{:S(2)}) %collective-permute-start.17) | collective-permute-done | bytes 294944 | tf_op jit(solution)/shard_map/ppermute | solution.py:140
  59.0 8.5 %collective-permute-start.7 = (bf16[2,2,4,48,768]{4,3,2,1,0:T(8,128)(2,1)S(1)}, bf16[2,2,4,48,768]{4,3,2,1,0:T(8,128)(2,1)}, u32[]{:S(2)}, u32[]{:S(2)}) collective-permute-start(bf16[2,2,4,48,768]{4,3,2,1,0:T(8,128)(2,1)S(1)} %pad_maximum_fusion.1.refs_0_), channel_id=1, source_target_pairs={{0,8},{1,9},{2,10},{3,11},{4,12},{5,13},{6,14},{7,15},{8,0},{9,1},... | collective-permute-start | bytes 3538952 | tf_op jit(solution)/shard_map/ppermute | solution.py:144
  84.8 9.7 %collective-permute-start.20 = (bf16[2,2,4,48,768]{4,3,2,1,0:T(8,128)(2,1)}, bf16[2,2,4,48,768]{4,3,2,1,0:T(8,128)(2,1)S(1)}, u32[]{:S(2)}, u32[]{:S(2)}) collective-permute-start(bf16[2,2,4,48,768]{4,3,2,1,0:T(8,128)(2,1)} %pad_maximum_fusion.4.refs_1_), channel_id=1, source_target_pairs={{0,8},{1,9},{2,10},{3,11},{4,12},{5,13},{6,14},{7,15},{8,0},{9,1},... | collective-permute-start | bytes 3538952 | tf_op jit(solution)/shard_map/ppermute | solution.py:144
  98.2 3.6 %place.3 = bf16[768,3072]{1,0:T(8,128)(2,1)S(1)} custom-call(s32[2]{0:T(128)S(1)} %pad_add_fusion.replica_shard, bf16[2,2,4,48,768]{4,3,2,1,0:T(8,128)(2,1)S(1)} %pad_maximum_fusion.1.refs_0_, bf16[2,2,4,48,768]{4,3,2,1,0:T(8,128)(2,1)S(1)} %pad_maximum_fusion.2.refs_1_, bf16[2,2,4,48,768]{4,3,2,1,0:T(8,128)(2,1)} %collective-permute-done.7.refs_2_, ...), custom_call_target="tpu_custom_call" | custom-call | tf_op jit(solution)/shard_map/place/pallas_call | solution.py:225
  106.2 6.1 %collective-permute-done.27 = bf16[2,4,48,768]{3,2,1,0:T(8,128)(2,1)S(1)} collective-permute-done((bf16[2,4,48,768]{3,2,1,0:T(8,128)(2,1)S(1)}, bf16[2,4,48,768]{3,2,1,0:T(8,128)(2,1)S(1)}, u32[]{:S(2)}, u32[]{:S(2)}) %collective-permute-start.27) | collective-permute-done | bytes 589856 | tf_op jit(solution)/shard_map/ppermute | solution.py:148
  114.4 2.5 place.4
  116.9 4.2 %multiply_convert_fusion = (bf16[128,3072]{1,0:T(8,128)(2,1)S(1)}, f32[128,3072]{1,0:T(8,128)S(1)}, f32[128,3072]{1,0:T(8,128)S(1)}) fusion(f32[3072]{0:T(1024)S(1)} %copy-done.39, bf16[768,3072]{1,0:T(8,128)(2,1)S(1)} %place.4, f32[128,768]{1,0:T(8,128)S(1)} %get-tuple-element.205, f32[768]{0:T(1024)S(1)} %reshape.311, f32[768]{0:T(1024)S(1)} %reshape.310, ...), kind=kOutput, calls=%fused_computation.28 | convolution fusion | flops 630423552 | bytes 9063424 | tf_op jit(solution)/shard_map/dot_general | solution.py:27
  121.1 8.4 %place.5 = bf16[3072,768]{1,0:T(8,128)(2,1)S(1)} custom-call(s32[2]{0:T(128)S(1)} %pad_add_fusion.replica_shard, bf16[2,2,4,48,768]{4,3,2,1,0:T(8,128)(2,1)S(1)} %pad_maximum_fusion.5.refs_0_, bf16[2,2,4,48,768]{4,3,2,1,0:T(8,128)(2,1)S(1)} %pad_maximum_fusion.6.refs_1_, bf16[2,2,4,48,768]{4,3,2,1,0:T(8,128)(2,1)S(1)} %collective-permute-done.28.refs_2_, ...), custom_call_target="tpu_custom_call" | custom-call | tf_op jit(solution)/shard_map/place/pallas_call | solution.py:225
  133.0 2.5 convert_reduce_fusion
  135.5 2.4 multiply_reduce_fusion.2
  153.4 2.8 split.3
  162.5 2.5 split.4
  166.6 8.1 %split.5 = (bf16[2,2,4,48,768]{4,3,2,1,0:T(8,128)(2,1)S(1)}, bf16[2,2,4,48,768]{4,3,2,1,0:T(8,128)(2,1)S(1)}, bf16[2,2,4,48,768]{4,3,2,1,0:T(8,128)(2,1)S(1)}, bf16[2,2,4,48,768]{4,3,2,1,0:T(8,128)(2,1)S(1)}) custom-call(s32[2]{0:T(128)S(1)} %pad_add_fusion.replica_shard, bf16[3072,768]{1,0:T(8,128)(2,1)S(1)} %convolution_convert_fusion.whole), custom_call_target="tpu_custom_call" | custom-call | tf_op jit(solution)/shard_map/split/pallas_call | solution.py:239
  182.9 9.2 %collective-permute-done.31 = bf16[2,4,48,768]{3,2,1,0:T(8,128)(2,1)S(1)} collective-permute-done((bf16[2,4,48,768]{3,2,1,0:T(8,128)(2,1)S(1)}, bf16[2,4,48,768]{3,2,1,0:T(8,128)(2,1)S(1)}, u32[]{:S(2)}, u32[]{:S(2)}) %collective-permute-start.31) | collective-permute-done | bytes 589856 | tf_op jit(solution)/shard_map/ppermute | solution.py:140
  194.0 10.7 %collective-permute-done.47 = bf16[2,4,48,768]{3,2,1,0:T(8,128)(2,1)S(1)} collective-permute-done((bf16[2,4,48,768]{3,2,1,0:T(8,128)(2,1)S(1)}, bf16[2,4,48,768]{3,2,1,0:T(8,128)(2,1)S(1)}, u32[]{:S(2)}, u32[]{:S(2)}) %collective-permute-start.47) | collective-permute-done | bytes 589856 | tf_op jit(solution)/shard_map/ppermute | solution.py:140
  206.7 10.6 %collective-permute-done.58 = bf16[2,4,48,768]{3,2,1,0:T(8,128)(2,1)S(1)} collective-permute-done((bf16[2,4,48,768]{3,2,1,0:T(8,128)(2,1)S(1)}, bf16[2,4,48,768]{3,2,1,0:T(8,128)(2,1)S(1)}, u32[]{:S(2)}, u32[]{:S(2)}) %collective-permute-start.58) | collective-permute-done | bytes 589856 | tf_op jit(solution)/shard_map/ppermute | solution.py:140
  219.4 4.7 %collective-permute-done.32 = bf16[4,48,768]{2,1,0:T(8,128)(2,1)S(1)} collective-permute-done((bf16[4,48,768]{2,1,0:T(8,128)(2,1)S(1)}, bf16[4,48,768]{2,1,0:T(8,128)(2,1)S(1)}, u32[]{:S(2)}, u32[]{:S(2)}) %collective-permute-start.32) | collective-permute-done | bytes 294944 | tf_op jit(solution)/shard_map/ppermute | solution.py:148
  225.5 4.9 %collective-permute-done.48 = bf16[4,48,768]{2,1,0:T(8,128)(2,1)S(1)} collective-permute-done((bf16[4,48,768]{2,1,0:T(8,128)(2,1)S(1)}, bf16[4,48,768]{2,1,0:T(8,128)(2,1)S(1)}, u32[]{:S(2)}, u32[]{:S(2)}) %collective-permute-start.48) | collective-permute-done | bytes 294944 | tf_op jit(solution)/shard_map/ppermute | solution.py:148
  232.4 4.3 %collective-permute-done.59 = bf16[4,48,768]{2,1,0:T(8,128)(2,1)S(1)} collective-permute-done((bf16[4,48,768]{2,1,0:T(8,128)(2,1)S(1)}, bf16[4,48,768]{2,1,0:T(8,128)(2,1)S(1)}, u32[]{:S(2)}, u32[]{:S(2)}) %collective-permute-start.59) | collective-permute-done | bytes 294944 | tf_op jit(solution)/shard_map/ppermute | solution.py:148
  236.8 3.0 %collective-permute-start.54 = (bf16[96,768]{1,0:T(8,128)(2,1)S(1)}, bf16[96,768]{1,0:T(8,128)(2,1)S(1)}, u32[]{:S(2)}, u32[]{:S(2)}) collective-permute-start(bf16[96,768]{1,0:T(8,128)(2,1)S(1)} %get-tuple-element.130), channel_id=1, source_target_pairs={{0,6},{1,7},{2,4},{3,5},{4,2},{5,3},{6,0},{7,1},{8,14},{9,15},{10,... | collective-permute-start | bytes 442376 | tf_op jit(solution)/shard_map/ppermute | solution.py:152
  241.6 4.2 %collective-permute-done.37 = bf16[96,768]{1,0:T(8,128)(2,1)S(1)} collective-permute-done((bf16[96,768]{1,0:T(8,128)(2,1)S(1)}, bf16[96,768]{1,0:T(8,128)(2,1)S(1)}, u32[]{:S(2)}, u32[]{:S(2)}) %collective-permute-start.37) | collective-permute-done | bytes 147488 | tf_op jit(solution)/shard_map/ppermute | solution.py:152
  245.7 8.3 %collective-permute-start.65 = (bf16[96,768]{1,0:T(8,128)(2,1)S(1)}, bf16[96,768]{1,0:T(8,128)(2,1)S(1)}, u32[]{:S(2)}, u32[]{:S(2)}) collective-permute-start(bf16[96,768]{1,0:T(8,128)(2,1)S(1)} %get-tuple-element.125), channel_id=1, source_target_pairs={{0,6},{1,7},{2,4},{3,5},{4,2},{5,3},{6,0},{7,1},{8,14},{9,15},{10,... | collective-permute-start | bytes 442376 | tf_op jit(solution)/shard_map/ppermute | solution.py:152
  255.5 7.5 %collective-permute-done.53 = bf16[96,768]{1,0:T(8,128)(2,1)S(1)} collective-permute-done((bf16[96,768]{1,0:T(8,128)(2,1)S(1)}, bf16[96,768]{1,0:T(8,128)(2,1)S(1)}, u32[]{:S(2)}, u32[]{:S(2)}) %collective-permute-start.53) | collective-permute-done | bytes 147488 | tf_op jit(solution)/shard_map/ppermute | solution.py:152
  264.8 4.5 %collective-permute-done.64 = bf16[96,768]{1,0:T(8,128)(2,1)S(1)} collective-permute-done((bf16[96,768]{1,0:T(8,128)(2,1)S(1)}, bf16[96,768]{1,0:T(8,128)(2,1)S(1)}, u32[]{:S(2)}, u32[]{:S(2)}) %collective-permute-start.64) | collective-permute-done | bytes 147488 | tf_op jit(solution)/shard_map/ppermute | solution.py:152
  271.2 2.3 collective-permute-start.40
  273.8 3.3 %collective-permute-start.67 = (bf16[2,96,768]{2,1,0:T(8,128)(2,1)S(1)}, bf16[2,96,768]{2,1,0:T(8,128)(2,1)S(1)}, u32[]{:S(2)}, u32[]{:S(2)}) collective-permute-start(bf16[2,96,768]{2,1,0:T(8,128)(2,1)S(1)} %pad_maximum_fusion.24), channel_id=1, source_target_pairs={{0,8},{1,9},{2,10},{3,11},{4,12},{5,13},{6,14},{7,15},{8,0},{9,1},... | collective-permute-start | bytes 884744 | tf_op jit(solution)/shard_map/ppermute | solution.py:144
  (389 shorter events, 115.5 us)
Async XLA Ops:
  2.7 17.9 %collective-permute-start.2 = (bf16[96,768]{1,0:T(8,128)(2,1)S(1)}, bf16[96,768]{1,0:T(8,128)(2,1)S(1)}, u32[]{:S(2)}, u32[]{:S(2)}) collective-permute-start(bf16[96,768]{1,0:T(8,128)(2,1)S(1)} %get-tuple-element.62), channel_id=1, source_target_pairs={{0,6},{1,7},{2,4},{3,5},{4,2},{5,3},{6,0},{7,1},{8,14},{9,15},{10,... | collective-permute-start | bytes 442376 | tf_op jit(solution)/shard_map/ppermute | solution.py:152
  28.2 14.7 %collective-permute-start.6 = (bf16[2,4,48,768]{3,2,1,0:T(8,128)(2,1)S(1)}, bf16[2,4,48,768]{3,2,1,0:T(8,128)(2,1)S(1)}, u32[]{:S(2)}, u32[]{:S(2)}) collective-permute-start(bf16[2,4,48,768]{3,2,1,0:T(8,128)(2,1)S(1)} %get-tuple-element.146), channel_id=1, source_target_pairs={{0,1},{1,0},{2,3},{3,2},{4,5},{5,4},{6,7},{7,6},{8,9},{9,8},{10,11... | collective-permute-start | bytes 1769480 | tf_op jit(solution)/shard_map/ppermute | solution.py:148
  48.9 18.7 %collective-permute-start.21 = (bf16[96,768]{1,0:T(8,128)(2,1)}, bf16[96,768]{1,0:T(8,128)(2,1)S(1)}, u32[]{:S(2)}, u32[]{:S(2)}) collective-permute-start(bf16[96,768]{1,0:T(8,128)(2,1)} %constant_dynamic-slice_fusion), channel_id=1, source_target_pairs={{0,2},{1,3},{2,0},{3,1},{4,6},{5,7},{6,4},{7,5},{8,10},{9,11},{10,... | collective-permute-start | bytes 442376 | tf_op jit(solution)/shard_map/ppermute | solution.py:152
  52.2 17.1 %collective-permute-start.16 = (bf16[2,4,48,768]{3,2,1,0:T(8,128)(2,1)S(1)}, bf16[2,4,48,768]{3,2,1,0:T(8,128)(2,1)S(1)}, u32[]{:S(2)}, u32[]{:S(2)}) collective-permute-start(bf16[2,4,48,768]{3,2,1,0:T(8,128)(2,1)S(1)} %get-tuple-element.144), channel_id=1, source_target_pairs={{0,16},{1,17},{2,18},{3,19},{4,20},{5,21},{6,22},{7,23},{8,24},{9,... | collective-permute-start | bytes 1769480 | tf_op jit(solution)/shard_map/ppermute | solution.py:140
  59.0 39.1 %collective-permute-start.7 = (bf16[2,2,4,48,768]{4,3,2,1,0:T(8,128)(2,1)S(1)}, bf16[2,2,4,48,768]{4,3,2,1,0:T(8,128)(2,1)}, u32[]{:S(2)}, u32[]{:S(2)}) collective-permute-start(bf16[2,2,4,48,768]{4,3,2,1,0:T(8,128)(2,1)S(1)} %pad_maximum_fusion.1.refs_0_), channel_id=1, source_target_pairs={{0,8},{1,9},{2,10},{3,11},{4,12},{5,13},{6,14},{7,15},{8,0},{9,1},... | collective-permute-start | bytes 3538952 | tf_op jit(solution)/shard_map/ppermute | solution.py:144
  67.5 30.7 %collective-permute-start.8 = (bf16[2,2,4,48,768]{4,3,2,1,0:T(8,128)(2,1)S(1)}, bf16[2,2,4,48,768]{4,3,2,1,0:T(8,128)(2,1)}, u32[]{:S(2)}, u32[]{:S(2)}) collective-permute-start(bf16[2,2,4,48,768]{4,3,2,1,0:T(8,128)(2,1)S(1)} %pad_maximum_fusion.2.refs_1_), channel_id=1, source_target_pairs={{0,8},{1,9},{2,10},{3,11},{4,12},{5,13},{6,14},{7,15},{8,0},{9,1},... | collective-permute-start | bytes 3538952 | tf_op jit(solution)/shard_map/ppermute | solution.py:144
  70.5 24.0 %collective-permute-start.24 = (bf16[4,48,768]{2,1,0:T(8,128)(2,1)}, bf16[4,48,768]{2,1,0:T(8,128)(2,1)}, u32[]{:S(2)}, u32[]{:S(2)}) collective-permute-start(bf16[4,48,768]{2,1,0:T(8,128)(2,1)} %pad_maximum_fusion.20), channel_id=1, source_target_pairs={{0,1},{1,0},{2,3},{3,2},{4,5},{5,4},{6,7},{7,6},{8,9},{9,8},{10,11... | collective-permute-start | bytes 884744 | tf_op jit(solution)/shard_map/ppermute | solution.py:148
  72.0 23.6 %collective-permute-start.26 = (bf16[4,48,768]{2,1,0:T(8,128)(2,1)}, bf16[4,48,768]{2,1,0:T(8,128)(2,1)}, u32[]{:S(2)}, u32[]{:S(2)}) collective-permute-start(bf16[4,48,768]{2,1,0:T(8,128)(2,1)} %pad_maximum_fusion.21), channel_id=1, source_target_pairs={{0,16},{1,17},{2,18},{3,19},{4,20},{5,21},{6,22},{7,23},{8,24},{9,... | collective-permute-start | bytes 884744 | tf_op jit(solution)/shard_map/ppermute | solution.py:140
  84.8 29.6 %collective-permute-start.20 = (bf16[2,2,4,48,768]{4,3,2,1,0:T(8,128)(2,1)}, bf16[2,2,4,48,768]{4,3,2,1,0:T(8,128)(2,1)S(1)}, u32[]{:S(2)}, u32[]{:S(2)}) collective-permute-start(bf16[2,2,4,48,768]{4,3,2,1,0:T(8,128)(2,1)} %pad_maximum_fusion.4.refs_1_), channel_id=1, source_target_pairs={{0,8},{1,9},{2,10},{3,11},{4,12},{5,13},{6,14},{7,15},{8,0},{9,1},... | collective-permute-start | bytes 3538952 | tf_op jit(solution)/shard_map/ppermute | solution.py:144
  94.5 19.9 %collective-permute-start.19 = (bf16[2,2,4,48,768]{4,3,2,1,0:T(8,128)(2,1)S(1)}, bf16[2,2,4,48,768]{4,3,2,1,0:T(8,128)(2,1)S(1)}, u32[]{:S(2)}, u32[]{:S(2)}) collective-permute-start(bf16[2,2,4,48,768]{4,3,2,1,0:T(8,128)(2,1)S(1)} %pad_maximum_fusion.3.refs_0_), channel_id=1, source_target_pairs={{0,8},{1,9},{2,10},{3,11},{4,12},{5,13},{6,14},{7,15},{8,0},{9,1},... | collective-permute-start | bytes 3538952 | tf_op jit(solution)/shard_map/ppermute | solution.py:144
  95.6 18.5 %collective-permute-start.25 = (bf16[2,4,48,768]{3,2,1,0:T(8,128)(2,1)S(1)}, bf16[2,4,48,768]{3,2,1,0:T(8,128)(2,1)S(1)}, u32[]{:S(2)}, u32[]{:S(2)}) collective-permute-start(bf16[2,4,48,768]{3,2,1,0:T(8,128)(2,1)S(1)} %get-tuple-element.140), channel_id=1, source_target_pairs={{0,16},{1,17},{2,18},{3,19},{4,20},{5,21},{6,22},{7,23},{8,24},{9,... | collective-permute-start | bytes 1769480 | tf_op jit(solution)/shard_map/ppermute | solution.py:140
  156.2 20.9 %collective-permute-start.30 = (bf16[2,2,4,48,768]{4,3,2,1,0:T(8,128)(2,1)S(1)}, bf16[2,2,4,48,768]{4,3,2,1,0:T(8,128)(2,1)S(1)}, u32[]{:S(2)}, u32[]{:S(2)}) collective-permute-start(bf16[2,2,4,48,768]{4,3,2,1,0:T(8,128)(2,1)S(1)} %get-tuple-element.71), channel_id=1, source_target_pairs={{0,8},{1,9},{2,10},{3,11},{4,12},{5,13},{6,14},{7,15},{8,0},{9,1},... | collective-permute-start | bytes 3538952 | tf_op jit(solution)/shard_map/ppermute | solution.py:144
  159.3 18.2 %collective-permute-start.33 = (bf16[2,2,4,48,768]{4,3,2,1,0:T(8,128)(2,1)S(1)}, bf16[2,2,4,48,768]{4,3,2,1,0:T(8,128)(2,1)S(1)}, u32[]{:S(2)}, u32[]{:S(2)}) collective-permute-start(bf16[2,2,4,48,768]{4,3,2,1,0:T(8,128)(2,1)S(1)} %get-tuple-element.73), channel_id=1, source_target_pairs={{0,8},{1,9},{2,10},{3,11},{4,12},{5,13},{6,14},{7,15},{8,0},{9,1},... | collective-permute-start | bytes 3538952 | tf_op jit(solution)/shard_map/ppermute | solution.py:144
  177.5 14.5 %collective-permute-start.31 = (bf16[2,4,48,768]{3,2,1,0:T(8,128)(2,1)S(1)}, bf16[2,4,48,768]{3,2,1,0:T(8,128)(2,1)S(1)}, u32[]{:S(2)}, u32[]{:S(2)}) collective-permute-start(bf16[2,4,48,768]{3,2,1,0:T(8,128)(2,1)S(1)} %slice_bitcast_fusion.18), channel_id=1, source_target_pairs={{0,16},{1,17},{2,18},{3,19},{4,20},{5,21},{6,22},{7,23},{8,24},{9,... | collective-permute-start | bytes 1769480 | tf_op jit(solution)/shard_map/ppermute | solution.py:140
  178.2 15.3 %collective-permute-start.34 = (bf16[2,4,48,768]{3,2,1,0:T(8,128)(2,1)S(1)}, bf16[2,4,48,768]{3,2,1,0:T(8,128)(2,1)S(1)}, u32[]{:S(2)}, u32[]{:S(2)}) collective-permute-start(bf16[2,4,48,768]{3,2,1,0:T(8,128)(2,1)S(1)} %slice_bitcast_fusion.16), channel_id=1, source_target_pairs={{0,1},{1,0},{2,3},{3,2},{4,5},{5,4},{6,7},{7,6},{8,9},{9,8},{10,11... | collective-permute-start | bytes 1769480 | tf_op jit(solution)/shard_map/ppermute | solution.py:148
  180.0 24.7 %collective-permute-start.47 = (bf16[2,4,48,768]{3,2,1,0:T(8,128)(2,1)S(1)}, bf16[2,4,48,768]{3,2,1,0:T(8,128)(2,1)S(1)}, u32[]{:S(2)}, u32[]{:S(2)}) collective-permute-start(bf16[2,4,48,768]{3,2,1,0:T(8,128)(2,1)S(1)} %slice_bitcast_fusion.14), channel_id=1, source_target_pairs={{0,16},{1,17},{2,18},{3,19},{4,20},{5,21},{6,22},{7,23},{8,24},{9,... | collective-permute-start | bytes 1769480 | tf_op jit(solution)/shard_map/ppermute | solution.py:140
  181.6 23.6 %collective-permute-start.50 = (bf16[2,4,48,768]{3,2,1,0:T(8,128)(2,1)S(1)}, bf16[2,4,48,768]{3,2,1,0:T(8,128)(2,1)S(1)}, u32[]{:S(2)}, u32[]{:S(2)}) collective-permute-start(bf16[2,4,48,768]{3,2,1,0:T(8,128)(2,1)S(1)} %slice_bitcast_fusion.12), channel_id=1, source_target_pairs={{0,1},{1,0},{2,3},{3,2},{4,5},{5,4},{6,7},{7,6},{8,9},{9,8},{10,11... | collective-permute-start | bytes 1769480 | tf_op jit(solution)/shard_map/ppermute | solution.py:148
  182.2 35.2 %collective-permute-start.58 = (bf16[2,4,48,768]{3,2,1,0:T(8,128)(2,1)S(1)}, bf16[2,4,48,768]{3,2,1,0:T(8,128)(2,1)S(1)}, u32[]{:S(2)}, u32[]{:S(2)}) collective-permute-start(bf16[2,4,48,768]{3,2,1,0:T(8,128)(2,1)S(1)} %slice_bitcast_fusion.10), channel_id=1, source_target_pairs={{0,16},{1,17},{2,18},{3,19},{4,20},{5,21},{6,22},{7,23},{8,24},{9,... | collective-permute-start | bytes 1769480 | tf_op jit(solution)/shard_map/ppermute | solution.py:140
  192.1 25.8 %collective-permute-start.61 = (bf16[2,4,48,768]{3,2,1,0:T(8,128)(2,1)S(1)}, bf16[2,4,48,768]{3,2,1,0:T(8,128)(2,1)S(1)}, u32[]{:S(2)}, u32[]{:S(2)}) collective-permute-start(bf16[2,4,48,768]{3,2,1,0:T(8,128)(2,1)S(1)} %slice_bitcast_fusion.8), channel_id=1, source_target_pairs={{0,1},{1,0},{2,3},{3,2},{4,5},{5,4},{6,7},{7,6},{8,9},{9,8},{10,11... | collective-permute-start | bytes 1769480 | tf_op jit(solution)/shard_map/ppermute | solution.py:148
  193.5 30.5 %collective-permute-start.32 = (bf16[4,48,768]{2,1,0:T(8,128)(2,1)S(1)}, bf16[4,48,768]{2,1,0:T(8,128)(2,1)S(1)}, u32[]{:S(2)}, u32[]{:S(2)}) collective-permute-start(bf16[4,48,768]{2,1,0:T(8,128)(2,1)S(1)} %slice_bitcast_fusion.38), channel_id=1, source_target_pairs={{0,1},{1,0},{2,3},{3,2},{4,5},{5,4},{6,7},{7,6},{8,9},{9,8},{10,11... | collective-permute-start | bytes 884744 | tf_op jit(solution)/shard_map/ppermute | solution.py:148
  204.7 20.6 %collective-permute-start.35 = (bf16[4,48,768]{2,1,0:T(8,128)(2,1)S(1)}, bf16[4,48,768]{2,1,0:T(8,128)(2,1)S(1)}, u32[]{:S(2)}, u32[]{:S(2)}) collective-permute-start(bf16[4,48,768]{2,1,0:T(8,128)(2,1)S(1)} %slice_bitcast_fusion.36), channel_id=1, source_target_pairs={{0,16},{1,17},{2,18},{3,19},{4,20},{5,21},{6,22},{7,23},{8,24},{9,... | collective-permute-start | bytes 884744 | tf_op jit(solution)/shard_map/ppermute | solution.py:140
  205.2 25.2 %collective-permute-start.48 = (bf16[4,48,768]{2,1,0:T(8,128)(2,1)S(1)}, bf16[4,48,768]{2,1,0:T(8,128)(2,1)S(1)}, u32[]{:S(2)}, u32[]{:S(2)}) collective-permute-start(bf16[4,48,768]{2,1,0:T(8,128)(2,1)S(1)} %slice_bitcast_fusion.30), channel_id=1, source_target_pairs={{0,1},{1,0},{2,3},{3,2},{4,5},{5,4},{6,7},{7,6},{8,9},{9,8},{10,11... | collective-permute-start | bytes 884744 | tf_op jit(solution)/shard_map/ppermute | solution.py:148
  217.3 14.5 %collective-permute-start.51 = (bf16[4,48,768]{2,1,0:T(8,128)(2,1)S(1)}, bf16[4,48,768]{2,1,0:T(8,128)(2,1)S(1)}, u32[]{:S(2)}, u32[]{:S(2)}) collective-permute-start(bf16[4,48,768]{2,1,0:T(8,128)(2,1)S(1)} %slice_bitcast_fusion.28), channel_id=1, source_target_pairs={{0,16},{1,17},{2,18},{3,19},{4,20},{5,21},{6,22},{7,23},{8,24},{9,... | collective-permute-start | bytes 884744 | tf_op jit(solution)/shard_map/ppermute | solution.py:140
  217.8 18.9 %collective-permute-start.59 = (bf16[4,48,768]{2,1,0:T(8,128)(2,1)S(1)}, bf16[4,48,768]{2,1,0:T(8,128)(2,1)S(1)}, u32[]{:S(2)}, u32[]{:S(2)}) collective-permute-start(bf16[4,48,768]{2,1,0:T(8,128)(2,1)S(1)} %slice_bitcast_fusion.22), channel_id=1, source_target_pairs={{0,1},{1,0},{2,3},{3,2},{4,5},{5,4},{6,7},{7,6},{8,9},{9,8},{10,11... | collective-permute-start | bytes 884744 | tf_op jit(solution)/shard_map/ppermute | solution.py:148
  225.4 14.5 %collective-permute-start.36 = (bf16[96,768]{1,0:T(8,128)(2,1)S(1)}, bf16[96,768]{1,0:T(8,128)(2,1)S(1)}, u32[]{:S(2)}, u32[]{:S(2)}) collective-permute-start(bf16[96,768]{1,0:T(8,128)(2,1)S(1)} %get-tuple-element.134), channel_id=1, source_target_pairs={{0,2},{1,3},{2,0},{3,1},{4,6},{5,7},{6,4},{7,5},{8,10},{9,11},{10,... | collective-permute-start | bytes 442376 | tf_op jit(solution)/shard_map/ppermute | solution.py:152
  236.7 17.4 %collective-permute-start.52 = (bf16[96,768]{1,0:T(8,128)(2,1)S(1)}, bf16[96,768]{1,0:T(8,128)(2,1)S(1)}, u32[]{:S(2)}, u32[]{:S(2)}) collective-permute-start(bf16[96,768]{1,0:T(8,128)(2,1)S(1)} %get-tuple-element.129), channel_id=1, source_target_pairs={{0,2},{1,3},{2,0},{3,1},{4,6},{5,7},{6,4},{7,5},{8,10},{9,11},{10,... | collective-permute-start | bytes 442376 | tf_op jit(solution)/shard_map/ppermute | solution.py:152
  236.8 17.4 %collective-permute-start.54 = (bf16[96,768]{1,0:T(8,128)(2,1)S(1)}, bf16[96,768]{1,0:T(8,128)(2,1)S(1)}, u32[]{:S(2)}, u32[]{:S(2)}) collective-permute-start(bf16[96,768]{1,0:T(8,128)(2,1)S(1)} %get-tuple-element.130), channel_id=1, source_target_pairs={{0,6},{1,7},{2,4},{3,5},{4,2},{5,3},{6,0},{7,1},{8,14},{9,15},{10,... | collective-permute-start | bytes 442376 | tf_op jit(solution)/shard_map/ppermute | solution.py:152
  239.9 23.2 %collective-permute-start.53 = (bf16[96,768]{1,0:T(8,128)(2,1)S(1)}, bf16[96,768]{1,0:T(8,128)(2,1)S(1)}, u32[]{:S(2)}, u32[]{:S(2)}) collective-permute-start(bf16[96,768]{1,0:T(8,128)(2,1)S(1)} %get-tuple-element.131), channel_id=1, source_target_pairs={{0,4},{1,5},{2,6},{3,7},{4,0},{5,1},{6,2},{7,3},{8,12},{9,13},{10,... | collective-permute-start | bytes 442376 | tf_op jit(solution)/shard_map/ppermute | solution.py:152
  240.0 24.8 %collective-permute-start.63 = (bf16[96,768]{1,0:T(8,128)(2,1)S(1)}, bf16[96,768]{1,0:T(8,128)(2,1)S(1)}, u32[]{:S(2)}, u32[]{:S(2)}) collective-permute-start(bf16[96,768]{1,0:T(8,128)(2,1)S(1)} %get-tuple-element.124), channel_id=1, source_target_pairs={{0,2},{1,3},{2,0},{3,1},{4,6},{5,7},{6,4},{7,5},{8,10},{9,11},{10,... | collective-permute-start | bytes 442376 | tf_op jit(solution)/shard_map/ppermute | solution.py:152
  245.7 19.1 %collective-permute-start.65 = (bf16[96,768]{1,0:T(8,128)(2,1)S(1)}, bf16[96,768]{1,0:T(8,128)(2,1)S(1)}, u32[]{:S(2)}, u32[]{:S(2)}) collective-permute-start(bf16[96,768]{1,0:T(8,128)(2,1)S(1)} %get-tuple-element.125), channel_id=1, source_target_pairs={{0,6},{1,7},{2,4},{3,5},{4,2},{5,3},{6,0},{7,1},{8,14},{9,15},{10,... | collective-permute-start | bytes 442376 | tf_op jit(solution)/shard_map/ppermute | solution.py:152
  254.1 15.3 %collective-permute-start.64 = (bf16[96,768]{1,0:T(8,128)(2,1)S(1)}, bf16[96,768]{1,0:T(8,128)(2,1)S(1)}, u32[]{:S(2)}, u32[]{:S(2)}) collective-permute-start(bf16[96,768]{1,0:T(8,128)(2,1)S(1)} %get-tuple-element.126), channel_id=1, source_target_pairs={{0,4},{1,5},{2,6},{3,7},{4,0},{5,1},{6,2},{7,3},{8,12},{9,13},{10,... | collective-permute-start | bytes 442376 | tf_op jit(solution)/shard_map/ppermute | solution.py:152
  254.2 17.0 %collective-permute-start.39 = (bf16[96,768]{1,0:T(8,128)(2,1)S(1)}, bf16[96,768]{1,0:T(8,128)(2,1)S(1)}, u32[]{:S(2)}, u32[]{:S(2)}) collective-permute-start(bf16[96,768]{1,0:T(8,128)(2,1)S(1)} %fusion.53), channel_id=1, source_target_pairs={{0,16},{1,17},{2,18},{3,19},{4,20},{5,21},{6,22},{7,23},{8,24},{9,... | collective-permute-start | bytes 442376 | tf_op jit(solution)/shard_map/ppermute | solution.py:140
  (89 other events, 637.9 us)

commit v2 on v0

--- a/solution.py
+++ b/solution.py
@@ -3,6 +3,8 @@
 import jax
 import jax.numpy as jnp
 from jax import lax
+from jax.experimental import pallas as pl
+from jax.experimental.pallas import tpu as pltpu
 from jax.sharding import PartitionSpec as P
 
 HEADS = 12
@@ -119,7 +121,403 @@
     )
 
 
-def on_device(
+AXES = ("replica", "shard")
+REPLICAS = 4
+SHARDS = 8
+
+
+def swap_pairs(dx, dcore, dz, dy):
+    pairs = []
+    for replica in range(REPLICAS):
+        for shard in range(SHARDS):
+            to_replica = replica ^ (dx * 2 + dcore)
+            to_shard = shard ^ (dz * 2 + dy)
+            pairs.append((replica * SHARDS + shard, to_replica * SHARDS + to_shard))
+    return pairs
+
+
+def swap_x(value):
+    return lax.ppermute(value, AXES, swap_pairs(1, 0, 0, 0))
+
+
+def swap_core(value):
+    return lax.ppermute(value, AXES, swap_pairs(0, 1, 0, 0))
+
+
+def swap_y(value):
+    return lax.ppermute(value, AXES, swap_pairs(0, 0, 0, 1))
+
+
+def swap_z(value, distance):
+    return lax.ppermute(value, AXES, swap_pairs(0, 0, distance, 0))
+
+
+def after(value, *others):
+    return lax.optimization_barrier((value,) + others)[0]
+
+
+def share(block):
+    across = swap_x(block)
+    return [block, swap_core(block), across, swap_core(across)]
+
+
+def collect(near, far):
+    pair = plus(near, swap_core(far))
+    return pair[0], swap_x(pair[1])
+
+
+def swap_zs(piece):
+    return [piece] + [swap_z(piece, distance) for distance in (1, 2, 3)]
+
+
+def halves_of(pieces):
+    half = pieces[0].shape[0] // 2
+    return [jnp.stack([entry[at : at + half] for entry in pieces]) for at in (0, half)]
+
+
+def cross_first(halves):
+    return [swap_y(halves[0]), swap_x(halves[1])]
+
+
+def near_of(halves, come):
+    return [jnp.stack(pair) for pair in zip(halves, come)]
+
+
+def cross_second(near):
+    return [swap_x(near[0]), swap_y(near[1])]
+
+
+def swap_cores(parts):
+    return [swap_core(entry) for entry in parts]
+
+
+def parts_of(near, far, core_near, core_far):
+    return [entry for group in zip(near, far, core_near, core_far) for entry in group]
+
+
+def route(leading, start, rows):
+    return [(leading, fixed, core, start, rows) for core in range(2) for fixed in range(2)]
+
+
+PLAN = route("y", 0, 48) + route("x", 48, 48)
+
+
+def plus(left_side, right_side):
+    return (left_side.astype(jnp.float32) + right_side.astype(jnp.float32)).astype(jnp.bfloat16)
+
+
+def swap_parts(parts):
+    return [swap_core(parts[at]) for at in (3, 7, 2, 6)]
+
+
+def sum_parts(parts, come):
+    far = [plus(parts[1], come[0]), plus(parts[5], come[1])]
+    return far, [plus(parts[0], come[2]), plus(parts[4], come[3])]
+
+
+def sum_plane(near, come):
+    onward = [plus(mine[1], other[1]) for mine, other in zip(near, come)]
+    return onward, [plus(mine[0], other[0]) for mine, other in zip(near, come)]
+
+
+def sum_last(stay, come):
+    return jnp.concatenate([plus(mine, other) for mine, other in zip(stay, come)], axis=1)
+
+
+def send_zs(block):
+    return [swap_z(block[distance], distance) for distance in (1, 2, 3)]
+
+
+def sum_zs(block, come):
+    total = block[0].astype(jnp.float32)
+    for entry in come:
+        total = total + entry.astype(jnp.float32)
+    return total.astype(jnp.bfloat16)
+
+
+def spread(quarter, x, core):
+    other = swap_x(quarter)
+    pair = jnp.stack([jnp.where(x == 0, quarter, other), jnp.where(x == 0, other, quarter)])
+    far = swap_core(pair)
+    return jnp.stack(
+        [jnp.where(core == 0, pair, far), jnp.where(core == 0, far, pair)], axis=1
+    ).reshape((REPLICAS,) + quarter.shape)
+
+
+KERNEL_VMEM = 24 * 2**20
+ROOT_HALF = 0.7071067811865476
+ROOT_TWO_PI = 0.3989422804014327
+VMEM = pl.BlockSpec(memory_space=pltpu.VMEM)
+SMEM = pl.BlockSpec(memory_space=pltpu.SMEM)
+ROWS_OF = (2, 1, 1, 1, 4, 1, 1, 1)
+
+
+def kernel_call(kernel, name, out_shapes, inputs, scratch=(), scalars=1):
+    return pl.pallas_call(
+        kernel,
+        out_shape=tuple(out_shapes),
+        in_specs=[SMEM] * scalars + [VMEM] * (len(inputs) - scalars),
+        out_specs=(VMEM,) * len(out_shapes),
+        scratch_shapes=list(scratch),
+        compiler_params=pltpu.CompilerParams(vmem_limit_bytes=KERNEL_VMEM),
+        cost_estimate=pl.CostEstimate(flops=2**20, bytes_accessed=2**20, transcendentals=0),
+        name=name,
+    )(*inputs)
+
+
+def places(replica, shard):
+    for at, (leading, fixed, core, start, count) in enumerate(PLAN):
+        for first in range(2):
+            x, y = (first, fixed) if leading == "x" else (fixed, first)
+            columns = pl.ds(pl.multiple_of((replica ^ (x * 2 + core)) * 768, 128), 768)
+            for z in range(4):
+                owner = shard ^ (z * 2 + y)
+                rows = pl.ds(pl.multiple_of(owner * 96 + start, 16), count)
+                yield at, first, z, rows, columns
+
+
+def segments(lengths, dim, shape):
+    at = lax.broadcasted_iota(jnp.int32, shape, dim)
+    bound = jnp.int32(0)
+    segment = jnp.zeros(shape, jnp.int32)
+    for sequence in range(lengths.shape[1]):
+        bound = bound + lengths[0, sequence]
+        segment = segment + (at >= bound).astype(jnp.int32)
+    return jnp.where(at < bound, segment, lengths.shape[1] + at), at < bound
+
+
+def head_masks(width):
+    lane = lax.broadcasted_iota(jnp.int32, (1, width), 1)
+    low = lane < width // 2
+    return low, [low.astype(jnp.bfloat16), 1.0 - low.astype(jnp.bfloat16)]
+
+
+def attend_kernel(position, lengths, tokens, packed, *refs):
+    parts, refs = refs[:8], refs[8:]
+    whole, proj, weights, context, hidden, hidden_low, normed_one, inverse_one, table, keep = refs
+    for at, first, z, rows, columns in places(position[0], position[1]):
+        whole[rows, columns] = parts[at][first, z]
+    pieces = packed[...].astype(jnp.float32)
+    row, column = 0, 0
+    for count in ROWS_OF:
+        for at in range(count):
+            if count == 2:
+                owners = range(at * 4, at * 4 + 4)
+                values = [pieces[owner : owner + 1, 0:192] for owner in owners]
+            else:
+                start = column + at * 96
+                values = [pieces[owner : owner + 1, start : start + 96] for owner in range(SHARDS)]
+            table[row : row + 1, :] = jnp.concatenate(values, axis=1)
+            row += 1
+        column += count * 96
+    for step in range(3):
+        columns = slice(step * 768, (step + 1) * 768)
+        projected = matmul(tokens[...], whole[:, columns])
+        if step == 0:
+            projected = projected + table[0:1, :]
+        if step == 2:
+            projected = projected + table[1:2, :]
+        proj[:, columns] = projected.astype(jnp.bfloat16)
+    count = tokens.shape[0]
+    across, usable = segments(lengths, 0, (count, 1))
+    along, _ = segments(lengths, 1, (1, count))
+    keep[...] = usable.astype(jnp.float32)
+    same = across == along
+    low, masks = head_masks(128)
+    for pair in range(HEADS // 2):
+        queries, key_rows, values = (
+            proj[:, step * 768 + pair * 128 : step * 768 + (pair + 1) * 128] for step in range(3)
+        )
+        sums = []
+        for which in range(2):
+            scores = matmul_nt(queries * masks[which], key_rows) * 0.125
+            masked = jnp.where(same, scores, NEG_FILL)
+            entries = jnp.exp(masked - jnp.max(masked, axis=1, keepdims=True))
+            share_of = entries / jnp.sum(entries, axis=1, keepdims=True)
+            weights[pair * 2 + which] = share_of
+            sums.append(matmul(share_of.astype(jnp.bfloat16), values))
+        context[:, pair * 128 : (pair + 1) * 128] = jnp.where(low, sums[0], sums[1]).astype(
+            jnp.bfloat16
+        )
+    attn_out = matmul(context[...], whole[:, 2304:]) + table[2:3, :]
+    result, normed, inverse = normalize(
+        tokens[...].astype(jnp.float32) + attn_out, table[3:4, :], table[4:5, :]
+    )
+    hidden[...] = result
+    hidden_low[...] = result.astype(jnp.bfloat16)
+    normed_one[...] = normed
+    inverse_one[...] = inverse
+
+
+def column_sum(values):
+    return jnp.sum(values.astype(jnp.float32), axis=0, keepdims=True)
+
+
+def attend_back_kernel(
+    position,
+    mine,
+    come,
+    grad_second,
+    normed_one,
+    inverse_one,
+    table,
+    context,
+    proj,
+    weights,
+    whole,
+    tokens,
+    *refs,
+):
+    parts, refs = refs[:8], refs[8:]
+    grad_first, grad_proj, small, total = refs
+    grad_hidden = grad_second[...] + (mine[...].astype(jnp.float32) + come[...].astype(jnp.float32))
+    grad_in, grad_gain, grad_shift = normalize_back(
+        grad_hidden, normed_one[...], inverse_one[...], table[3:4, :]
+    )
+    grad_first[...] = grad_in
+    grad_attn = grad_in.astype(jnp.bfloat16)
+    small[2:3, :] = column_sum(grad_attn)
+    small[3:4, :] = grad_gain[None, :]
+    small[4:5, :] = grad_shift[None, :]
+    total[:, 2304:] = matmul_tn(context[...], grad_attn).astype(jnp.bfloat16)
+    grad_context = matmul_nt(grad_attn, whole[:, 2304:]).astype(jnp.bfloat16)
+    low, masks = head_masks(128)
+    for pair in range(HEADS // 2):
+        queries, key_rows, values = (
+            proj[:, step * 768 + pair * 128 : step * 768 + (pair + 1) * 128] for step in range(3)
+        )
+        grad_pair = grad_context[:, pair * 128 : (pair + 1) * 128]
+        sums = []
+        for which in range(2):
+            share_of = weights[pair * 2 + which]
+            grad_probs = matmul_nt(grad_pair * masks[which], values)
+            inner = jnp.sum(share_of * grad_probs, axis=1, keepdims=True)
+            grad_scores = (share_of * (grad_probs - inner)).astype(jnp.bfloat16)
+            sums.append(
+                (
+                    matmul(grad_scores, key_rows) * 0.125,
+                    matmul_tn(grad_scores, queries) * 0.125,
+                    matmul_tn(share_of.astype(jnp.bfloat16), grad_pair),
+                )
+            )
+        for step in range(3):
+            grad_proj[:, step * 768 + pair * 128 : step * 768 + (pair + 1) * 128] = jnp.where(
+                low, sums[0][step], sums[1][step]
+            ).astype(jnp.bfloat16)
+    for step in range(3):
+        columns = slice(step * 768, (step + 1) * 768)
+        total[:, columns] = matmul_tn(tokens[...], grad_proj[:, columns]).astype(jnp.bfloat16)
+    small[0:1, :] = column_sum(grad_proj[:, :768])
+    small[1:2, :] = column_sum(grad_proj[:, 1536:])
+    for at, first, z, rows, columns in places(position[0], position[1]):
+        parts[at][first, z] = total[rows, columns]
+
+
+def tokens_kernel(position, grad_first, grad_proj, whole, grad_tokens):
+    grad_tokens[...] = (grad_first[...] + matmul_nt(grad_proj[...], whole[:, :2304])).astype(
+        jnp.bfloat16
+    )
+
+
+def fill(whole, near, far, shard):
+    for y, part in enumerate((near, far)):
+        for z in range(4):
+            owner = shard ^ (z * 2 + y)
+            whole[pl.ds(pl.multiple_of(owner * 96, 16), 96), :] = part[z]
+
+
+def drain(near, far, whole, shard):
+    for y, part in enumerate((near, far)):
+        for z in range(4):
+            owner = shard ^ (z * 2 + y)
+            part[z] = whole[pl.ds(pl.multiple_of(owner * 96, 16), 96), :]
+
+
+def feed_kernel(
+    position, own, from_core, from_x, from_both, table, up_near, up_far, down_near, down_far, *outs
+):
+    w_up, w_down, activated, slope, near, far = outs
+    fill(w_up, up_near, up_far, position[1])
+    fill(w_down, down_near, down_far, position[1])
+    bias = table[pl.ds(5 + position[0], 1), :]
+    spots = ((near, 0), (far, 0), (near, 1), (far, 1))
+    for step, block in enumerate((own, from_core, from_x, from_both)):
+        rows = slice(step * 128, (step + 1) * 128)
+        pre_act = matmul(block[...], w_up[...]) + bias
+        below = 0.5 * (1.0 + lax.erf(pre_act * ROOT_HALF))
+        active = (pre_act * below).astype(jnp.bfloat16)
+        activated[rows, :] = active
+        slope[rows, :] = below + pre_act * (ROOT_TWO_PI * jnp.exp(-0.5 * pre_act * pre_act))
+        out, at = spots[step]
+        out[at] = matmul(active, w_down[...]).astype(jnp.bfloat16)
+
+
+def close_kernel(position, mine, come, hidden, table, keep, cotangent, *outs):
+    layer_out, grad_second, grad_branch, small = outs
+    gain = table[10:11, :]
+    branch = mine[...].astype(jnp.float32) + come[...].astype(jnp.float32) + table[9:10, :]
+    output_full, normed, inverse = normalize(hidden[...] + branch, gain, table[11:12, :])
+    layer_out[...] = (output_full * keep[...]).astype(jnp.bfloat16)
+    grad_out = cotangent[...].astype(jnp.float32) * keep[...]
+    grad_in, grad_gain, grad_shift = normalize_back(grad_out, normed, inverse, gain)
+    low_grad = grad_in.astype(jnp.bfloat16)
+    grad_second[...] = grad_in
+    grad_branch[...] = low_grad
+    small[0:1, :] = jnp.sum(low_grad.astype(jnp.float32), axis=0, keepdims=True)
+    small[1:2, :] = grad_gain[None, :]
+    small[2:3, :] = grad_shift[None, :]
+
+
+def back_kernel(position, own, from_core, from_x, from_both, slope, w_up, w_down, *outs):
+    grad_pre, near, far, small = outs
+    spots = ((near, 0), (far, 0), (near, 1), (far, 1))
+    total = jnp.zeros((1, slope.shape[1]), jnp.float32)
+    for step, block in enumerate((own, from_core, from_x, from_both)):
+        rows = slice(step * 128, (step + 1) * 128)
+        grad = matmul_nt(block[...], w_down[...]) * slope[rows, :]
+        low_grad = grad.astype(jnp.bfloat16)
+        grad_pre[rows, :] = low_grad
+        total = total + jnp.sum(low_grad.astype(jnp.float32), axis=0, keepdims=True)
+        out, at = spots[step]
+        out[at] = matmul_nt(low_grad, w_up[...]).astype(jnp.bfloat16)
+    small[...] = total
+
+
+def weight_kernel(count, position, *refs):
+    blocks, right, (near, far, total) = refs[:count], refs[count:-3], refs[-3:]
+    if count == 1:
+        total[...] = matmul_tn(blocks[0][...], joined(right)).astype(jnp.bfloat16)
+    else:
+        total[...] = matmul_tn(joined(blocks), right[0][...]).astype(jnp.bfloat16)
+    drain(near, far, total, position[1])
+
+
+def joined(refs):
+    return jnp.concatenate([entry[...] for entry in refs], axis=0)
+
+
+def small_gather(vector, z, y):
+    block = vector[None]
+    other = swap_y(block)
+    block = jnp.concatenate([jnp.where(y == 0, block, other), jnp.where(y == 0, other, block)])
+    for distance in (1, 2):
+        other = swap_z(block, distance)
+        low_side = (z & distance) == 0
+        block = jnp.concatenate(
+            [jnp.where(low_side, block, other), jnp.where(low_side, other, block)]
+        )
+    return block
+
+
+def small_sum(vector):
+    vector = vector + swap_core(vector)
+    vector = vector + swap_x(vector)
+    vector = vector + swap_y(vector)
+    vector = vector + swap_z(vector, 1)
+    return vector + swap_z(vector, 2)
+
+
+def on_device_general(
     tokens,
     lengths,
     qkv_weight,
@@ -282,7 +680,217 @@
     )
 
 
+def on_device_direct(
+    tokens,
+    lengths,
+    qkv_weight,
+    qv_bias,
+    out_weight,
+    out_bias,
+    first_gain,
+    first_shift,
+    up_weight,
+    up_bias,
+    down_weight,
+    down_bias,
+    second_gain,
+    second_shift,
+    cotangent,
+):
+    rows, model_width = tokens.shape
+    replica = lax.axis_index("replica").astype(jnp.int32)
+    shard = lax.axis_index("shard").astype(jnp.int32)
+    x, core, z, y = replica // 2, replica % 2, shard // 2, shard % 2
+    position = jnp.stack([replica, shard])
+    small = (qv_bias, out_bias, first_gain, first_shift, up_bias, down_bias, second_gain, second_shift)
+
+    def shaped(*shape, dtype=jnp.bfloat16):
+        return jax.ShapeDtypeStruct(shape, dtype)
+
+    quarter_attn = jnp.where(
+        replica == 3,
+        out_weight,
+        lax.dynamic_slice_in_dim(qkv_weight, jnp.minimum(replica, 2) * 768, 768, axis=1),
+    )
+    quarter_up = lax.dynamic_index_in_dim(
+        up_weight.reshape(up_weight.shape[0], SHARDS, REPLICAS, -1), replica, 2, False
+    ).reshape(-1, 768)
+    quarter_down = lax.dynamic_slice_in_dim(down_weight, replica * 96, 96, axis=0)
+    z_attn = swap_zs(quarter_attn)
+    z_up = swap_zs(after(quarter_up, *z_attn))
+    half_attn = halves_of(z_attn)
+    first_attn = cross_first(half_attn)
+    packed = small_gather(after(jnp.concatenate(small), *first_attn), z, y)
+    near_attn = near_of(half_attn, first_attn)
+    far_attn = cross_second(near_attn)
+    z_down = swap_zs(after(quarter_down, *z_up))
+    near_up = jnp.stack(z_up)
+    far_up = swap_y(near_up)
+    near_down = jnp.stack(z_down)
+    far_down = swap_y(near_down)
+    core_attn = parts_of(near_attn, far_attn, swap_cores(near_attn), swap_cores(far_attn))
+    core_attn = [after(core_attn[0], near_up, near_down)] + core_attn[1:]
+    f32 = jnp.float32
+    (
+        w_attn,
+        proj,
+        weights,
+        context,
+        hidden,
+        hidden_low,
+        normed_one,
+        inverse_one,
+        table,
+        keep,
+    ) = kernel_call(
+        attend_kernel,
+        "attend",
+        (
+            shaped(768, 3072),
+            shaped(rows, 2304),
+            shaped(HEADS, rows, rows, dtype=f32),
+            shaped(rows, 768),
+            shaped(rows, 768, dtype=f32),
+            shaped(rows, 768),
+            shaped(rows, 768, dtype=f32),
+            shaped(rows, 1, dtype=f32),
+            shaped(12, 768, dtype=f32),
+            shaped(rows, 1, dtype=f32),
+        ),
+        [position, lengths, tokens, packed] + core_attn,
+        scalars=2,
+    )
+    hidden_blocks = share(after(hidden_low, far_up))
+    w_up, w_down, activated, slope, near, far = kernel_call(
+        feed_kernel,
+        "feed",
+        (
+            shaped(768, 768),
+            shaped(768, 768),
+            shaped(4 * rows, 768),
+            shaped(4 * rows, 768, dtype=f32),
+            shaped(2, rows, 768),
+            shaped(2, rows, 768),
+        ),
+        [position, *hidden_blocks, table, near_up, far_up, near_down, far_down],
+    )
+    mine, come = collect(near, far)
+    layer_out, grad_second, grad_branch, small_down = kernel_call(
+        close_kernel,
+        "close",
+        (
+            shaped(rows, 768),
+            shaped(rows, 768, dtype=f32),
+            shaped(rows, 768),
+            shaped(3, 768, dtype=f32),
+        ),
+        [position, mine, come, hidden, table, keep, cotangent],
+    )
+    grad_blocks = share(grad_branch)
+    grad_pre, near, far, grad_b_quarter = kernel_call(
+        back_kernel,
+        "back",
+        (
+            shaped(4 * rows, 768),
+            shaped(2, rows, 768),
+            shaped(2, rows, 768),
+            shaped(1, 768, dtype=f32),
+        ),
+        [position, *grad_blocks, slope, w_up, w_down],
+    )
+    block = shaped(4, 96, 768)
+    total = [pltpu.VMEM((768, 768), jnp.bfloat16)]
+    near_up, far_up = kernel_call(
+        partial(weight_kernel, 4),
+        "grad_up",
+        (block, block),
+        [position, *hidden_blocks, grad_pre],
+        total,
+    )
+    near_down, far_down = kernel_call(
+        partial(weight_kernel, 1),
+        "grad_down",
+        (block, block),
+        [position, activated, *grad_blocks],
+        total,
+    )
+    come_up = swap_y(far_up)
+    come_down = swap_y(after(far_down, come_up))
+    last_up = plus(near_up, come_up)
+    zs_up = send_zs(last_up)
+    mine, come = collect(near, far)
+    outs = kernel_call(
+        attend_back_kernel,
+        "attend_back",
+        tuple(shaped(2, 4, 48, 768) for _ in range(8))
+        + (
+            shaped(rows, 768, dtype=f32),
+            shaped(rows, 2304),
+            shaped(5, 768, dtype=f32),
+        ),
+        [position, mine, come, grad_second, normed_one, inverse_one, table]
+        + [context, proj, weights, w_attn, tokens],
+        [pltpu.VMEM((768, 3072), jnp.bfloat16)],
+    )
+    parts_attn = outs[:8]
+    grad_first, grad_proj, small_attn = outs[8:]
+    last_down = plus(near_down, come_down)
+    zs_down = send_zs(last_down)
+    far, near = sum_parts(parts_attn, swap_parts(parts_attn))
+    (grad_tokens,) = kernel_call(
+        tokens_kernel,
+        "grad_tokens",
+        (shaped(rows, 768),),
+        [position, after(grad_first, *far), grad_proj, w_attn],
+    )
+    small_attn = after(small_attn, *far)
+    small_total = small_sum(
+        jnp.concatenate(
+            [
+                small_attn,
+                jnp.where(jnp.arange(REPLICAS)[:, None] == replica, grad_b_quarter, 0.0),
+                small_down,
+            ]
+        )
+    )
+    near[0] = after(near[0], *zs_down)
+    onward, stay_attn = sum_plane(near, cross_second(far))
+    last_attn = sum_last(stay_attn, cross_first(onward))
+    zs_attn = send_zs(last_attn)
+    reduced_up = after(sum_zs(last_up, zs_up), *onward)
+    reduced_down = after(sum_zs(last_down, zs_down), *onward)
+    reduced_attn = sum_zs(last_attn, zs_attn)
+    d_down = spread(reduced_down, x, core).reshape(-1, 768).astype(f32)
+    up_quarters = spread(reduced_up, x, core).astype(f32)
+    d_up = jnp.stack(
+        [up_quarters[at].reshape(-1, SHARDS, 96) for at in range(REPLICAS)], axis=2
+    ).reshape(-1, 3072)
+    attn_quarters = spread(reduced_attn, x, core).astype(f32)
+    d_qkv = jnp.concatenate([attn_quarters[at] for at in range(3)], axis=1)
+    d_out = attn_quarters[3]
+    d_qv_bias = lax.dynamic_slice_in_dim(small_total[:2].reshape(-1), shard * 192, 192)
+    mine = lax.dynamic_slice_in_dim(small_total[2:], shard * 96, 96, axis=1)
+    return (
+        layer_out,
+        grad_tokens,
+        d_qkv,
+        d_qv_bias,
+        d_out,
+        mine[0],
+        mine[1],
+        mine[2],
+        d_up,
+        mine[3:7].reshape(-1),
+        d_down,
+        mine[7],
+        mine[8],
+        mine[9],
+    )
+
+
 def solution(mesh):
+    shape = dict(mesh.shape)
+    direct = shape["replica"] == REPLICAS and shape["shard"] == SHARDS
     placed = (
         P(("replica", "shard"), None),
         P(("replica", "shard"), None),
@@ -301,7 +909,7 @@
         P(("replica", "shard"), None),
     )
     return jax.shard_map(
-        on_device,
+        on_device_direct if direct else on_device_general,
         mesh=mesh,
         in_specs=placed,
         out_specs=(

time: 718 us -> 228 us (0.32)
  waiting for transfers between devices: 528 us -> 64.5 us
  starting transfers between devices: 0.58 us -> 97.8 us
  blocking collectives: 96.5 us -> 0 us
  matrix products: 42.4 us -> 0 us
  Pallas kernels: 0 us -> 26 us
  between operations: 17.8 us -> 1.45 us
  local copies, waits for them, and re-layouts: 16.9 us -> 29.3 us
    reduce_scatter x3 -> x0, waiting for transfers between devices: 262 us -> none  [the longest x1 99.4 us: on_device(): lax.psum_scatter(grad_w_up.astype(jnp.bfloat16), 'shard', scatter_dimensi...]
    all_gather x4 -> x0, waiting for transfers between devices: 195 us -> none  [the longest x1 79.2 us: on_device(): lax.all_gather(up_weight, 'shard', axis=0, tiled=True)]
    ppermute x0 -> x62, starting transfers between devices: none -> 97.8 us  [the longest x18 39.9 us: swap_core(): return lax.ppermute(value, AXES, swap_pairs(0, 1, 0, 0))]
    unnamed x10 -> x0, waiting for transfers between devices: 70.8 us -> none
    ppermute x0 -> x62, waiting for transfers between devices: none -> 64.5 us  [the longest x22 27 us: swap_z(): return lax.ppermute(value, AXES, swap_pairs(0, 0, distance, 0))]
    unnamed x2 -> x0, blocking collectives: 60.4 us -> none
    dot_general x18 -> x0, matrix products: 42.4 us -> none  [the longest x4 16.1 us: matmul(): return jnp.dot(left_side, right_side, preferred_element_type=jnp.float32)]
    pallas_call x0 -> x8, Pallas kernels: none -> 26 us  [kernel_call(): pl.pallas_call(kernel, out_shape=tuple(out_shapes), in_specs=[SMEM] * sca...]
  transfers between devices with their start and end apart: 9 -> 62, of which waited for: 8 -> 25; matrix products, arithmetic and copies ran while one was open for 5% -> 8% of each run, Pallas kernels for 0% -> 8%
where the time goes in v2:
time: 228 us
  starting transfers between devices  97.8 us (43%)
  waiting for transfers between devices  64.5 us (28%)
  local copies, waits for them, and re-layouts  29.3 us (13%)
  Pallas kernels  26 us (11%)
  other arithmetic  8.55 us (4%)
    ppermute x18, starting transfers between devices, swap_core(): return lax.ppermute(value, AXES, swap_pairs(0, 1, 0, 0))  39.9 us
    ppermute x22, starting transfers between devices, swap_z(): return lax.ppermute(value, AXES, swap_pairs(0, 0, distance, 0))  31.3 us
    ppermute x22, waiting for transfers between devices, swap_z(): return lax.ppermute(value, AXES, swap_pairs(0, 0, distance, 0))  27 us
    pallas_call x8, Pallas kernels, kernel_call(): pl.pallas_call(kernel, out_shape=tuple(out_shapes), in_specs=[SMEM] * sca...  26 us
    ppermute x12, waiting for transfers between devices, swap_x(): return lax.ppermute(value, AXES, swap_pairs(1, 0, 0, 0))  21.4 us
    unnamed x68, local copies, waits for them, and re-layouts  16.4 us
    ppermute x12, starting transfers between devices, swap_x(): return lax.ppermute(value, AXES, swap_pairs(1, 0, 0, 0))  13.4 us
    ppermute x10, starting transfers between devices, swap_y(): return lax.ppermute(value, AXES, swap_pairs(0, 0, 0, 1))  13.3 us
  transfers between devices with their start and end apart: 62, of which 25 were waited for; matrix products, arithmetic and copies ran while one was open for 8% of the time, Pallas kernels for 8%

profile of v2, /device:TPU:1, one launch (start us, length us, event | category | flops | bytes accessed | tf_op | source)
XLA Modules:
  0.0 227.6 jit_solution(12949058037127187460)
XLA Ops:
  3.9 2.3 %collective-permute-start.1 = (bf16[96,768]{1,0:T(8,128)(2,1)S(1)}, bf16[96,768]{1,0:T(8,128)(2,1)S(1)}, u32[]{:S(2)}, u32[]{:S(2)}) collective-permute-start(bf16[96,768]{1,0:T(8,128)(2,1)S(1)} %dynamic-slice_select_fusion), channel_id=1, source_target_pairs={{0,4},{1,5},{2,6},{3,7},{4,0},{5,1},{6,2},{7,3},{8,12},{9,13},{10,... | collective-permute-start | bytes 442376 | tf_op jit(solution)/shard_map/ppermute | solution.py:152
  6.2 2.3 %reshape.83 = bf16[96,8,4,96]{3,2,1,0:T(4,128)(2,1)S(1)} reshape(bf16[96,3072]{1,0:T(8,128)(2,1)} %param.23) | data formatting | bytes 1179648 | tf_op jit(solution)/shard_map/reshape | solution.py:716
  10.0 5.7 %collective-permute-done.2 = bf16[96,768]{1,0:T(8,128)(2,1)S(1)} collective-permute-done((bf16[96,768]{1,0:T(8,128)(2,1)S(1)}, bf16[96,768]{1,0:T(8,128)(2,1)S(1)}, u32[]{:S(2)}, u32[]{:S(2)}) %collective-permute-start.2) | collective-permute-done | bytes 147488 | tf_op jit(solution)/shard_map/ppermute | solution.py:152
  15.7 2.3 %collective-permute-start.10 = (bf16[96,768]{1,0:T(8,128)(2,1)S(1)}, bf16[96,768]{1,0:T(8,128)(2,1)S(1)}, u32[]{:S(2)}, u32[]{:S(2)}) collective-permute-start(bf16[96,768]{1,0:T(8,128)(2,1)S(1)} %reshape.84), channel_id=1, source_target_pairs={{0,6},{1,7},{2,4},{3,5},{4,2},{5,3},{6,0},{7,1},{8,14},{9,15},{10,... | collective-permute-start | bytes 442376 | tf_op jit(solution)/shard_map/ppermute | solution.py:152
  18.0 2.5 %collective-permute-start.8 = (bf16[96,768]{1,0:T(8,128)(2,1)S(1)}, bf16[96,768]{1,0:T(8,128)(2,1)S(1)}, u32[]{:S(2)}, u32[]{:S(2)}) collective-permute-start(bf16[96,768]{1,0:T(8,128)(2,1)S(1)} %reshape.84), channel_id=1, source_target_pairs={{0,2},{1,3},{2,0},{3,1},{4,6},{5,7},{6,4},{7,5},{8,10},{9,11},{10,... | collective-permute-start | bytes 442376 | tf_op jit(solution)/shard_map/ppermute | solution.py:152
  23.8 8.1 %collective-permute-done.9 = bf16[96,768]{1,0:T(8,128)(2,1)S(1)} collective-permute-done((bf16[96,768]{1,0:T(8,128)(2,1)S(1)}, bf16[96,768]{1,0:T(8,128)(2,1)S(1)}, u32[]{:S(2)}, u32[]{:S(2)}) %collective-permute-start.9) | collective-permute-done | bytes 147488 | tf_op jit(solution)/shard_map/ppermute | solution.py:152
  38.6 2.7 %collective-permute-done.6 = bf16[2,1152]{1,0:T(2,128)(2,1)S(1)} collective-permute-done((bf16[2,1152]{1,0:T(2,128)(2,1)S(1)}, bf16[2,1152]{1,0:T(2,128)(2,1)S(1)}, u32[]{:S(2)}, u32[]{:S(2)}) %collective-permute-start.6) | collective-permute-done | bytes 4640 | tf_op jit(solution)/shard_map/ppermute | solution.py:152
  42.5 4.8 %collective-permute-start.18 = (bf16[2,4,48,768]{3,2,1,0:T(8,128)(2,1)S(1)}, bf16[2,4,48,768]{3,2,1,0:T(8,128)(2,1)S(1)}, u32[]{:S(2)}, u32[]{:S(2)}) collective-permute-start(bf16[2,4,48,768]{3,2,1,0:T(8,128)(2,1)S(1)} %pad_maximum_fusion.5.refs_4_), channel_id=1, source_target_pairs={{0,8},{1,9},{2,10},{3,11},{4,12},{5,13},{6,14},{7,15},{8,0},{9,1},... | collective-permute-start | bytes 1769480 | tf_op jit(solution)/shard_map/ppermute | solution.py:144
  49.2 2.9 %collective-permute-done.7 = bf16[4,1152]{1,0:T(4,128)(2,1)S(1)} collective-permute-done((bf16[4,1152]{1,0:T(4,128)(2,1)S(1)}, bf16[4,1152]{1,0:T(4,128)(2,1)S(1)}, u32[]{:S(2)}, u32[]{:S(2)}) %collective-permute-start.7) | collective-permute-done | bytes 9248 | tf_op jit(solution)/shard_map/ppermute | solution.py:152
  58.6 5.3 %attend.1 = (bf16[768,3072]{1,0:T(8,128)(2,1)S(1)}, bf16[128,2304]{1,0:T(8,128)(2,1)S(1)}, f32[12,128,128]{2,1,0:T(8,128)S(1)}, bf16[128,768]{1,0:T(8,128)(2,1)S...) custom-call(s32[2]{0:T(128)S(1)} %pad_add_fusion.position, ...), custom_call_target="tpu_custom_call" | custom-call | flops 1048576 | bytes 1048576 | tf_op jit(solution)/shard_map/attend/pallas_call | solution.py:256
  70.1 3.7 %collective-permute-done.22.from_x.refs_2_ = bf16[128,768]{1,0:T(8,128)(2,1)S(1)} collective-permute-done((bf16[128,768]{1,0:T(8,128)(2,1)S(1)}, bf16[128,768]{1,0:T(8,128)(2,1)S(1)}, u32[]{:S(2)}, u32[]{:S(2)}) %collective-permute-start.22) | collective-permute-done | bytes 196640 | tf_op jit(solution)/shard_map/ppermute | solution.py:140
  76.1 2.6 %feed.1 = (bf16[768,768]{1,0:T(8,128)(2,1)S(1)}, bf16[768,768]{1,0:T(8,128)(2,1)S(1)}, bf16[512,768]{1,0:T(8,128)(2,1)S(1)}, f32[512,768]{1,0:T(8,128)S(1)}, bf1...) custom-call(s32[2]{0:T(128)S(1)} %pad_add_fusion.position, ...), custom_call_target="tpu_custom_call" | custom-call | flops 1048576 | bytes 1048576 | tf_op jit(solution)/shard_map/feed/pallas_call | solution.py:256
  83.6 4.9 %collective-permute-done.26.come = bf16[128,768]{1,0:T(8,128)(2,1)S(1)} collective-permute-done((bf16[128,768]{1,0:T(8,128)(2,1)S(1)}, bf16[128,768]{1,0:T(8,128)(2,1)S(1)}, u32[]{:S(2)}, u32[]{:S(2)}) %collective-permute-start.26) | collective-permute-done | bytes 196640 | tf_op jit(solution)/shard_map/ppermute | solution.py:140
  93.7 2.5 %collective-permute-done.28.from_x.refs_3_ = bf16[128,768]{1,0:T(8,128)(2,1)S(1)} collective-permute-done((bf16[128,768]{1,0:T(8,128)(2,1)S(1)}, bf16[128,768]{1,0:T(8,128)(2,1)S(1)}, u32[]{:S(2)}, u32[]{:S(2)}) %collective-permute-start.28) | collective-permute-done | bytes 196640 | tf_op jit(solution)/shard_map/ppermute | solution.py:140
  99.3 3.4 %back.1 = (bf16[512,768]{1,0:T(8,128)(2,1)S(1)}, bf16[2,128,768]{2,1,0:T(8,128)(2,1)S(1)}, bf16[2,128,768]{2,1,0:T(8,128)(2,1)S(1)}, f32[1,768]{1,0:T(1,128)S(1)}) custom-call(s32[2]{0:T(128)S(1)} %pad_add_fusion.position, bf16[128,768]{1,0:T(8,128)(2,1)S(1)} %get-tuple-element.76.own.refs_1_, ...), custom_call_target="tpu_custom_call" | custom-call | flops 1048576 | bytes 1048576 | tf_op jit(solution)/shard_map/back/pallas_call | solution.py:256
  103.2 2.4 %grad_up.1 = (bf16[4,96,768]{2,1,0:T(8,128)(2,1)S(1)}, bf16[4,96,768]{2,1,0:T(8,128)(2,1)}) custom-call(s32[2]{0:T(128)S(1)} %pad_add_fusion.position, bf16[128,768]{1,0:T(8,128)(2,1)S(1)} %get-tuple-element.69.own.refs_0_, bf16[128,768]{1,0:T(8,128)(2,1)S(1)} %collective-permute-done.21.from_core.refs_1_, ...), custom_call_target="tpu_custom_call" | custom-call | flops 1048576 | bytes 1048576 | tf_op jit(solution)/shard_map/grad_up/pallas_call | solution.py:256
  108.2 4.9 %collective-permute-done.31.come = bf16[128,768]{1,0:T(8,128)(2,1)S(1)} collective-permute-done((bf16[128,768]{1,0:T(8,128)(2,1)S(1)}, bf16[128,768]{1,0:T(8,128)(2,1)S(1)}, u32[]{:S(2)}, u32[]{:S(2)}) %collective-permute-start.31) | collective-permute-done | bytes 196640 | tf_op jit(solution)/shard_map/ppermute | solution.py:140
  113.7 2.3 %copy-done.3 = bf16[768,3072]{1,0:T(8,128)(2,1)S(1)} copy-done((bf16[768,3072]{1,0:T(8,128)(2,1)S(1)}, bf16[768,3072]{1,0:T(8,128)(2,1)}, u32[]{:S(2)}) %copy-start.3) | copy-done | bytes 4718616
  121.0 6.5 %attend_back.1 = (bf16[2,4,48,768]{3,2,1,0:T(8,128)(2,1)S(1)}, bf16[2,4,48,768]{3,2,1,0:T(8,128)(2,1)S(1)}, bf16[2,4,48,768]{3,2,1,0:T(8,128)(2,1)S(1)}, bf16[2,...) custom-call(s32[2]{0:T(128)S(1)} %pad_add_fusion.position, ...), custom_call_target="tpu_custom_call" | custom-call | flops 1048576 | bytes 1048576 | tf_op jit(solution)/shard_map/attend_back/pallas_call | solution.py:256
  139.0 5.1 %collective-permute-start.36 = (bf16[4,96,768]{2,1,0:T(8,128)(2,1)S(1)}, bf16[4,96,768]{2,1,0:T(8,128)(2,1)S(1)}, u32[]{:S(2)}, u32[]{:S(2)}) collective-permute-start(bf16[4,96,768]{2,1,0:T(8,128)(2,1)S(1)} %get-tuple-element.103), channel_id=1, source_target_pairs={{0,1},{1,0},{2,3},{3,2},{4,5},{5,4},{6,7},{7,6},{8,9},{9,8},{10,11... | collective-permute-start | bytes 1769480 | tf_op jit(solution)/shard_map/ppermute | solution.py:148
  148.9 6.4 %collective-permute-done.36 = bf16[4,96,768]{2,1,0:T(8,128)(2,1)S(1)} collective-permute-done((bf16[4,96,768]{2,1,0:T(8,128)(2,1)S(1)}, bf16[4,96,768]{2,1,0:T(8,128)(2,1)S(1)}, u32[]{:S(2)}, u32[]{:S(2)}) %collective-permute-start.36) | collective-permute-done | bytes 589856 | tf_op jit(solution)/shard_map/ppermute | solution.py:148
  155.3 5.7 %collective-permute-start.50 = (f32[12,768]{1,0:T(8,128)S(1)}, f32[12,768]{1,0:T(8,128)S(1)}, u32[]{:S(2)}, u32[]{:S(2)}) collective-permute-start(f32[12,768]{1,0:T(8,128)S(1)} %pad_maximum_fusion.12), channel_id=1, source_target_pairs={{0,8},{1,9},{2,10},{3,11},{4,12},{5,13},{6,14},{7,15},{8,0},{9,1},... | collective-permute-start | bytes 110600 | tf_op jit(solution)/shard_map/ppermute | solution.py:144
  169.1 2.3 %collective-permute-start.39 = (bf16[96,768]{1,0:T(8,128)(2,1)S(1)}, bf16[96,768]{1,0:T(8,128)(2,1)S(1)}, u32[]{:S(2)}, u32[]{:S(2)}) collective-permute-start(bf16[96,768]{1,0:T(8,128)(2,1)S(1)} %get-tuple-element.134), channel_id=1, source_target_pairs={{0,6},{1,7},{2,4},{3,5},{4,2},{5,3},{6,0},{7,1},{8,14},{9,15},{10,... | collective-permute-start | bytes 442376 | tf_op jit(solution)/shard_map/ppermute | solution.py:152
  171.7 4.5 %collective-permute-done.39 = bf16[96,768]{1,0:T(8,128)(2,1)S(1)} collective-permute-done((bf16[96,768]{1,0:T(8,128)(2,1)S(1)}, bf16[96,768]{1,0:T(8,128)(2,1)S(1)}, u32[]{:S(2)}, u32[]{:S(2)}) %collective-permute-start.39) | collective-permute-done | bytes 147488 | tf_op jit(solution)/shard_map/ppermute | solution.py:152
  176.3 6.2 %collective-permute-start.54 = (f32[12,768]{1,0:T(8,128)S(1)}, f32[12,768]{1,0:T(8,128)S(1)}, u32[]{:S(2)}, u32[]{:S(2)}) collective-permute-start(f32[12,768]{1,0:T(8,128)S(1)} %add.137), channel_id=1, source_target_pairs={{0,4},{1,5},{2,6},{3,7},{4,0},{5,1},{6,2},{7,3},{8,12},{9,13},{10,... | collective-permute-start | bytes 110600 | tf_op jit(solution)/shard_map/ppermute | solution.py:152
  185.7 2.3 %copy-done.4 = bf16[768,3072]{1,0:T(8,128)(2,1)S(1)} copy-done((bf16[768,3072]{1,0:T(8,128)(2,1)S(1)}, bf16[768,3072]{1,0:T(8,128)(2,1)}, u32[]{:S(2)}) %copy-start.4) | copy-done | bytes 4718616
  188.0 2.5 %grad_tokens.1 = bf16[128,768]{1,0:T(8,128)(2,1)} custom-call(s32[2]{0:T(128)S(1)} %pad_add_fusion.position, f32[128,768]{1,0:T(8,128)S(1)} %copy-done.15, bf16[128,2304]{1,0:T(8,128)(2,1)S(1)} %get-tuple-element.95.grad_proj, bf16[768,3072]{1,0:T(8,128)(2,1)S(1)} %copy-done.4), custom_call_target="tpu_custom_call" | custom-call | flops 1048576 | bytes 1048576 | tf_op jit(solution)/shard_map/grad_tokens/pallas_call | solution.py:256
  197.1 2.7 %collective-permute-done.41 = bf16[4,48,768]{2,1,0:T(8,128)(2,1)S(1)} collective-permute-done((bf16[4,48,768]{2,1,0:T(8,128)(2,1)S(1)}, bf16[4,48,768]{2,1,0:T(8,128)(2,1)S(1)}, u32[]{:S(2)}, u32[]{:S(2)}) %collective-permute-start.41) | collective-permute-done | bytes 294944 | tf_op jit(solution)/shard_map/ppermute | solution.py:148
  203.6 4.5 %collective-permute-start.61 = (bf16[2,96,768]{2,1,0:T(8,128)(2,1)S(1)}, bf16[2,96,768]{2,1,0:T(8,128)(2,1)S(1)}, u32[]{:S(2)}, u32[]{:S(2)}) collective-permute-start(bf16[2,96,768]{2,1,0:T(8,128)(2,1)S(1)} %pad_maximum_fusion.10), channel_id=1, source_target_pairs={{0,8},{1,9},{2,10},{3,11},{4,12},{5,13},{6,14},{7,15},{8,0},{9,1},... | collective-permute-start | bytes 884744 | tf_op jit(solution)/shard_map/ppermute | solution.py:144
  211.2 2.4 %collective-permute-done.48 = bf16[96,768]{1,0:T(8,128)(2,1)S(1)} collective-permute-done((bf16[96,768]{1,0:T(8,128)(2,1)S(1)}, bf16[96,768]{1,0:T(8,128)(2,1)S(1)}, u32[]{:S(2)}, u32[]{:S(2)}) %collective-permute-start.48) | collective-permute-done | bytes 147488 | tf_op jit(solution)/shard_map/ppermute | solution.py:140
  213.7 7.0 %collective-permute-start.49 = (bf16[2,96,768]{2,1,0:T(8,128)(2,1)S(1)}, bf16[2,96,768]{2,1,0:T(8,128)(2,1)S(1)}, u32[]{:S(2)}, u32[]{:S(2)}) collective-permute-start(bf16[2,96,768]{2,1,0:T(8,128)(2,1)S(1)} %pad_maximum_fusion.8), channel_id=1, source_target_pairs={{0,8},{1,9},{2,10},{3,11},{4,12},{5,13},{6,14},{7,15},{8,0},{9,1},... | collective-permute-start | bytes 884744 | tf_op jit(solution)/shard_map/ppermute | solution.py:144
  222.9 2.6 %reshape.86 = f32[96,3072]{1,0:T(8,128)} reshape(f32[96,8,4,96]{3,2,1,0:T(4,128)S(1)} %copy.33) | data formatting | bytes 2359296 | tf_op jit(solution)/shard_map/reshape | solution.py:867
  (252 shorter events, 99.7 us)
Async XLA Ops:
  1.7 8.2 %collective-permute-start = (bf16[96,768]{1,0:T(8,128)(2,1)S(1)}, bf16[96,768]{1,0:T(8,128)(2,1)S(1)}, u32[]{:S(2)}, u32[]{:S(2)}) collective-permute-start(bf16[96,768]{1,0:T(8,128)(2,1)S(1)} %dynamic-slice_select_fusion), channel_id=1, source_target_pairs={{0,2},{1,3},{2,0},{3,1},{4,6},{5,7},{6,4},{7,5},{8,10},{9,11},{10,... | collective-permute-start | bytes 442376 | tf_op jit(solution)/shard_map/ppermute | solution.py:152
  6.2 9.5 %collective-permute-start.2 = (bf16[96,768]{1,0:T(8,128)(2,1)S(1)}, bf16[96,768]{1,0:T(8,128)(2,1)S(1)}, u32[]{:S(2)}, u32[]{:S(2)}) collective-permute-start(bf16[96,768]{1,0:T(8,128)(2,1)S(1)} %dynamic-slice_select_fusion), channel_id=1, source_target_pairs={{0,6},{1,7},{2,4},{3,5},{4,2},{5,3},{6,0},{7,1},{8,14},{9,15},{10,... | collective-permute-start | bytes 442376 | tf_op jit(solution)/shard_map/ppermute | solution.py:152
  15.7 8.0 %collective-permute-start.10 = (bf16[96,768]{1,0:T(8,128)(2,1)S(1)}, bf16[96,768]{1,0:T(8,128)(2,1)S(1)}, u32[]{:S(2)}, u32[]{:S(2)}) collective-permute-start(bf16[96,768]{1,0:T(8,128)(2,1)S(1)} %reshape.84), channel_id=1, source_target_pairs={{0,6},{1,7},{2,4},{3,5},{4,2},{5,3},{6,0},{7,1},{8,14},{9,15},{10,... | collective-permute-start | bytes 442376 | tf_op jit(solution)/shard_map/ppermute | solution.py:152
  20.5 11.4 %collective-permute-start.9 = (bf16[96,768]{1,0:T(8,128)(2,1)S(1)}, bf16[96,768]{1,0:T(8,128)(2,1)S(1)}, u32[]{:S(2)}, u32[]{:S(2)}) collective-permute-start(bf16[96,768]{1,0:T(8,128)(2,1)S(1)} %reshape.84), channel_id=1, source_target_pairs={{0,4},{1,5},{2,6},{3,7},{4,0},{5,1},{6,2},{7,3},{8,12},{9,13},{10,... | collective-permute-start | bytes 442376 | tf_op jit(solution)/shard_map/ppermute | solution.py:152
  20.7 14.8 %collective-permute-start.3 = (bf16[4,48,768]{2,1,0:T(8,128)(2,1)S(1)}, bf16[4,48,768]{2,1,0:T(8,128)(2,1)S(1)}, u32[]{:S(2)}, u32[]{:S(2)}) collective-permute-start(bf16[4,48,768]{2,1,0:T(8,128)(2,1)S(1)} %get-tuple-element.150), channel_id=1, source_target_pairs={{0,1},{1,0},{2,3},{3,2},{4,5},{5,4},{6,7},{7,6},{8,9},{9,8},{10,11... | collective-permute-start | bytes 884744 | tf_op jit(solution)/shard_map/ppermute | solution.py:148
  22.1 13.4 %collective-permute-start.4 = (bf16[4,48,768]{2,1,0:T(8,128)(2,1)S(1)}, bf16[4,48,768]{2,1,0:T(8,128)(2,1)S(1)}, u32[]{:S(2)}, u32[]{:S(2)}) collective-permute-start(bf16[4,48,768]{2,1,0:T(8,128)(2,1)S(1)} %get-tuple-element.148), channel_id=1, source_target_pairs={{0,16},{1,17},{2,18},{3,19},{4,20},{5,21},{6,22},{7,23},{8,24},{9,... | collective-permute-start | bytes 884744 | tf_op jit(solution)/shard_map/ppermute | solution.py:140
  31.9 10.7 %collective-permute-start.11 = (bf16[96,768]{1,0:T(8,128)(2,1)S(1)}, bf16[96,768]{1,0:T(8,128)(2,1)S(1)}, u32[]{:S(2)}, u32[]{:S(2)}) collective-permute-start(bf16[96,768]{1,0:T(8,128)(2,1)S(1)} %constant_dynamic-slice_fusion.1), channel_id=1, source_target_pairs={{0,2},{1,3},{2,0},{3,1},{4,6},{5,7},{6,4},{7,5},{8,10},{9,11},{10,... | collective-permute-start | bytes 442376 | tf_op jit(solution)/shard_map/ppermute | solution.py:152
  31.9 15.5 %collective-permute-start.12 = (bf16[96,768]{1,0:T(8,128)(2,1)S(1)}, bf16[96,768]{1,0:T(8,128)(2,1)S(1)}, u32[]{:S(2)}, u32[]{:S(2)}) collective-permute-start(bf16[96,768]{1,0:T(8,128)(2,1)S(1)} %constant_dynamic-slice_fusion.1), channel_id=1, source_target_pairs={{0,4},{1,5},{2,6},{3,7},{4,0},{5,1},{6,2},{7,3},{8,12},{9,13},{10,... | collective-permute-start | bytes 442376 | tf_op jit(solution)/shard_map/ppermute | solution.py:152
  33.2 15.5 %collective-permute-start.13 = (bf16[96,768]{1,0:T(8,128)(2,1)S(1)}, bf16[96,768]{1,0:T(8,128)(2,1)S(1)}, u32[]{:S(2)}, u32[]{:S(2)}) collective-permute-start(bf16[96,768]{1,0:T(8,128)(2,1)S(1)} %constant_dynamic-slice_fusion.1), channel_id=1, source_target_pairs={{0,6},{1,7},{2,4},{3,5},{4,2},{5,3},{6,0},{7,1},{8,14},{9,15},{10,... | collective-permute-start | bytes 442376 | tf_op jit(solution)/shard_map/ppermute | solution.py:152
  36.9 16.6 %collective-permute-start.17 = (bf16[2,4,48,768]{3,2,1,0:T(8,128)(2,1)S(1)}, bf16[2,4,48,768]{3,2,1,0:T(8,128)(2,1)S(1)}, u32[]{:S(2)}, u32[]{:S(2)}) collective-permute-start(bf16[2,4,48,768]{3,2,1,0:T(8,128)(2,1)S(1)} %pad_maximum_fusion.5.refs_4_), channel_id=1, source_target_pairs={{0,1},{1,0},{2,3},{3,2},{4,5},{5,4},{6,7},{7,6},{8,9},{9,8},{10,11... | collective-permute-start | bytes 1769480 | tf_op jit(solution)/shard_map/ppermute | solution.py:148
  41.3 13.7 %collective-permute-start.14 = (bf16[2,4,48,768]{3,2,1,0:T(8,128)(2,1)S(1)}, bf16[2,4,48,768]{3,2,1,0:T(8,128)(2,1)S(1)}, u32[]{:S(2)}, u32[]{:S(2)}) collective-permute-start(bf16[2,4,48,768]{3,2,1,0:T(8,128)(2,1)S(1)} %pad_maximum_fusion.2.refs_0_), channel_id=1, source_target_pairs={{0,16},{1,17},{2,18},{3,19},{4,20},{5,21},{6,22},{7,23},{8,24},{9,... | collective-permute-start | bytes 1769480 | tf_op jit(solution)/shard_map/ppermute | solution.py:140
  42.5 14.5 %collective-permute-start.18 = (bf16[2,4,48,768]{3,2,1,0:T(8,128)(2,1)S(1)}, bf16[2,4,48,768]{3,2,1,0:T(8,128)(2,1)S(1)}, u32[]{:S(2)}, u32[]{:S(2)}) collective-permute-start(bf16[2,4,48,768]{3,2,1,0:T(8,128)(2,1)S(1)} %pad_maximum_fusion.5.refs_4_), channel_id=1, source_target_pairs={{0,8},{1,9},{2,10},{3,11},{4,12},{5,13},{6,14},{7,15},{8,0},{9,1},... | collective-permute-start | bytes 1769480 | tf_op jit(solution)/shard_map/ppermute | solution.py:144
  47.3 20.4 %collective-permute-start.20 = (bf16[4,96,768]{2,1,0:T(8,128)(2,1)S(1)}, bf16[4,96,768]{2,1,0:T(8,128)(2,1)S(1)}, u32[]{:S(2)}, u32[]{:S(2)}) collective-permute-start(bf16[4,96,768]{2,1,0:T(8,128)(2,1)S(1)} %pad_maximum_fusion.3.up_near), channel_id=1, source_target_pairs={{0,1},{1,0},{2,3},{3,2},{4,5},{5,4},{6,7},{7,6},{8,9},{9,8},{10,11... | collective-permute-start | bytes 1769480 | tf_op jit(solution)/shard_map/ppermute | solution.py:148
  57.0 18.4 %collective-permute-start.24 = (bf16[4,96,768]{2,1,0:T(8,128)(2,1)S(1)}, bf16[4,96,768]{2,1,0:T(8,128)(2,1)S(1)}, u32[]{:S(2)}, u32[]{:S(2)}) collective-permute-start(bf16[4,96,768]{2,1,0:T(8,128)(2,1)S(1)} %pad_maximum_fusion.4.down_near), channel_id=1, source_target_pairs={{0,1},{1,0},{2,3},{3,2},{4,5},{5,4},{6,7},{7,6},{8,9},{9,8},{10,11... | collective-permute-start | bytes 1769480 | tf_op jit(solution)/shard_map/ppermute | solution.py:148
  106.5 22.3 %collective-permute-start.35 = (bf16[4,96,768]{2,1,0:T(8,128)(2,1)}, bf16[4,96,768]{2,1,0:T(8,128)(2,1)}, u32[]{:S(2)}, u32[]{:S(2)}) collective-permute-start(bf16[4,96,768]{2,1,0:T(8,128)(2,1)} %get-tuple-element.102), channel_id=1, source_target_pairs={{0,1},{1,0},{2,3},{3,2},{4,5},{5,4},{6,7},{7,6},{8,9},{9,8},{10,11... | collective-permute-start | bytes 1769480 | tf_op jit(solution)/shard_map/ppermute | solution.py:148
  127.5 18.9 %collective-permute-start.33 = (bf16[2,4,48,768]{3,2,1,0:T(8,128)(2,1)S(1)}, bf16[2,4,48,768]{3,2,1,0:T(8,128)(2,1)S(1)}, u32[]{:S(2)}, u32[]{:S(2)}) collective-permute-start(bf16[2,4,48,768]{3,2,1,0:T(8,128)(2,1)S(1)} %get-tuple-element.93), channel_id=1, source_target_pairs={{0,8},{1,9},{2,10},{3,11},{4,12},{5,13},{6,14},{7,15},{8,0},{9,1},... | collective-permute-start | bytes 1769480 | tf_op jit(solution)/shard_map/ppermute | solution.py:144
  130.0 8.1 %collective-permute-start.55 = (bf16[96,768]{1,0:T(8,128)(2,1)S(1)}, bf16[96,768]{1,0:T(8,128)(2,1)S(1)}, u32[]{:S(2)}, u32[]{:S(2)}) collective-permute-start(bf16[96,768]{1,0:T(8,128)(2,1)S(1)} %get-tuple-element.126), channel_id=1, source_target_pairs={{0,2},{1,3},{2,0},{3,1},{4,6},{5,7},{6,4},{7,5},{8,10},{9,11},{10,... | collective-permute-start | bytes 442376 | tf_op jit(solution)/shard_map/ppermute | solution.py:152
  130.4 8.5 %collective-permute-start.56 = (bf16[96,768]{1,0:T(8,128)(2,1)S(1)}, bf16[96,768]{1,0:T(8,128)(2,1)S(1)}, u32[]{:S(2)}, u32[]{:S(2)}) collective-permute-start(bf16[96,768]{1,0:T(8,128)(2,1)S(1)} %get-tuple-element.128), channel_id=1, source_target_pairs={{0,4},{1,5},{2,6},{3,7},{4,0},{5,1},{6,2},{7,3},{8,12},{9,13},{10,... | collective-permute-start | bytes 442376 | tf_op jit(solution)/shard_map/ppermute | solution.py:152
  131.4 12.6 %collective-permute-start.57 = (bf16[96,768]{1,0:T(8,128)(2,1)S(1)}, bf16[96,768]{1,0:T(8,128)(2,1)S(1)}, u32[]{:S(2)}, u32[]{:S(2)}) collective-permute-start(bf16[96,768]{1,0:T(8,128)(2,1)S(1)} %get-tuple-element.127), channel_id=1, source_target_pairs={{0,6},{1,7},{2,4},{3,5},{4,2},{5,3},{6,0},{7,1},{8,14},{9,15},{10,... | collective-permute-start | bytes 442376 | tf_op jit(solution)/shard_map/ppermute | solution.py:152
  133.6 13.9 %collective-permute-start.32 = (bf16[2,4,48,768]{3,2,1,0:T(8,128)(2,1)S(1)}, bf16[2,4,48,768]{3,2,1,0:T(8,128)(2,1)S(1)}, u32[]{:S(2)}, u32[]{:S(2)}) collective-permute-start(bf16[2,4,48,768]{3,2,1,0:T(8,128)(2,1)S(1)} %get-tuple-element.91), channel_id=1, source_target_pairs={{0,8},{1,9},{2,10},{3,11},{4,12},{5,13},{6,14},{7,15},{8,0},{9,1},... | collective-permute-start | bytes 1769480 | tf_op jit(solution)/shard_map/ppermute | solution.py:144
  138.1 27.1 %collective-permute-start.42 = (bf16[2,4,48,768]{3,2,1,0:T(8,128)(2,1)S(1)}, bf16[2,4,48,768]{3,2,1,0:T(8,128)(2,1)S(1)}, u32[]{:S(2)}, u32[]{:S(2)}) collective-permute-start(bf16[2,4,48,768]{3,2,1,0:T(8,128)(2,1)S(1)} %get-tuple-element.106), channel_id=1, source_target_pairs={{0,8},{1,9},{2,10},{3,11},{4,12},{5,13},{6,14},{7,15},{8,0},{9,1},... | collective-permute-start | bytes 1769480 | tf_op jit(solution)/shard_map/ppermute | solution.py:144
  139.0 16.4 %collective-permute-start.36 = (bf16[4,96,768]{2,1,0:T(8,128)(2,1)S(1)}, bf16[4,96,768]{2,1,0:T(8,128)(2,1)S(1)}, u32[]{:S(2)}, u32[]{:S(2)}) collective-permute-start(bf16[4,96,768]{2,1,0:T(8,128)(2,1)S(1)} %get-tuple-element.103), channel_id=1, source_target_pairs={{0,1},{1,0},{2,3},{3,2},{4,5},{5,4},{6,7},{7,6},{8,9},{9,8},{10,11... | collective-permute-start | bytes 1769480 | tf_op jit(solution)/shard_map/ppermute | solution.py:148
  144.0 22.0 %collective-permute-start.34 = (bf16[2,4,48,768]{3,2,1,0:T(8,128)(2,1)S(1)}, bf16[2,4,48,768]{3,2,1,0:T(8,128)(2,1)S(1)}, u32[]{:S(2)}, u32[]{:S(2)}) collective-permute-start(bf16[2,4,48,768]{3,2,1,0:T(8,128)(2,1)S(1)} %get-tuple-element.97), channel_id=1, source_target_pairs={{0,8},{1,9},{2,10},{3,11},{4,12},{5,13},{6,14},{7,15},{8,0},{9,1},... | collective-permute-start | bytes 1769480 | tf_op jit(solution)/shard_map/ppermute | solution.py:144
  146.5 36.0 %collective-permute-start.43 = (bf16[2,4,48,768]{3,2,1,0:T(8,128)(2,1)S(1)}, bf16[2,4,48,768]{3,2,1,0:T(8,128)(2,1)S(1)}, u32[]{:S(2)}, u32[]{:S(2)}) collective-permute-start(bf16[2,4,48,768]{3,2,1,0:T(8,128)(2,1)S(1)} %add_convert_fusion.4), channel_id=1, source_target_pairs={{0,1},{1,0},{2,3},{3,2},{4,5},{5,4},{6,7},{7,6},{8,9},{9,8},{10,11... | collective-permute-start | bytes 1769480 | tf_op jit(solution)/shard_map/ppermute | solution.py:148
  147.6 35.8 %collective-permute-start.40 = (bf16[2,4,48,768]{3,2,1,0:T(8,128)(2,1)S(1)}, bf16[2,4,48,768]{3,2,1,0:T(8,128)(2,1)S(1)}, u32[]{:S(2)}, u32[]{:S(2)}) collective-permute-start(bf16[2,4,48,768]{3,2,1,0:T(8,128)(2,1)S(1)} %add_convert_fusion.5), channel_id=1, source_target_pairs={{0,16},{1,17},{2,18},{3,19},{4,20},{5,21},{6,22},{7,23},{8,24},{9,... | collective-permute-start | bytes 1769480 | tf_op jit(solution)/shard_map/ppermute | solution.py:140
  176.3 14.3 %collective-permute-start.54 = (f32[12,768]{1,0:T(8,128)S(1)}, f32[12,768]{1,0:T(8,128)S(1)}, u32[]{:S(2)}, u32[]{:S(2)}) collective-permute-start(f32[12,768]{1,0:T(8,128)S(1)} %add.137), channel_id=1, source_target_pairs={{0,4},{1,5},{2,6},{3,7},{4,0},{5,1},{6,2},{7,3},{8,12},{9,13},{10,... | collective-permute-start | bytes 110600 | tf_op jit(solution)/shard_map/ppermute | solution.py:152
  184.2 10.6 %collective-permute-start.58 = (bf16[96,768]{1,0:T(8,128)(2,1)}, bf16[96,768]{1,0:T(8,128)(2,1)S(1)}, u32[]{:S(2)}, u32[]{:S(2)}) collective-permute-start(bf16[96,768]{1,0:T(8,128)(2,1)} %fusion.11), channel_id=1, source_target_pairs={{0,16},{1,17},{2,18},{3,19},{4,20},{5,21},{6,22},{7,23},{8,24},{9,... | collective-permute-start | bytes 442376 | tf_op jit(solution)/shard_map/ppermute | solution.py:140
  185.5 9.3 %collective-permute-start.60 = (bf16[96,768]{1,0:T(8,128)(2,1)S(1)}, bf16[96,768]{1,0:T(8,128)(2,1)}, u32[]{:S(2)}, u32[]{:S(2)}) collective-permute-start(bf16[96,768]{1,0:T(8,128)(2,1)S(1)} %fusion.8), channel_id=1, source_target_pairs={{0,16},{1,17},{2,18},{3,19},{4,20},{5,21},{6,22},{7,23},{8,24},{9,... | collective-permute-start | bytes 442376 | tf_op jit(solution)/shard_map/ppermute | solution.py:140
  200.0 8.2 %collective-permute-start.45 = (bf16[96,768]{1,0:T(8,128)(2,1)S(1)}, bf16[96,768]{1,0:T(8,128)(2,1)S(1)}, u32[]{:S(2)}, u32[]{:S(2)}) collective-permute-start(bf16[96,768]{1,0:T(8,128)(2,1)S(1)} %get-tuple-element.131), channel_id=1, source_target_pairs={{0,2},{1,3},{2,0},{3,1},{4,6},{5,7},{6,4},{7,5},{8,10},{9,11},{10,... | collective-permute-start | bytes 442376 | tf_op jit(solution)/shard_map/ppermute | solution.py:152
  200.1 8.2 %collective-permute-start.46 = (bf16[96,768]{1,0:T(8,128)(2,1)S(1)}, bf16[96,768]{1,0:T(8,128)(2,1)S(1)}, u32[]{:S(2)}, u32[]{:S(2)}) collective-permute-start(bf16[96,768]{1,0:T(8,128)(2,1)S(1)} %get-tuple-element.133), channel_id=1, source_target_pairs={{0,4},{1,5},{2,6},{3,7},{4,0},{5,1},{6,2},{7,3},{8,12},{9,13},{10,... | collective-permute-start | bytes 442376 | tf_op jit(solution)/shard_map/ppermute | solution.py:152
  201.6 7.6 %collective-permute-start.47 = (bf16[96,768]{1,0:T(8,128)(2,1)S(1)}, bf16[96,768]{1,0:T(8,128)(2,1)S(1)}, u32[]{:S(2)}, u32[]{:S(2)}) collective-permute-start(bf16[96,768]{1,0:T(8,128)(2,1)S(1)} %get-tuple-element.132), channel_id=1, source_target_pairs={{0,6},{1,7},{2,4},{3,5},{4,2},{5,3},{6,0},{7,1},{8,14},{9,15},{10,... | collective-permute-start | bytes 442376 | tf_op jit(solution)/shard_map/ppermute | solution.py:152
  213.7 11.9 %collective-permute-start.49 = (bf16[2,96,768]{2,1,0:T(8,128)(2,1)S(1)}, bf16[2,96,768]{2,1,0:T(8,128)(2,1)S(1)}, u32[]{:S(2)}, u32[]{:S(2)}) collective-permute-start(bf16[2,96,768]{2,1,0:T(8,128)(2,1)S(1)} %pad_maximum_fusion.8), channel_id=1, source_target_pairs={{0,8},{1,9},{2,10},{3,11},{4,12},{5,13},{6,14},{7,15},{8,0},{9,1},... | collective-permute-start | bytes 884744 | tf_op jit(solution)/shard_map/ppermute | solution.py:144
  (64 other events, 305.5 us)

commit v3 on v2

--- a/solution.py
+++ b/solution.py
@@ -152,8 +152,8 @@
     return lax.ppermute(value, AXES, swap_pairs(0, 0, distance, 0))
 
 
-def after(value, *others):
-    return lax.optimization_barrier((value,) + others)[0]
+def together(*trees):
+    return lax.optimization_barrier(trees)
 
 
 def share(block):
@@ -235,16 +235,7 @@
     return total.astype(jnp.bfloat16)
 
 
-def spread(quarter, x, core):
-    other = swap_x(quarter)
-    pair = jnp.stack([jnp.where(x == 0, quarter, other), jnp.where(x == 0, other, quarter)])
-    far = swap_core(pair)
-    return jnp.stack(
-        [jnp.where(core == 0, pair, far), jnp.where(core == 0, far, pair)], axis=1
-    ).reshape((REPLICAS,) + quarter.shape)
-
-
-KERNEL_VMEM = 24 * 2**20
+KERNEL_VMEM = 10 * 2**20
 ROOT_HALF = 0.7071067811865476
 ROOT_TWO_PI = 0.3989422804014327
 VMEM = pl.BlockSpec(memory_space=pltpu.VMEM)
@@ -252,17 +243,24 @@
 ROWS_OF = (2, 1, 1, 1, 4, 1, 1, 1)
 
 
-def kernel_call(kernel, name, out_shapes, inputs, scratch=(), scalars=1):
+def kernel_call(kernel, name, out_shapes, inputs, scratch=(), scalars=1, behind=()):
+    count = len(inputs)
+
+    def body(*refs):
+        kernel(*refs[:count], *refs[count + len(behind) :])
+
     return pl.pallas_call(
-        kernel,
+        body,
         out_shape=tuple(out_shapes),
-        in_specs=[SMEM] * scalars + [VMEM] * (len(inputs) - scalars),
+        in_specs=[SMEM] * scalars
+        + [VMEM] * (count - scalars)
+        + [pl.BlockSpec(memory_space=pl.ANY)] * len(behind),
         out_specs=(VMEM,) * len(out_shapes),
         scratch_shapes=list(scratch),
         compiler_params=pltpu.CompilerParams(vmem_limit_bytes=KERNEL_VMEM),
         cost_estimate=pl.CostEstimate(flops=2**20, bytes_accessed=2**20, transcendentals=0),
         name=name,
-    )(*inputs)
+    )(*inputs, *behind)
 
 
 def places(replica, shard):
@@ -294,9 +292,11 @@
 
 def attend_kernel(position, lengths, tokens, packed, *refs):
     parts, refs = refs[:8], refs[8:]
-    whole, proj, weights, context, hidden, hidden_low, normed_one, inverse_one, table, keep = refs
+    whole, w_out, proj, weights, context, hidden, hidden_low, normed_one = refs[:8]
+    inverse_one, table, keep = refs[8:]
     for at, first, z, rows, columns in places(position[0], position[1]):
         whole[rows, columns] = parts[at][first, z]
+    w_out[...] = whole[:, 2304:]
     pieces = packed[...].astype(jnp.float32)
     row, column = 0, 0
     for count in ROWS_OF:
@@ -364,7 +364,7 @@
     context,
     proj,
     weights,
-    whole,
+    w_out,
     tokens,
     *refs,
 ):
@@ -380,7 +380,7 @@
     small[3:4, :] = grad_gain[None, :]
     small[4:5, :] = grad_shift[None, :]
     total[:, 2304:] = matmul_tn(context[...], grad_attn).astype(jnp.bfloat16)
-    grad_context = matmul_nt(grad_attn, whole[:, 2304:]).astype(jnp.bfloat16)
+    grad_context = matmul_nt(grad_attn, w_out[...]).astype(jnp.bfloat16)
     low, masks = head_masks(128)
     for pair in range(HEADS // 2):
         queries, key_rows, values = (
@@ -419,26 +419,20 @@
     )
 
 
-def fill(whole, near, far, shard):
+def blocks_of(near, far, shard):
     for y, part in enumerate((near, far)):
         for z in range(4):
             owner = shard ^ (z * 2 + y)
-            whole[pl.ds(pl.multiple_of(owner * 96, 16), 96), :] = part[z]
-
-
-def drain(near, far, whole, shard):
-    for y, part in enumerate((near, far)):
-        for z in range(4):
-            owner = shard ^ (z * 2 + y)
-            part[z] = whole[pl.ds(pl.multiple_of(owner * 96, 16), 96), :]
+            yield part, z, pl.ds(pl.multiple_of(owner * 96, 16), 96)
 
 
 def feed_kernel(
-    position, own, from_core, from_x, from_both, table, up_near, up_far, down_near, down_far, *outs
+    position, own, from_core, from_x, from_both, table, quarter_near, quarter_far, *outs
 ):
     w_up, w_down, activated, slope, near, far = outs
-    fill(w_up, up_near, up_far, position[1])
-    fill(w_down, down_near, down_far, position[1])
+    for part, z, rows in blocks_of(quarter_near, quarter_far, position[1]):
+        w_up[rows, :] = part[z, :96]
+        w_down[rows, :] = part[z, 96:]
     bias = table[pl.ds(5 + position[0], 1), :]
     spots = ((near, 0), (far, 0), (near, 1), (far, 1))
     for step, block in enumerate((own, from_core, from_x, from_both)):
@@ -483,13 +477,42 @@
     small[...] = total
 
 
-def weight_kernel(count, position, *refs):
-    blocks, right, (near, far, total) = refs[:count], refs[count:-3], refs[-3:]
-    if count == 1:
-        total[...] = matmul_tn(blocks[0][...], joined(right)).astype(jnp.bfloat16)
-    else:
-        total[...] = matmul_tn(joined(blocks), right[0][...]).astype(jnp.bfloat16)
-    drain(near, far, total, position[1])
+def weight_kernel(position, activated, grad_pre, *refs):
+    hidden_blocks, grad_blocks, (near, far, up, down) = refs[:4], refs[4:8], refs[8:]
+    up[...] = matmul_tn(joined(hidden_blocks), grad_pre[...]).astype(jnp.bfloat16)
+    down[...] = matmul_tn(activated[...], joined(grad_blocks)).astype(jnp.bfloat16)
+    for part, z, rows in blocks_of(near, far, position[1]):
+        part[z, :96] = up[rows, :]
+        part[z, 96:] = down[rows, :]
+
+
+def order(position, mine, across, other, blocks):
+    replica = position[0]
+    blocks[replica] = mine[...]
+    blocks[replica ^ 2] = across[...]
+    blocks[replica ^ 1] = other[0]
+    blocks[replica ^ 3] = other[1]
+
+
+def finish_feed_kernel(position, mine, across, other, grad_up, grad_down, blocks):
+    order(position, mine, across, other, blocks)
+    for quarter in range(REPLICAS):
+        grad_down[quarter * 96 : (quarter + 1) * 96, :] = blocks[quarter, 96:].astype(jnp.float32)
+    for owner in range(SHARDS):
+        grad_up[:, owner * 384 : (owner + 1) * 384] = jnp.concatenate(
+            [
+                blocks[quarter, :96, owner * 96 : (owner + 1) * 96].astype(jnp.float32)
+                for quarter in range(REPLICAS)
+            ],
+            axis=1,
+        )
+
+
+def finish_attend_kernel(position, mine, across, other, grad_qkv, grad_out, blocks):
+    order(position, mine, across, other, blocks)
+    for quarter in range(3):
+        grad_qkv[:, quarter * 768 : (quarter + 1) * 768] = blocks[quarter].astype(jnp.float32)
+    grad_out[...] = blocks[3].astype(jnp.float32)
 
 
 def joined(refs):
@@ -507,14 +530,6 @@
             [jnp.where(low_side, block, other), jnp.where(low_side, other, block)]
         )
     return block
-
-
-def small_sum(vector):
-    vector = vector + swap_core(vector)
-    vector = vector + swap_x(vector)
-    vector = vector + swap_y(vector)
-    vector = vector + swap_z(vector, 1)
-    return vector + swap_z(vector, 2)
 
 
 def on_device_general(
@@ -700,7 +715,7 @@
     rows, model_width = tokens.shape
     replica = lax.axis_index("replica").astype(jnp.int32)
     shard = lax.axis_index("shard").astype(jnp.int32)
-    x, core, z, y = replica // 2, replica % 2, shard // 2, shard % 2
+    z, y = shard // 2, shard % 2
     position = jnp.stack([replica, shard])
     small = (qv_bias, out_bias, first_gain, first_shift, up_bias, down_bias, second_gain, second_shift)
 
@@ -717,22 +732,21 @@
     ).reshape(-1, 768)
     quarter_down = lax.dynamic_slice_in_dim(down_weight, replica * 96, 96, axis=0)
     z_attn = swap_zs(quarter_attn)
-    z_up = swap_zs(after(quarter_up, *z_attn))
+    packed = small_gather(jnp.concatenate(small), z, y)
+    quarter_feed = jnp.concatenate([quarter_up, quarter_down])
+    z_attn, quarter_feed = together(z_attn, quarter_feed)
+    z_feed = swap_zs(quarter_feed)
     half_attn = halves_of(z_attn)
-    first_attn = cross_first(half_attn)
-    packed = small_gather(after(jnp.concatenate(small), *first_attn), z, y)
-    near_attn = near_of(half_attn, first_attn)
+    near_attn = near_of(half_attn, cross_first(half_attn))
     far_attn = cross_second(near_attn)
-    z_down = swap_zs(after(quarter_down, *z_up))
-    near_up = jnp.stack(z_up)
-    far_up = swap_y(near_up)
-    near_down = jnp.stack(z_down)
-    far_down = swap_y(near_down)
+    far_attn, near_attn, packed = together(far_attn, near_attn, packed)
     core_attn = parts_of(near_attn, far_attn, swap_cores(near_attn), swap_cores(far_attn))
-    core_attn = [after(core_attn[0], near_up, near_down)] + core_attn[1:]
+    near_feed = jnp.stack(z_feed)
+    far_feed = swap_y(near_feed)
     f32 = jnp.float32
     (
         w_attn,
+        w_out,
         proj,
         weights,
         context,
@@ -747,6 +761,7 @@
         "attend",
         (
             shaped(768, 3072),
+            shaped(768, 768),
             shaped(rows, 2304),
             shaped(HEADS, rows, rows, dtype=f32),
             shaped(rows, 768),
@@ -759,8 +774,9 @@
         ),
         [position, lengths, tokens, packed] + core_attn,
         scalars=2,
-    )
-    hidden_blocks = share(after(hidden_low, far_up))
+        behind=(near_feed,),
+    )
+    hidden_blocks = share(hidden_low)
     w_up, w_down, activated, slope, near, far = kernel_call(
         feed_kernel,
         "feed",
@@ -772,7 +788,7 @@
             shaped(2, rows, 768),
             shaped(2, rows, 768),
         ),
-        [position, *hidden_blocks, table, near_up, far_up, near_down, far_down],
+        [position, *hidden_blocks, table, near_feed, far_feed],
     )
     mine, come = collect(near, far)
     layer_out, grad_second, grad_branch, small_down = kernel_call(
@@ -798,26 +814,14 @@
         ),
         [position, *grad_blocks, slope, w_up, w_down],
     )
-    block = shaped(4, 96, 768)
-    total = [pltpu.VMEM((768, 768), jnp.bfloat16)]
-    near_up, far_up = kernel_call(
-        partial(weight_kernel, 4),
-        "grad_up",
-        (block, block),
-        [position, *hidden_blocks, grad_pre],
-        total,
-    )
-    near_down, far_down = kernel_call(
-        partial(weight_kernel, 1),
-        "grad_down",
-        (block, block),
-        [position, activated, *grad_blocks],
-        total,
-    )
-    come_up = swap_y(far_up)
-    come_down = swap_y(after(far_down, come_up))
-    last_up = plus(near_up, come_up)
-    zs_up = send_zs(last_up)
+    near_feed, far_feed = kernel_call(
+        weight_kernel,
+        "grad_feed",
+        (shaped(4, 192, 768), shaped(4, 192, 768)),
+        [position, activated, grad_pre, *hidden_blocks, *grad_blocks],
+        [pltpu.VMEM((768, 768), jnp.bfloat16)] * 2,
+    )
+    come_feed = swap_y(far_feed)
     mine, come = collect(near, far)
     outs = kernel_call(
         attend_back_kernel,
@@ -829,45 +833,64 @@
             shaped(5, 768, dtype=f32),
         ),
         [position, mine, come, grad_second, normed_one, inverse_one, table]
-        + [context, proj, weights, w_attn, tokens],
+        + [context, proj, weights, w_out, tokens],
         [pltpu.VMEM((768, 3072), jnp.bfloat16)],
+        behind=(far_feed,),
     )
     parts_attn = outs[:8]
     grad_first, grad_proj, small_attn = outs[8:]
-    last_down = plus(near_down, come_down)
-    zs_down = send_zs(last_down)
+    last_feed = plus(near_feed, come_feed)
     far, near = sum_parts(parts_attn, swap_parts(parts_attn))
+    sums = jnp.concatenate(
+        [
+            small_attn,
+            jnp.where(jnp.arange(REPLICAS)[:, None] == replica, grad_b_quarter, 0.0),
+            small_down,
+        ]
+    )
+    sums = sums + swap_z(sums, 1)
+    sums = sums + swap_z(sums, 2)
+    last_feed, sums = together(last_feed, sums)
+    come_attn, across = together(cross_second(far), swap_core(sums))
+    zs_feed = send_zs(last_feed)
+    onward, stay_attn = sum_plane(near, come_attn)
+    sums = sums + across
+    come_attn, sums, zs_feed, grad_first = together(
+        cross_first(onward), sums, zs_feed, grad_first
+    )
+    last_attn = sum_last(stay_attn, come_attn)
+    zs_attn = send_zs(last_attn)
+    reduced_feed = sum_zs(last_feed, zs_feed)
     (grad_tokens,) = kernel_call(
         tokens_kernel,
         "grad_tokens",
         (shaped(rows, 768),),
-        [position, after(grad_first, *far), grad_proj, w_attn],
-    )
-    small_attn = after(small_attn, *far)
-    small_total = small_sum(
-        jnp.concatenate(
-            [
-                small_attn,
-                jnp.where(jnp.arange(REPLICAS)[:, None] == replica, grad_b_quarter, 0.0),
-                small_down,
-            ]
-        )
-    )
-    near[0] = after(near[0], *zs_down)
-    onward, stay_attn = sum_plane(near, cross_second(far))
-    last_attn = sum_last(stay_attn, cross_first(onward))
-    zs_attn = send_zs(last_attn)
-    reduced_up = after(sum_zs(last_up, zs_up), *onward)
-    reduced_down = after(sum_zs(last_down, zs_down), *onward)
+        [position, grad_first, grad_proj, w_attn],
+    )
+    sums = sums + swap_x(sums)
+    small_total = sums + swap_y(sums)
+    far_feed = swap_x(reduced_feed)
+    core_feed = swap_core(jnp.stack([reduced_feed, far_feed]))
+    d_up, d_down = kernel_call(
+        finish_feed_kernel,
+        "finish_feed",
+        (shaped(96, 3072, dtype=f32), shaped(384, 768, dtype=f32)),
+        [position, reduced_feed, far_feed, core_feed],
+        [pltpu.VMEM((REPLICAS, 192, 768), jnp.bfloat16)],
+    )
+    zs_attn, d_up, d_down, grad_tokens, small_total = together(
+        zs_attn, d_up, d_down, grad_tokens, small_total
+    )
     reduced_attn = sum_zs(last_attn, zs_attn)
-    d_down = spread(reduced_down, x, core).reshape(-1, 768).astype(f32)
-    up_quarters = spread(reduced_up, x, core).astype(f32)
-    d_up = jnp.stack(
-        [up_quarters[at].reshape(-1, SHARDS, 96) for at in range(REPLICAS)], axis=2
-    ).reshape(-1, 3072)
-    attn_quarters = spread(reduced_attn, x, core).astype(f32)
-    d_qkv = jnp.concatenate([attn_quarters[at] for at in range(3)], axis=1)
-    d_out = attn_quarters[3]
+    far_attn = swap_x(reduced_attn)
+    core_attn = swap_core(jnp.stack([reduced_attn, far_attn]))
+    d_qkv, d_out = kernel_call(
+        finish_attend_kernel,
+        "finish_attend",
+        (shaped(96, 2304, dtype=f32), shaped(96, 768, dtype=f32)),
+        [position, reduced_attn, far_attn, core_attn],
+        [pltpu.VMEM((REPLICAS, 96, 768), jnp.bfloat16)],
+    )
     d_qv_bias = lax.dynamic_slice_in_dim(small_total[:2].reshape(-1), shard * 192, 192)
     mine = lax.dynamic_slice_in_dim(small_total[2:], shard * 96, 96, axis=1)
     return (

time: 228 us -> 205 us (0.90)
  starting transfers between devices: 97.8 us -> 74.7 us
  local copies, waits for them, and re-layouts: 29.3 us -> 16.1 us
  waiting for transfers between devices: 64.5 us -> 75.3 us
  Pallas kernels: 26 us -> 30.3 us
  other arithmetic: 8.55 us -> 6 us
    ppermute x18 -> x17, starting transfers between devices: 39.9 us -> 26.2 us  [swap_core(): return lax.ppermute(value, AXES, swap_pairs(0, 1, 0, 0))]
    unnamed x68 -> x32, local copies, waits for them, and re-layouts: 16.4 us -> 4.75 us
    ppermute x12 -> x11, waiting for transfers between devices: 21.4 us -> 30.2 us  [swap_x(): return lax.ppermute(value, AXES, swap_pairs(1, 0, 0, 0))]
    ppermute x10 -> x8, starting transfers between devices: 13.3 us -> 6.39 us  [swap_y(): return lax.ppermute(value, AXES, swap_pairs(0, 0, 0, 1))]
    ppermute x12 -> x11, starting transfers between devices: 13.4 us -> 7.51 us  [swap_x(): return lax.ppermute(value, AXES, swap_pairs(1, 0, 0, 0))]
    concatenate x1, local copies, waits for them, and re-layouts: 0.09 us -> 5.44 us  [on_device_direct(): packed = small_gather(jnp.concatenate(small), z, y)]
    ppermute x10 -> x8, waiting for transfers between devices: 11.7 us -> 7.14 us  [swap_y(): return lax.ppermute(value, AXES, swap_pairs(0, 0, 0, 1))]
    pallas_call x8 -> x9, Pallas kernels: 26 us -> 30.3 us  [kernel_call(): pl.pallas_call(body, out_shape=tuple(out_shapes), in_specs=[SMEM] * scala...]
  transfers between devices with their start and end apart: 62 -> 52, of which waited for: 25 -> 25; matrix products, arithmetic and copies ran while one was open for 8% -> 8% of each run, Pallas kernels for 8% -> 10%
where the time goes in v3:
time: 205 us; the launch traced here: 204 us
  waiting for transfers between devices  75.3 us (37%)
  starting transfers between devices  74.7 us (36%)
  Pallas kernels  30.3 us (15%)
  local copies, waits for them, and re-layouts  16.1 us (8%)
  other arithmetic  6 us (3%)
    ppermute x16, starting transfers between devices, swap_z(): return lax.ppermute(value, AXES, swap_pairs(0, 0, distance, 0))  34.5 us
    ppermute x16, waiting for transfers between devices, swap_z(): return lax.ppermute(value, AXES, swap_pairs(0, 0, distance, 0))  31 us
    pallas_call x9, Pallas kernels, kernel_call(): pl.pallas_call(body, out_shape=tuple(out_shapes), in_specs=[SMEM] * scala...  30.3 us
    ppermute x11, waiting for transfers between devices, swap_x(): return lax.ppermute(value, AXES, swap_pairs(1, 0, 0, 0))  30.2 us
    ppermute x17, starting transfers between devices, swap_core(): return lax.ppermute(value, AXES, swap_pairs(0, 1, 0, 0))  26.2 us
    ppermute x11, starting transfers between devices, swap_x(): return lax.ppermute(value, AXES, swap_pairs(1, 0, 0, 0))  7.51 us
    ppermute x8, waiting for transfers between devices, swap_y(): return lax.ppermute(value, AXES, swap_pairs(0, 0, 0, 1))  7.14 us
    ppermute x17, waiting for transfers between devices, swap_core(): return lax.ppermute(value, AXES, swap_pairs(0, 1, 0, 0))  7 us
  transfers between devices with their start and end apart: 52, of which 25 were waited for; matrix products, arithmetic and copies ran while one was open for 8% of the time, Pallas kernels for 10%

profile of v3, /device:TPU:1, one launch (start us, length us, event | category | flops | bytes accessed | tf_op | source)
XLA Modules:
  0.0 203.6 jit_solution(2069603519359394946)
XLA Ops:
  1.7 2.2 %collective-permute-start = (bf16[96,768]{1,0:T(8,128)(2,1)S(1)}, bf16[96,768]{1,0:T(8,128)(2,1)S(1)}, u32[]{:S(2)}, u32[]{:S(2)}) collective-permute-start(bf16[96,768]{1,0:T(8,128)(2,1)S(1)} %dynamic-slice_select_fusion), channel_id=1, source_target_pairs={{0,2},{1,3},{2,0},{3,1},{4,6},{5,7},{6,4},{7,5},{8,10},{9,11},{10,... | collective-permute-start | bytes 442376 | tf_op jit(solution)/shard_map/ppermute | solution.py:152
  3.9 2.3 %collective-permute-start.1 = (bf16[96,768]{1,0:T(8,128)(2,1)S(1)}, bf16[96,768]{1,0:T(8,128)(2,1)S(1)}, u32[]{:S(2)}, u32[]{:S(2)}) collective-permute-start(bf16[96,768]{1,0:T(8,128)(2,1)S(1)} %dynamic-slice_select_fusion), channel_id=1, source_target_pairs={{0,4},{1,5},{2,6},{3,7},{4,0},{5,1},{6,2},{7,3},{8,12},{9,13},{10,... | collective-permute-start | bytes 442376 | tf_op jit(solution)/shard_map/ppermute | solution.py:152
  6.2 5.4 %concatenate.22 = bf16[1152]{0:T(1024)(128)(2,1)S(1)} concatenate(bf16[192]{0:T(256)(128)(2,1)} %param.18, bf16[96]{0:T(256)(128)(2,1)} %param.20, bf16[96]{0:T(256)(128)(2,1)} %param.21, bf16[96]{0:T(256)(128)(2,1)} %param.22, bf16[384]{0:T(512)(128)(2,1)} %param.24, bf16[96]{0:T(256)(128)(2,1)} %param.26, bf16[96]{0:T(256)(128)(2,1)} %param.27, bf16[96]{0:T(256)(128)(2,1)} %param.28), dimensions={0} | concatenate | bytes 4608 | tf_op jit(solution)/shard_map/concatenate | solution.py:735
  12.9 2.3 %reshape.70 = bf16[96,8,4,96]{3,2,1,0:T(4,128)(2,1)S(1)} reshape(bf16[96,3072]{1,0:T(8,128)(2,1)} %param.23) | data formatting | bytes 1179648 | tf_op jit(solution)/shard_map/reshape | solution.py:731
  21.3 2.4 %collective-permute-start.9 = (bf16[4,1152]{1,0:T(4,128)(2,1)S(1)}, bf16[4,1152]{1,0:T(4,128)(2,1)S(1)}, u32[]{:S(2)}, u32[]{:S(2)}) collective-permute-start(bf16[4,1152]{1,0:T(4,128)(2,1)S(1)} %pad_maximum_fusion.11), channel_id=1, source_target_pairs={{0,4},{1,5},{2,6},{3,7},{4,0},{5,1},{6,2},{7,3},{8,12},{9,13},{10,... | collective-permute-start | bytes 27656 | tf_op jit(solution)/shard_map/ppermute | solution.py:152
  25.1 3.3 %collective-permute-start.16 = (bf16[192,768]{1,0:T(8,128)(2,1)S(1)}, bf16[192,768]{1,0:T(8,128)(2,1)S(1)}, u32[]{:S(2)}, u32[]{:S(2)}) collective-permute-start(bf16[192,768]{1,0:T(8,128)(2,1)S(1)} %pad_maximum_fusion.4), channel_id=1, source_target_pairs={{0,6},{1,7},{2,4},{3,5},{4,2},{5,3},{6,0},{7,1},{8,14},{9,15},{10,... | collective-permute-start | bytes 884744 | tf_op jit(solution)/shard_map/ppermute | solution.py:152
  31.5 13.9 %collective-permute-done.15 = bf16[192,768]{1,0:T(8,128)(2,1)S(1)} collective-permute-done((bf16[192,768]{1,0:T(8,128)(2,1)S(1)}, bf16[192,768]{1,0:T(8,128)(2,1)S(1)}, u32[]{:S(2)}, u32[]{:S(2)}) %collective-permute-start.15) | collective-permute-done | bytes 294944 | tf_op jit(solution)/shard_map/ppermute | solution.py:152
  47.0 5.0 %collective-permute-start.10 = (bf16[2,4,48,768]{3,2,1,0:T(8,128)(2,1)S(1)}, bf16[2,4,48,768]{3,2,1,0:T(8,128)(2,1)S(1)}, u32[]{:S(2)}, u32[]{:S(2)}) collective-permute-start(bf16[2,4,48,768]{3,2,1,0:T(8,128)(2,1)S(1)} %pad_maximum_fusion.1.refs_4_), channel_id=1, source_target_pairs={{0,8},{1,9},{2,10},{3,11},{4,12},{5,13},{6,14},{7,15},{8,0},{9,1},... | collective-permute-start | bytes 1769480 | tf_op jit(solution)/shard_map/ppermute | solution.py:144
  56.1 5.4 %attend.1 = (bf16[768,3072]{1,0:T(8,128)(2,1)S(1)}, bf16[768,768]{1,0:T(8,128)(2,1)S(1)}, bf16[128,2304]{1,0:T(8,128)(2,1)S(1)}, f32[12,128,128]{2,1,0:T(8,128)S...) custom-call(s32[2]{0:T(128)S(1)} %pad_add_fusion.refs_0_, ...), custom_call_target="tpu_custom_call" | custom-call | flops 1048576 | bytes 1048576 | tf_op jit(solution)/shard_map/attend/pallas_call | solution.py:252
  61.6 2.2 %copy-done.1 = bf16[768,3072]{1,0:T(8,128)(2,1)} copy-done((bf16[768,3072]{1,0:T(8,128)(2,1)}, bf16[768,3072]{1,0:T(8,128)(2,1)S(1)}, u32[]{:S(2)}) %copy-start.1) | copy-done | bytes 4718616
  65.4 5.2 %collective-permute-done.18.refs_3_.refs_5_ = bf16[128,768]{1,0:T(8,128)(2,1)S(1)} collective-permute-done((bf16[128,768]{1,0:T(8,128)(2,1)S(1)}, bf16[128,768]{1,0:T(8,128)(2,1)S(1)}, u32[]{:S(2)}, u32[]{:S(2)}) %collective-permute-start.18) | collective-permute-done | bytes 196640 | tf_op jit(solution)/shard_map/ppermute | solution.py:140
  72.9 2.6 %feed.1 = (bf16[768,768]{1,0:T(8,128)(2,1)S(1)}, bf16[768,768]{1,0:T(8,128)(2,1)S(1)}, bf16[512,768]{1,0:T(8,128)(2,1)S(1)}, f32[512,768]{1,0:T(8,128)S(1)}, bf1...) custom-call(s32[2]{0:T(128)S(1)} %pad_add_fusion.refs_0_, ...), custom_call_target="tpu_custom_call" | custom-call | flops 1048576 | bytes 1048576 | tf_op jit(solution)/shard_map/feed/pallas_call | solution.py:252
  78.3 6.1 %collective-permute-done.22.refs_2_ = bf16[128,768]{1,0:T(8,128)(2,1)S(1)} collective-permute-done((bf16[128,768]{1,0:T(8,128)(2,1)S(1)}, bf16[128,768]{1,0:T(8,128)(2,1)S(1)}, u32[]{:S(2)}, u32[]{:S(2)}) %collective-permute-start.22) | collective-permute-done | bytes 196640 | tf_op jit(solution)/shard_map/ppermute | solution.py:140
  88.5 3.7 %collective-permute-done.24.refs_3_.refs_9_ = bf16[128,768]{1,0:T(8,128)(2,1)S(1)} collective-permute-done((bf16[128,768]{1,0:T(8,128)(2,1)S(1)}, bf16[128,768]{1,0:T(8,128)(2,1)S(1)}, u32[]{:S(2)}, u32[]{:S(2)}) %collective-permute-start.24) | collective-permute-done | bytes 196640 | tf_op jit(solution)/shard_map/ppermute | solution.py:140
  95.3 4.2 %back.1 = (bf16[512,768]{1,0:T(8,128)(2,1)S(1)}, bf16[2,128,768]{2,1,0:T(8,128)(2,1)S(1)}, bf16[2,128,768]{2,1,0:T(8,128)(2,1)}, f32[1,768]{1,0:T(1,128)S(1)}) custom-call(s32[2]{0:T(128)S(1)} %pad_add_fusion.refs_0_, bf16[128,768]{1,0:T(8,128)(2,1)S(1)} %get-tuple-element.102.refs_1_.refs_7_, bf16[128,768]{1,0:T(8,128)(2,1)S(1)} %collective-permute-done.23.refs_2_.refs_8_, ...), custom_call_target="tpu_custom_call" | custom-call | flops 1048576 | bytes 1048576 | tf_op jit(solution)/shard_map/back/pallas_call | solution.py:252
  99.9 3.3 %grad_feed.1 = (bf16[4,192,768]{2,1,0:T(8,128)(2,1)S(1)}, bf16[4,192,768]{2,1,0:T(8,128)(2,1)}) custom-call(s32[2]{0:T(128)S(1)} %pad_add_fusion.refs_0_, bf16[512,768]{1,0:T(8,128)(2,1)S(1)} %get-tuple-element.115.refs_1_, bf16[512,768]{1,0:T(8,128)(2,1)S(1)} %get-tuple-element.116.refs_2_, bf16[128,768]{1,0:T(8,128)(2,1)S(1)} %get-tuple-element.95.refs_1_.refs_3_, ...), custom_call_target="tpu_custom_call" | custom-call | flops 1048576 | bytes 1048576 | tf_op jit(solution)/shard_map/grad_feed/pallas_call | solution.py:252
  106.3 5.9 %collective-permute-done.27.refs_2_ = bf16[128,768]{1,0:T(8,128)(2,1)S(1)} collective-permute-done((bf16[128,768]{1,0:T(8,128)(2,1)S(1)}, bf16[128,768]{1,0:T(8,128)(2,1)S(1)}, u32[]{:S(2)}, u32[]{:S(2)}) %collective-permute-start.27) | collective-permute-done | bytes 196640 | tf_op jit(solution)/shard_map/ppermute | solution.py:140
  113.2 6.5 %attend_back.1 = (bf16[2,4,48,768]{3,2,1,0:T(8,128)(2,1)S(1)}, bf16[2,4,48,768]{3,2,1,0:T(8,128)(2,1)S(1)}, bf16[2,4,48,768]{3,2,1,0:T(8,128)(2,1)S(1)}, bf16[2,...) custom-call(s32[2]{0:T(128)S(1)} %pad_add_fusion.refs_0_, ...), custom_call_target="tpu_custom_call" | custom-call | flops 1048576 | bytes 1048576 | tf_op jit(solution)/shard_map/attend_back/pallas_call | solution.py:252
  119.7 6.6 %collective-permute-start.34 = (f32[12,768]{1,0:T(8,128)S(1)}, f32[12,768]{1,0:T(8,128)S(1)}, u32[]{:S(2)}, u32[]{:S(2)}) collective-permute-start(f32[12,768]{1,0:T(8,128)S(1)} %pad_maximum_fusion.9), channel_id=1, source_target_pairs={{0,2},{1,3},{2,0},{3,1},{4,6},{5,7},{6,4},{7,5},{8,10},{9,11},{10,... | collective-permute-start | bytes 110600 | tf_op jit(solution)/shard_map/ppermute | solution.py:152
  128.8 2.2 %collective-permute-start.29 = (bf16[2,4,48,768]{3,2,1,0:T(8,128)(2,1)S(1)}, bf16[2,4,48,768]{3,2,1,0:T(8,128)(2,1)S(1)}, u32[]{:S(2)}, u32[]{:S(2)}) collective-permute-start(bf16[2,4,48,768]{3,2,1,0:T(8,128)(2,1)S(1)} %get-tuple-element.121), channel_id=1, source_target_pairs={{0,8},{1,9},{2,10},{3,11},{4,12},{5,13},{6,14},{7,15},{8,0},{9,1},... | collective-permute-start | bytes 1769480 | tf_op jit(solution)/shard_map/ppermute | solution.py:144
  132.1 2.8 %collective-permute-start.28 = (bf16[2,4,48,768]{3,2,1,0:T(8,128)(2,1)S(1)}, bf16[2,4,48,768]{3,2,1,0:T(8,128)(2,1)S(1)}, u32[]{:S(2)}, u32[]{:S(2)}) collective-permute-start(bf16[2,4,48,768]{3,2,1,0:T(8,128)(2,1)S(1)} %get-tuple-element.119), channel_id=1, source_target_pairs={{0,8},{1,9},{2,10},{3,11},{4,12},{5,13},{6,14},{7,15},{8,0},{9,1},... | collective-permute-start | bytes 1769480 | tf_op jit(solution)/shard_map/ppermute | solution.py:144
  137.3 4.9 %collective-permute-start.40 = (bf16[192,768]{1,0:T(8,128)(2,1)S(1)}, bf16[192,768]{1,0:T(8,128)(2,1)S(1)}, u32[]{:S(2)}, u32[]{:S(2)}) collective-permute-start(bf16[192,768]{1,0:T(8,128)(2,1)S(1)} %get-tuple-element.158), channel_id=1, source_target_pairs={{0,2},{1,3},{2,0},{3,1},{4,6},{5,7},{6,4},{7,5},{8,10},{9,11},{10,... | collective-permute-start | bytes 884744 | tf_op jit(solution)/shard_map/ppermute | solution.py:152
  144.7 6.5 %collective-permute-done.32 = bf16[2,4,48,768]{3,2,1,0:T(8,128)(2,1)S(1)} collective-permute-done((bf16[2,4,48,768]{3,2,1,0:T(8,128)(2,1)S(1)}, bf16[2,4,48,768]{3,2,1,0:T(8,128)(2,1)S(1)}, u32[]{:S(2)}, u32[]{:S(2)}) %collective-permute-start.32) | collective-permute-done | bytes 589856 | tf_op jit(solution)/shard_map/ppermute | solution.py:148
  153.1 10.6 %collective-permute-done.41 = bf16[192,768]{1,0:T(8,128)(2,1)S(1)} collective-permute-done((bf16[192,768]{1,0:T(8,128)(2,1)S(1)}, bf16[192,768]{1,0:T(8,128)(2,1)S(1)}, u32[]{:S(2)}, u32[]{:S(2)}) %collective-permute-start.41) | collective-permute-done | bytes 294944 | tf_op jit(solution)/shard_map/ppermute | solution.py:152
  165.2 4.3 %collective-permute-done.46.refs_2_ = bf16[192,768]{1,0:T(8,128)(2,1)S(1)} collective-permute-done((bf16[192,768]{1,0:T(8,128)(2,1)S(1)}, bf16[192,768]{1,0:T(8,128)(2,1)S(1)}, u32[]{:S(2)}, u32[]{:S(2)}) %collective-permute-start.46) | collective-permute-done | bytes 294944 | tf_op jit(solution)/shard_map/ppermute | solution.py:140
  169.6 4.2 %collective-permute-start.47 = (bf16[2,192,768]{2,1,0:T(8,128)(2,1)S(1)}, bf16[2,192,768]{2,1,0:T(8,128)(2,1)S(1)}, u32[]{:S(2)}, u32[]{:S(2)}) collective-permute-start(bf16[2,192,768]{2,1,0:T(8,128)(2,1)S(1)} %pad_maximum_fusion.3), channel_id=1, source_target_pairs={{0,8},{1,9},{2,10},{3,11},{4,12},{5,13},{6,14},{7,15},{8,0},{9,1},... | collective-permute-start | bytes 1769480 | tf_op jit(solution)/shard_map/ppermute | solution.py:144
  174.1 6.3 %collective-permute-start.43 = (bf16[96,768]{1,0:T(8,128)(2,1)S(1)}, bf16[96,768]{1,0:T(8,128)(2,1)S(1)}, u32[]{:S(2)}, u32[]{:S(2)}) collective-permute-start(bf16[96,768]{1,0:T(8,128)(2,1)S(1)} %get-tuple-element.160), channel_id=1, source_target_pairs={{0,2},{1,3},{2,0},{3,1},{4,6},{5,7},{6,4},{7,5},{8,10},{9,11},{10,... | collective-permute-start | bytes 442376 | tf_op jit(solution)/shard_map/ppermute | solution.py:152
  180.4 2.2 %collective-permute-start.45 = (bf16[96,768]{1,0:T(8,128)(2,1)S(1)}, bf16[96,768]{1,0:T(8,128)(2,1)S(1)}, u32[]{:S(2)}, u32[]{:S(2)}) collective-permute-start(bf16[96,768]{1,0:T(8,128)(2,1)S(1)} %get-tuple-element.159), channel_id=1, source_target_pairs={{0,6},{1,7},{2,4},{3,5},{4,2},{5,3},{6,0},{7,1},{8,14},{9,15},{10,... | collective-permute-start | bytes 442376 | tf_op jit(solution)/shard_map/ppermute | solution.py:152
  185.9 2.5 %grad_tokens.1 = bf16[128,768]{1,0:T(8,128)(2,1)} custom-call(s32[2]{0:T(128)S(1)} %pad_add_fusion.refs_0_, f32[128,768]{1,0:T(8,128)S(1)} %get-tuple-element.143.refs_1_, bf16[128,2304]{1,0:T(8,128)(2,1)S(1)} %get-tuple-element.144.refs_2_, bf16[768,3072]{1,0:T(8,128)(2,1)S(1)} %bitcast.87), custom_call_target="tpu_custom_call" | custom-call | flops 1048576 | bytes 1048576 | tf_op jit(solution)/shard_map/grad_tokens/pallas_call | solution.py:252
  189.1 2.4 %finish_feed.1 = (f32[96,3072]{1,0:T(8,128)}, f32[384,768]{1,0:T(8,128)}) custom-call(s32[2]{0:T(128)S(1)} %pad_add_fusion.refs_0_, bf16[192,768]{1,0:T(8,128)(2,1)S(1)} %fusion.2.refs_1_, bf16[192,768]{1,0:T(8,128)(2,1)S(1)} %collective-permute-done.46.refs_2_, bf16[2,192,768]{2,1,0:T(8,128)(2,1)S(1)} %collective-permute-done.47.refs_3_), custom_call_target="tpu_custom_call" | custom-call | flops 1048576 | bytes 1048576 | tf_op jit(solution)/shard_map/finish_feed/pallas_call | solution.py:252
  194.3 2.7 %collective-permute-done.50.refs_2_ = bf16[96,768]{1,0:T(8,128)(2,1)S(1)} collective-permute-done((bf16[96,768]{1,0:T(8,128)(2,1)S(1)}, bf16[96,768]{1,0:T(8,128)(2,1)S(1)}, u32[]{:S(2)}, u32[]{:S(2)}) %collective-permute-start.50) | collective-permute-done | bytes 147488 | tf_op jit(solution)/shard_map/ppermute | solution.py:140
  197.0 2.9 %collective-permute-start.51 = (bf16[2,96,768]{2,1,0:T(8,128)(2,1)S(1)}, bf16[2,96,768]{2,1,0:T(8,128)(2,1)S(1)}, u32[]{:S(2)}, u32[]{:S(2)}) collective-permute-start(bf16[2,96,768]{2,1,0:T(8,128)(2,1)S(1)} %pad_maximum_fusion.7), channel_id=1, source_target_pairs={{0,8},{1,9},{2,10},{3,11},{4,12},{5,13},{6,14},{7,15},{8,0},{9,1},... | collective-permute-start | bytes 884744 | tf_op jit(solution)/shard_map/ppermute | solution.py:144
  (171 shorter events, 59.4 us)
Async XLA Ops:
  1.7 17.6 %collective-permute-start = (bf16[96,768]{1,0:T(8,128)(2,1)S(1)}, bf16[96,768]{1,0:T(8,128)(2,1)S(1)}, u32[]{:S(2)}, u32[]{:S(2)}) collective-permute-start(bf16[96,768]{1,0:T(8,128)(2,1)S(1)} %dynamic-slice_select_fusion), channel_id=1, source_target_pairs={{0,2},{1,3},{2,0},{3,1},{4,6},{5,7},{6,4},{7,5},{8,10},{9,11},{10,... | collective-permute-start | bytes 442376 | tf_op jit(solution)/shard_map/ppermute | solution.py:152
  3.9 15.5 %collective-permute-start.1 = (bf16[96,768]{1,0:T(8,128)(2,1)S(1)}, bf16[96,768]{1,0:T(8,128)(2,1)S(1)}, u32[]{:S(2)}, u32[]{:S(2)}) collective-permute-start(bf16[96,768]{1,0:T(8,128)(2,1)S(1)} %dynamic-slice_select_fusion), channel_id=1, source_target_pairs={{0,4},{1,5},{2,6},{3,7},{4,0},{5,1},{6,2},{7,3},{8,12},{9,13},{10,... | collective-permute-start | bytes 442376 | tf_op jit(solution)/shard_map/ppermute | solution.py:152
  6.2 13.2 %collective-permute-start.2 = (bf16[96,768]{1,0:T(8,128)(2,1)S(1)}, bf16[96,768]{1,0:T(8,128)(2,1)S(1)}, u32[]{:S(2)}, u32[]{:S(2)}) collective-permute-start(bf16[96,768]{1,0:T(8,128)(2,1)S(1)} %dynamic-slice_select_fusion), channel_id=1, source_target_pairs={{0,6},{1,7},{2,4},{3,5},{4,2},{5,3},{6,0},{7,1},{8,14},{9,15},{10,... | collective-permute-start | bytes 442376 | tf_op jit(solution)/shard_map/ppermute | solution.py:152
  20.9 7.6 %collective-permute-start.3 = (bf16[4,48,768]{2,1,0:T(8,128)(2,1)S(1)}, bf16[4,48,768]{2,1,0:T(8,128)(2,1)S(1)}, u32[]{:S(2)}, u32[]{:S(2)}) collective-permute-start(bf16[4,48,768]{2,1,0:T(8,128)(2,1)S(1)} %get-tuple-element.169), channel_id=1, source_target_pairs={{0,1},{1,0},{2,3},{3,2},{4,5},{5,4},{6,7},{7,6},{8,9},{9,8},{10,11... | collective-permute-start | bytes 884744 | tf_op jit(solution)/shard_map/ppermute | solution.py:148
  21.3 7.5 %collective-permute-start.9 = (bf16[4,1152]{1,0:T(4,128)(2,1)S(1)}, bf16[4,1152]{1,0:T(4,128)(2,1)S(1)}, u32[]{:S(2)}, u32[]{:S(2)}) collective-permute-start(bf16[4,1152]{1,0:T(4,128)(2,1)S(1)} %pad_maximum_fusion.11), channel_id=1, source_target_pairs={{0,4},{1,5},{2,6},{3,7},{4,0},{5,1},{6,2},{7,3},{8,12},{9,13},{10,... | collective-permute-start | bytes 27656 | tf_op jit(solution)/shard_map/ppermute | solution.py:152
  23.6 7.9 %collective-permute-start.14 = (bf16[192,768]{1,0:T(8,128)(2,1)S(1)}, bf16[192,768]{1,0:T(8,128)(2,1)S(1)}, u32[]{:S(2)}, u32[]{:S(2)}) collective-permute-start(bf16[192,768]{1,0:T(8,128)(2,1)S(1)} %pad_maximum_fusion.4), channel_id=1, source_target_pairs={{0,2},{1,3},{2,0},{3,1},{4,6},{5,7},{6,4},{7,5},{8,10},{9,11},{10,... | collective-permute-start | bytes 884744 | tf_op jit(solution)/shard_map/ppermute | solution.py:152
  24.8 20.6 %collective-permute-start.15 = (bf16[192,768]{1,0:T(8,128)(2,1)S(1)}, bf16[192,768]{1,0:T(8,128)(2,1)S(1)}, u32[]{:S(2)}, u32[]{:S(2)}) collective-permute-start(bf16[192,768]{1,0:T(8,128)(2,1)S(1)} %pad_maximum_fusion.4), channel_id=1, source_target_pairs={{0,4},{1,5},{2,6},{3,7},{4,0},{5,1},{6,2},{7,3},{8,12},{9,13},{10,... | collective-permute-start | bytes 884744 | tf_op jit(solution)/shard_map/ppermute | solution.py:152
  25.1 20.3 %collective-permute-start.16 = (bf16[192,768]{1,0:T(8,128)(2,1)S(1)}, bf16[192,768]{1,0:T(8,128)(2,1)S(1)}, u32[]{:S(2)}, u32[]{:S(2)}) collective-permute-start(bf16[192,768]{1,0:T(8,128)(2,1)S(1)} %pad_maximum_fusion.4), channel_id=1, source_target_pairs={{0,6},{1,7},{2,4},{3,5},{4,2},{5,3},{6,0},{7,1},{8,14},{9,15},{10,... | collective-permute-start | bytes 884744 | tf_op jit(solution)/shard_map/ppermute | solution.py:152
  28.4 18.5 %collective-permute-start.6 = (bf16[2,4,48,768]{3,2,1,0:T(8,128)(2,1)S(1)}, bf16[2,4,48,768]{3,2,1,0:T(8,128)(2,1)S(1)}, u32[]{:S(2)}, u32[]{:S(2)}) collective-permute-start(bf16[2,4,48,768]{3,2,1,0:T(8,128)(2,1)S(1)} %pad_maximum_fusion.2.refs_8_), channel_id=1, source_target_pairs={{0,1},{1,0},{2,3},{3,2},{4,5},{5,4},{6,7},{7,6},{8,9},{9,8},{10,11... | collective-permute-start | bytes 1769480 | tf_op jit(solution)/shard_map/ppermute | solution.py:148
  28.8 18.2 %collective-permute-start.4 = (bf16[2,4,48,768]{3,2,1,0:T(8,128)(2,1)S(1)}, bf16[2,4,48,768]{3,2,1,0:T(8,128)(2,1)S(1)}, u32[]{:S(2)}, u32[]{:S(2)}) collective-permute-start(bf16[2,4,48,768]{3,2,1,0:T(8,128)(2,1)S(1)} %pad_maximum_fusion.1.refs_4_), channel_id=1, source_target_pairs={{0,16},{1,17},{2,18},{3,19},{4,20},{5,21},{6,22},{7,23},{8,24},{9,... | collective-permute-start | bytes 1769480 | tf_op jit(solution)/shard_map/ppermute | solution.py:140
  45.6 26.2 %collective-permute-start.20 = (bf16[4,192,768]{2,1,0:T(8,128)(2,1)S(1)}, bf16[4,192,768]{2,1,0:T(8,128)(2,1)S(1)}, u32[]{:S(2)}, u32[]{:S(2)}) collective-permute-start(bf16[4,192,768]{2,1,0:T(8,128)(2,1)S(1)} %pad_maximum_fusion.refs_12_.refs_6_), channel_id=1, source_target_pairs={{0,1},{1,0},{2,3},{3,2},{4,5},{5,4},{6,7},{7,6},{8,9},{9,8},{10,11... | collective-permute-start | bytes 3538952 | tf_op jit(solution)/shard_map/ppermute | solution.py:148
  47.0 6.6 %collective-permute-start.10 = (bf16[2,4,48,768]{3,2,1,0:T(8,128)(2,1)S(1)}, bf16[2,4,48,768]{3,2,1,0:T(8,128)(2,1)S(1)}, u32[]{:S(2)}, u32[]{:S(2)}) collective-permute-start(bf16[2,4,48,768]{3,2,1,0:T(8,128)(2,1)S(1)} %pad_maximum_fusion.1.refs_4_), channel_id=1, source_target_pairs={{0,8},{1,9},{2,10},{3,11},{4,12},{5,13},{6,14},{7,15},{8,0},{9,1},... | collective-permute-start | bytes 1769480 | tf_op jit(solution)/shard_map/ppermute | solution.py:144
  64.7 7.1 %collective-permute-start.17 = (bf16[128,768]{1,0:T(8,128)(2,1)S(1)}, bf16[128,768]{1,0:T(8,128)(2,1)S(1)}, u32[]{:S(2)}, u32[]{:S(2)}) collective-permute-start(bf16[128,768]{1,0:T(8,128)(2,1)S(1)} %get-tuple-element.95.refs_1_.refs_3_), channel_id=1, source_target_pairs={{0,8},{1,9},{2,10},{3,11},{4,12},{5,13},{6,14},{7,15},{8,0},{9,1},... | collective-permute-start | bytes 589832 | tf_op jit(solution)/shard_map/ppermute | solution.py:144
  87.0 7.3 %collective-permute-start.23 = (bf16[128,768]{1,0:T(8,128)(2,1)S(1)}, bf16[128,768]{1,0:T(8,128)(2,1)S(1)}, u32[]{:S(2)}, u32[]{:S(2)}) collective-permute-start(bf16[128,768]{1,0:T(8,128)(2,1)S(1)} %get-tuple-element.102.refs_1_.refs_7_), channel_id=1, source_target_pairs={{0,8},{1,9},{2,10},{3,11},{4,12},{5,13},{6,14},{7,15},{8,0},{9,1},... | collective-permute-start | bytes 589832 | tf_op jit(solution)/shard_map/ppermute | solution.py:144
  103.2 31.7 %collective-permute-start.33 = (bf16[4,192,768]{2,1,0:T(8,128)(2,1)}, bf16[4,192,768]{2,1,0:T(8,128)(2,1)}, u32[]{:S(2)}, u32[]{:S(2)}) collective-permute-start(bf16[4,192,768]{2,1,0:T(8,128)(2,1)} %get-tuple-element.117.refs_12_), channel_id=1, source_target_pairs={{0,1},{1,0},{2,3},{3,2},{4,5},{5,4},{6,7},{7,6},{8,9},{9,8},{10,11... | collective-permute-start | bytes 3538952 | tf_op jit(solution)/shard_map/ppermute | solution.py:148
  106.0 6.2 %collective-permute-start.27 = (bf16[128,768]{1,0:T(8,128)(2,1)S(1)}, bf16[128,768]{1,0:T(8,128)(2,1)S(1)}, u32[]{:S(2)}, u32[]{:S(2)}) collective-permute-start(bf16[128,768]{1,0:T(8,128)(2,1)S(1)} %get-tuple-element.162), channel_id=1, source_target_pairs={{0,16},{1,17},{2,18},{3,19},{4,20},{5,21},{6,22},{7,23},{8,24},{9,... | collective-permute-start | bytes 589832 | tf_op jit(solution)/shard_map/ppermute | solution.py:140
  119.7 8.5 %collective-permute-start.34 = (f32[12,768]{1,0:T(8,128)S(1)}, f32[12,768]{1,0:T(8,128)S(1)}, u32[]{:S(2)}, u32[]{:S(2)}) collective-permute-start(f32[12,768]{1,0:T(8,128)S(1)} %pad_maximum_fusion.9), channel_id=1, source_target_pairs={{0,2},{1,3},{2,0},{3,1},{4,6},{5,7},{6,4},{7,5},{8,10},{9,11},{10,... | collective-permute-start | bytes 110600 | tf_op jit(solution)/shard_map/ppermute | solution.py:152
  126.3 10.2 %collective-permute-start.31 = (bf16[2,4,48,768]{3,2,1,0:T(8,128)(2,1)S(1)}, bf16[2,4,48,768]{3,2,1,0:T(8,128)(2,1)S(1)}, u32[]{:S(2)}, u32[]{:S(2)}) collective-permute-start(bf16[2,4,48,768]{3,2,1,0:T(8,128)(2,1)S(1)} %get-tuple-element.123), channel_id=1, source_target_pairs={{0,8},{1,9},{2,10},{3,11},{4,12},{5,13},{6,14},{7,15},{8,0},{9,1},... | collective-permute-start | bytes 1769480 | tf_op jit(solution)/shard_map/ppermute | solution.py:144
  128.8 8.2 %collective-permute-start.29 = (bf16[2,4,48,768]{3,2,1,0:T(8,128)(2,1)S(1)}, bf16[2,4,48,768]{3,2,1,0:T(8,128)(2,1)S(1)}, u32[]{:S(2)}, u32[]{:S(2)}) collective-permute-start(bf16[2,4,48,768]{3,2,1,0:T(8,128)(2,1)S(1)} %get-tuple-element.121), channel_id=1, source_target_pairs={{0,8},{1,9},{2,10},{3,11},{4,12},{5,13},{6,14},{7,15},{8,0},{9,1},... | collective-permute-start | bytes 1769480 | tf_op jit(solution)/shard_map/ppermute | solution.py:144
  131.0 6.3 %collective-permute-start.38 = (bf16[2,4,48,768]{3,2,1,0:T(8,128)(2,1)S(1)}, bf16[2,4,48,768]{3,2,1,0:T(8,128)(2,1)S(1)}, u32[]{:S(2)}, u32[]{:S(2)}) collective-permute-start(bf16[2,4,48,768]{3,2,1,0:T(8,128)(2,1)S(1)} %get-tuple-element.131), channel_id=1, source_target_pairs={{0,8},{1,9},{2,10},{3,11},{4,12},{5,13},{6,14},{7,15},{8,0},{9,1},... | collective-permute-start | bytes 1769480 | tf_op jit(solution)/shard_map/ppermute | solution.py:144
  132.1 10.2 %collective-permute-start.28 = (bf16[2,4,48,768]{3,2,1,0:T(8,128)(2,1)S(1)}, bf16[2,4,48,768]{3,2,1,0:T(8,128)(2,1)S(1)}, u32[]{:S(2)}, u32[]{:S(2)}) collective-permute-start(bf16[2,4,48,768]{3,2,1,0:T(8,128)(2,1)S(1)} %get-tuple-element.119), channel_id=1, source_target_pairs={{0,8},{1,9},{2,10},{3,11},{4,12},{5,13},{6,14},{7,15},{8,0},{9,1},... | collective-permute-start | bytes 1769480 | tf_op jit(solution)/shard_map/ppermute | solution.py:144
  136.7 14.5 %collective-permute-start.32 = (bf16[2,4,48,768]{3,2,1,0:T(8,128)(2,1)S(1)}, bf16[2,4,48,768]{3,2,1,0:T(8,128)(2,1)S(1)}, u32[]{:S(2)}, u32[]{:S(2)}) collective-permute-start(bf16[2,4,48,768]{3,2,1,0:T(8,128)(2,1)S(1)} %add_convert_fusion.2), channel_id=1, source_target_pairs={{0,1},{1,0},{2,3},{3,2},{4,5},{5,4},{6,7},{7,6},{8,9},{9,8},{10,11... | collective-permute-start | bytes 1769480 | tf_op jit(solution)/shard_map/ppermute | solution.py:148
  137.1 14.2 %collective-permute-start.30 = (bf16[2,4,48,768]{3,2,1,0:T(8,128)(2,1)S(1)}, bf16[2,4,48,768]{3,2,1,0:T(8,128)(2,1)S(1)}, u32[]{:S(2)}, u32[]{:S(2)}) collective-permute-start(bf16[2,4,48,768]{3,2,1,0:T(8,128)(2,1)S(1)} %add_convert_fusion.3), channel_id=1, source_target_pairs={{0,16},{1,17},{2,18},{3,19},{4,20},{5,21},{6,22},{7,23},{8,24},{9,... | collective-permute-start | bytes 1769480 | tf_op jit(solution)/shard_map/ppermute | solution.py:140
  137.3 15.7 %collective-permute-start.40 = (bf16[192,768]{1,0:T(8,128)(2,1)S(1)}, bf16[192,768]{1,0:T(8,128)(2,1)S(1)}, u32[]{:S(2)}, u32[]{:S(2)}) collective-permute-start(bf16[192,768]{1,0:T(8,128)(2,1)S(1)} %get-tuple-element.158), channel_id=1, source_target_pairs={{0,2},{1,3},{2,0},{3,1},{4,6},{5,7},{6,4},{7,5},{8,10},{9,11},{10,... | collective-permute-start | bytes 884744 | tf_op jit(solution)/shard_map/ppermute | solution.py:152
  142.3 21.4 %collective-permute-start.41 = (bf16[192,768]{1,0:T(8,128)(2,1)S(1)}, bf16[192,768]{1,0:T(8,128)(2,1)S(1)}, u32[]{:S(2)}, u32[]{:S(2)}) collective-permute-start(bf16[192,768]{1,0:T(8,128)(2,1)S(1)} %get-tuple-element.157), channel_id=1, source_target_pairs={{0,4},{1,5},{2,6},{3,7},{4,0},{5,1},{6,2},{7,3},{8,12},{9,13},{10,... | collective-permute-start | bytes 884744 | tf_op jit(solution)/shard_map/ppermute | solution.py:152
  142.6 21.1 %collective-permute-start.42 = (bf16[192,768]{1,0:T(8,128)(2,1)S(1)}, bf16[192,768]{1,0:T(8,128)(2,1)S(1)}, u32[]{:S(2)}, u32[]{:S(2)}) collective-permute-start(bf16[192,768]{1,0:T(8,128)(2,1)S(1)} %get-tuple-element.156), channel_id=1, source_target_pairs={{0,6},{1,7},{2,4},{3,5},{4,2},{5,3},{6,0},{7,1},{8,14},{9,15},{10,... | collective-permute-start | bytes 884744 | tf_op jit(solution)/shard_map/ppermute | solution.py:152
  151.4 12.3 %collective-permute-start.39 = (bf16[4,48,768]{2,1,0:T(8,128)(2,1)S(1)}, bf16[4,48,768]{2,1,0:T(8,128)(2,1)S(1)}, u32[]{:S(2)}, u32[]{:S(2)}) collective-permute-start(bf16[4,48,768]{2,1,0:T(8,128)(2,1)S(1)} %fusion.7), channel_id=1, source_target_pairs={{0,16},{1,17},{2,18},{3,19},{4,20},{5,21},{6,22},{7,23},{8,24},{9,... | collective-permute-start | bytes 884744 | tf_op jit(solution)/shard_map/ppermute | solution.py:140
  151.6 12.1 %collective-permute-start.37 = (bf16[4,48,768]{2,1,0:T(8,128)(2,1)S(1)}, bf16[4,48,768]{2,1,0:T(8,128)(2,1)S(1)}, u32[]{:S(2)}, u32[]{:S(2)}) collective-permute-start(bf16[4,48,768]{2,1,0:T(8,128)(2,1)S(1)} %fusion.6), channel_id=1, source_target_pairs={{0,1},{1,0},{2,3},{3,2},{4,5},{5,4},{6,7},{7,6},{8,9},{9,8},{10,11... | collective-permute-start | bytes 884744 | tf_op jit(solution)/shard_map/ppermute | solution.py:148
  169.6 19.6 %collective-permute-start.47 = (bf16[2,192,768]{2,1,0:T(8,128)(2,1)S(1)}, bf16[2,192,768]{2,1,0:T(8,128)(2,1)S(1)}, u32[]{:S(2)}, u32[]{:S(2)}) collective-permute-start(bf16[2,192,768]{2,1,0:T(8,128)(2,1)S(1)} %pad_maximum_fusion.3), channel_id=1, source_target_pairs={{0,8},{1,9},{2,10},{3,11},{4,12},{5,13},{6,14},{7,15},{8,0},{9,1},... | collective-permute-start | bytes 1769480 | tf_op jit(solution)/shard_map/ppermute | solution.py:144
  174.1 17.4 %collective-permute-start.43 = (bf16[96,768]{1,0:T(8,128)(2,1)S(1)}, bf16[96,768]{1,0:T(8,128)(2,1)S(1)}, u32[]{:S(2)}, u32[]{:S(2)}) collective-permute-start(bf16[96,768]{1,0:T(8,128)(2,1)S(1)} %get-tuple-element.160), channel_id=1, source_target_pairs={{0,2},{1,3},{2,0},{3,1},{4,6},{5,7},{6,4},{7,5},{8,10},{9,11},{10,... | collective-permute-start | bytes 442376 | tf_op jit(solution)/shard_map/ppermute | solution.py:152
  180.4 12.5 %collective-permute-start.44 = (bf16[96,768]{1,0:T(8,128)(2,1)S(1)}, bf16[96,768]{1,0:T(8,128)(2,1)S(1)}, u32[]{:S(2)}, u32[]{:S(2)}) collective-permute-start(bf16[96,768]{1,0:T(8,128)(2,1)S(1)} %get-tuple-element.161), channel_id=1, source_target_pairs={{0,4},{1,5},{2,6},{3,7},{4,0},{5,1},{6,2},{7,3},{8,12},{9,13},{10,... | collective-permute-start | bytes 442376 | tf_op jit(solution)/shard_map/ppermute | solution.py:152
  180.4 12.5 %collective-permute-start.45 = (bf16[96,768]{1,0:T(8,128)(2,1)S(1)}, bf16[96,768]{1,0:T(8,128)(2,1)S(1)}, u32[]{:S(2)}, u32[]{:S(2)}) collective-permute-start(bf16[96,768]{1,0:T(8,128)(2,1)S(1)} %get-tuple-element.159), channel_id=1, source_target_pairs={{0,6},{1,7},{2,4},{3,5},{4,2},{5,3},{6,0},{7,1},{8,14},{9,15},{10,... | collective-permute-start | bytes 442376 | tf_op jit(solution)/shard_map/ppermute | solution.py:152
  (36 other events, 274.7 us)

commit v4 on v3

--- a/solution.py
+++ b/solution.py
@@ -850,26 +850,28 @@
     )
     sums = sums + swap_z(sums, 1)
     sums = sums + swap_z(sums, 2)
-    last_feed, sums = together(last_feed, sums)
-    come_attn, across = together(cross_second(far), swap_core(sums))
+    come_attn = cross_second(far)
     zs_feed = send_zs(last_feed)
     onward, stay_attn = sum_plane(near, come_attn)
-    sums = sums + across
     come_attn, sums, zs_feed, grad_first = together(
         cross_first(onward), sums, zs_feed, grad_first
     )
     last_attn = sum_last(stay_attn, come_attn)
     zs_attn = send_zs(last_attn)
     reduced_feed = sum_zs(last_feed, zs_feed)
+    far_feed = swap_x(reduced_feed)
     (grad_tokens,) = kernel_call(
         tokens_kernel,
         "grad_tokens",
         (shaped(rows, 768),),
         [position, grad_first, grad_proj, w_attn],
     )
+    sums = sums + swap_core(sums)
     sums = sums + swap_x(sums)
     small_total = sums + swap_y(sums)
-    far_feed = swap_x(reduced_feed)
+    zs_attn, far_feed, grad_tokens, small_total = together(
+        zs_attn, far_feed, grad_tokens, small_total
+    )
     core_feed = swap_core(jnp.stack([reduced_feed, far_feed]))
     d_up, d_down = kernel_call(
         finish_feed_kernel,
@@ -877,9 +879,6 @@
         (shaped(96, 3072, dtype=f32), shaped(384, 768, dtype=f32)),
         [position, reduced_feed, far_feed, core_feed],
         [pltpu.VMEM((REPLICAS, 192, 768), jnp.bfloat16)],
-    )
-    zs_attn, d_up, d_down, grad_tokens, small_total = together(
-        zs_attn, d_up, d_down, grad_tokens, small_total
     )
     reduced_attn = sum_zs(last_attn, zs_attn)
     far_attn = swap_x(reduced_attn)

time: 205 us -> 198 us (0.966)
  starting transfers between devices: 74.7 us -> 59.1 us
  waiting for transfers between devices: 75.3 us -> 83.1 us
  local copies, waits for them, and re-layouts: 16.1 us -> 19.4 us
    ppermute x16, starting transfers between devices: 34.5 us -> 24.1 us  [swap_z(): return lax.ppermute(value, AXES, swap_pairs(0, 0, distance, 0))]
    ppermute x17, starting transfers between devices: 26.2 us -> 20.4 us  [swap_core(): return lax.ppermute(value, AXES, swap_pairs(0, 1, 0, 0))]
    ppermute x8, waiting for transfers between devices: 7.14 us -> 12.3 us  [swap_y(): return lax.ppermute(value, AXES, swap_pairs(0, 0, 0, 1))]
    ppermute x16, waiting for transfers between devices: 31 us -> 33.7 us  [swap_z(): return lax.ppermute(value, AXES, swap_pairs(0, 0, distance, 0))]
    unnamed x32 -> x34, local copies, waits for them, and re-layouts: 4.75 us -> 7.34 us
    ppermute x8, starting transfers between devices: 6.39 us -> 8.7 us  [swap_y(): return lax.ppermute(value, AXES, swap_pairs(0, 0, 0, 1))]
  transfers between devices with their start and end apart: 52 -> 52, of which waited for: 25 -> 24; matrix products, arithmetic and copies ran while one was open for 8% -> 7% of each run, Pallas kernels for 10% -> 10%
where the time goes in v4:
time: 198 us
  waiting for transfers between devices  83.1 us (42%)
  starting transfers between devices  59.1 us (30%)
  Pallas kernels  29.9 us (15%)
  local copies, waits for them, and re-layouts  19.4 us (10%)
  other arithmetic  4.85 us (2%)
    ppermute x16, waiting for transfers between devices, swap_z(): return lax.ppermute(value, AXES, swap_pairs(0, 0, distance, 0))  33.7 us
    pallas_call x9, Pallas kernels, kernel_call(): pl.pallas_call(body, out_shape=tuple(out_shapes), in_specs=[SMEM] * scala...  29.9 us
    ppermute x11, waiting for transfers between devices, swap_x(): return lax.ppermute(value, AXES, swap_pairs(1, 0, 0, 0))  28.9 us
    ppermute x16, starting transfers between devices, swap_z(): return lax.ppermute(value, AXES, swap_pairs(0, 0, distance, 0))  24.1 us
    ppermute x17, starting transfers between devices, swap_core(): return lax.ppermute(value, AXES, swap_pairs(0, 1, 0, 0))  20.4 us
    ppermute x8, waiting for transfers between devices, swap_y(): return lax.ppermute(value, AXES, swap_pairs(0, 0, 0, 1))  12.3 us
    ppermute x8, starting transfers between devices, swap_y(): return lax.ppermute(value, AXES, swap_pairs(0, 0, 0, 1))  8.7 us
    ppermute x17, waiting for transfers between devices, swap_core(): return lax.ppermute(value, AXES, swap_pairs(0, 1, 0, 0))  8.17 us
  transfers between devices with their start and end apart: 52, of which 24 were waited for; matrix products, arithmetic and copies ran while one was open for 7% of the time, Pallas kernels for 10%

profile of v4, /device:TPU:1, one launch (start us, length us, event | category | flops | bytes accessed | tf_op | source)
XLA Modules:
  0.0 197.5 jit_solution(17709824868508979308)
XLA Ops:
  1.7 2.2 %collective-permute-start = (bf16[96,768]{1,0:T(8,128)(2,1)S(1)}, bf16[96,768]{1,0:T(8,128)(2,1)S(1)}, u32[]{:S(2)}, u32[]{:S(2)}) collective-permute-start(bf16[96,768]{1,0:T(8,128)(2,1)S(1)} %dynamic-slice_select_fusion), channel_id=1, source_target_pairs={{0,2},{1,3},{2,0},{3,1},{4,6},{5,7},{6,4},{7,5},{8,10},{9,11},{10,... | collective-permute-start | bytes 442376 | tf_op jit(solution)/shard_map/ppermute | solution.py:152
  3.9 2.3 %collective-permute-start.1 = (bf16[96,768]{1,0:T(8,128)(2,1)S(1)}, bf16[96,768]{1,0:T(8,128)(2,1)S(1)}, u32[]{:S(2)}, u32[]{:S(2)}) collective-permute-start(bf16[96,768]{1,0:T(8,128)(2,1)S(1)} %dynamic-slice_select_fusion), channel_id=1, source_target_pairs={{0,4},{1,5},{2,6},{3,7},{4,0},{5,1},{6,2},{7,3},{8,12},{9,13},{10,... | collective-permute-start | bytes 442376 | tf_op jit(solution)/shard_map/ppermute | solution.py:152
  6.2 5.4 %concatenate.22 = bf16[1152]{0:T(1024)(128)(2,1)S(1)} concatenate(bf16[192]{0:T(256)(128)(2,1)} %param.18, bf16[96]{0:T(256)(128)(2,1)} %param.20, bf16[96]{0:T(256)(128)(2,1)} %param.21, bf16[96]{0:T(256)(128)(2,1)} %param.22, bf16[384]{0:T(512)(128)(2,1)} %param.24, bf16[96]{0:T(256)(128)(2,1)} %param.26, bf16[96]{0:T(256)(128)(2,1)} %param.27, bf16[96]{0:T(256)(128)(2,1)} %param.28), dimensions={0} | concatenate | bytes 4608 | tf_op jit(solution)/shard_map/concatenate | solution.py:735
  12.9 2.3 %reshape.70 = bf16[96,8,4,96]{3,2,1,0:T(4,128)(2,1)S(1)} reshape(bf16[96,3072]{1,0:T(8,128)(2,1)} %param.23) | data formatting | bytes 1179648 | tf_op jit(solution)/shard_map/reshape | solution.py:731
  17.2 2.1 %collective-permute-done.8 = bf16[2,1152]{1,0:T(2,128)(2,1)S(1)} collective-permute-done((bf16[2,1152]{1,0:T(2,128)(2,1)S(1)}, bf16[2,1152]{1,0:T(2,128)(2,1)S(1)}, u32[]{:S(2)}, u32[]{:S(2)}) %collective-permute-start.8) | collective-permute-done | bytes 4640 | tf_op jit(solution)/shard_map/ppermute | solution.py:152
  21.3 2.4 %collective-permute-start.9 = (bf16[4,1152]{1,0:T(4,128)(2,1)S(1)}, bf16[4,1152]{1,0:T(4,128)(2,1)S(1)}, u32[]{:S(2)}, u32[]{:S(2)}) collective-permute-start(bf16[4,1152]{1,0:T(4,128)(2,1)S(1)} %pad_maximum_fusion.11), channel_id=1, source_target_pairs={{0,4},{1,5},{2,6},{3,7},{4,0},{5,1},{6,2},{7,3},{8,12},{9,13},{10,... | collective-permute-start | bytes 27656 | tf_op jit(solution)/shard_map/ppermute | solution.py:152
  28.7 2.6 %collective-permute-done.16 = bf16[192,768]{1,0:T(8,128)(2,1)S(1)} collective-permute-done((bf16[192,768]{1,0:T(8,128)(2,1)S(1)}, bf16[192,768]{1,0:T(8,128)(2,1)S(1)}, u32[]{:S(2)}, u32[]{:S(2)}) %collective-permute-start.16) | collective-permute-done | bytes 294944 | tf_op jit(solution)/shard_map/ppermute | solution.py:152
  31.3 20.2 %collective-permute-done.15 = bf16[192,768]{1,0:T(8,128)(2,1)S(1)} collective-permute-done((bf16[192,768]{1,0:T(8,128)(2,1)S(1)}, bf16[192,768]{1,0:T(8,128)(2,1)S(1)}, u32[]{:S(2)}, u32[]{:S(2)}) %collective-permute-start.15) | collective-permute-done | bytes 294944 | tf_op jit(solution)/shard_map/ppermute | solution.py:152
  59.1 5.4 %attend.1 = (bf16[768,3072]{1,0:T(8,128)(2,1)S(1)}, bf16[768,768]{1,0:T(8,128)(2,1)S(1)}, bf16[128,2304]{1,0:T(8,128)(2,1)S(1)}, f32[12,128,128]{2,1,0:T(8,128)S...) custom-call(s32[2]{0:T(128)S(1)} %pad_add_fusion.refs_0_, ...), custom_call_target="tpu_custom_call" | custom-call | flops 1048576 | bytes 1048576 | tf_op jit(solution)/shard_map/attend/pallas_call | solution.py:252
  64.5 2.2 %copy-done.1 = bf16[768,3072]{1,0:T(8,128)(2,1)} copy-done((bf16[768,3072]{1,0:T(8,128)(2,1)}, bf16[768,3072]{1,0:T(8,128)(2,1)S(1)}, u32[]{:S(2)}) %copy-start.1) | copy-done | bytes 4718616
  67.6 5.3 %collective-permute-done.18.refs_3_.refs_5_ = bf16[128,768]{1,0:T(8,128)(2,1)S(1)} collective-permute-done((bf16[128,768]{1,0:T(8,128)(2,1)S(1)}, bf16[128,768]{1,0:T(8,128)(2,1)S(1)}, u32[]{:S(2)}, u32[]{:S(2)}) %collective-permute-start.18) | collective-permute-done | bytes 196640 | tf_op jit(solution)/shard_map/ppermute | solution.py:140
  74.1 3.5 %collective-permute-done.20.refs_7_ = bf16[4,192,768]{2,1,0:T(8,128)(2,1)S(1)} collective-permute-done((bf16[4,192,768]{2,1,0:T(8,128)(2,1)S(1)}, bf16[4,192,768]{2,1,0:T(8,128)(2,1)S(1)}, u32[]{:S(2)}, u32[]{:S(2)}) %collective-permute-start.20) | collective-permute-done | bytes 1179680 | tf_op jit(solution)/shard_map/ppermute | solution.py:148
  77.6 2.6 %feed.1 = (bf16[768,768]{1,0:T(8,128)(2,1)S(1)}, bf16[768,768]{1,0:T(8,128)(2,1)S(1)}, bf16[512,768]{1,0:T(8,128)(2,1)S(1)}, f32[512,768]{1,0:T(8,128)S(1)}, bf1...) custom-call(s32[2]{0:T(128)S(1)} %pad_add_fusion.refs_0_, ...), custom_call_target="tpu_custom_call" | custom-call | flops 1048576 | bytes 1048576 | tf_op jit(solution)/shard_map/feed/pallas_call | solution.py:252
  80.3 2.6 %collective-permute-start.21 = (bf16[2,128,768]{2,1,0:T(8,128)(2,1)S(1)}, bf16[2,128,768]{2,1,0:T(8,128)(2,1)S(1)}, u32[]{:S(2)}, u32[]{:S(2)}) collective-permute-start(bf16[2,128,768]{2,1,0:T(8,128)(2,1)S(1)} %get-tuple-element.92), channel_id=1, source_target_pairs={{0,8},{1,9},{2,10},{3,11},{4,12},{5,13},{6,14},{7,15},{8,0},{9,1},... | collective-permute-start | bytes 1179656 | tf_op jit(solution)/shard_map/ppermute | solution.py:144
  84.7 5.9 %collective-permute-done.22.refs_2_ = bf16[128,768]{1,0:T(8,128)(2,1)S(1)} collective-permute-done((bf16[128,768]{1,0:T(8,128)(2,1)S(1)}, bf16[128,768]{1,0:T(8,128)(2,1)S(1)}, u32[]{:S(2)}, u32[]{:S(2)}) %collective-permute-start.22) | collective-permute-done | bytes 196640 | tf_op jit(solution)/shard_map/ppermute | solution.py:140
  94.0 3.5 %collective-permute-done.24.refs_3_.refs_9_ = bf16[128,768]{1,0:T(8,128)(2,1)S(1)} collective-permute-done((bf16[128,768]{1,0:T(8,128)(2,1)S(1)}, bf16[128,768]{1,0:T(8,128)(2,1)S(1)}, u32[]{:S(2)}, u32[]{:S(2)}) %collective-permute-start.24) | collective-permute-done | bytes 196640 | tf_op jit(solution)/shard_map/ppermute | solution.py:140
  97.5 2.1 %collective-permute-start.25 = (bf16[128,768]{1,0:T(8,128)(2,1)S(1)}, bf16[128,768]{1,0:T(8,128)(2,1)S(1)}, u32[]{:S(2)}, u32[]{:S(2)}) collective-permute-start(bf16[128,768]{1,0:T(8,128)(2,1)S(1)} %collective-permute-done.24.refs_3_.refs_9_), channel_id=1, source_target_pairs={{0,8},{1,9},{2,10},{3,11},{4,12},{5,13},{6,14},{7,15},{8,0},{9,1},... | collective-permute-start | bytes 589832 | tf_op jit(solution)/shard_map/ppermute | solution.py:144
  100.7 3.4 %back.1 = (bf16[512,768]{1,0:T(8,128)(2,1)S(1)}, bf16[2,128,768]{2,1,0:T(8,128)(2,1)S(1)}, bf16[2,128,768]{2,1,0:T(8,128)(2,1)S(1)}, f32[1,768]{1,0:T(1,128)S(1)}) custom-call(s32[2]{0:T(128)S(1)} %pad_add_fusion.refs_0_, bf16[128,768]{1,0:T(8,128)(2,1)S(1)} %get-tuple-element.96.refs_1_.refs_7_, ...), custom_call_target="tpu_custom_call" | custom-call | flops 1048576 | bytes 1048576 | tf_op jit(solution)/shard_map/back/pallas_call | solution.py:252
  106.9 3.3 %grad_feed.1 = (bf16[4,192,768]{2,1,0:T(8,128)(2,1)S(1)}, bf16[4,192,768]{2,1,0:T(8,128)(2,1)}) custom-call(s32[2]{0:T(128)S(1)} %pad_add_fusion.refs_0_, bf16[512,768]{1,0:T(8,128)(2,1)S(1)} %get-tuple-element.109.refs_1_, bf16[512,768]{1,0:T(8,128)(2,1)S(1)} %get-tuple-element.110.refs_2_, bf16[128,768]{1,0:T(8,128)(2,1)S(1)} %get-tuple-element.89.refs_1_.refs_3_, ...), custom_call_target="tpu_custom_call" | custom-call | flops 1048576 | bytes 1048576 | tf_op jit(solution)/shard_map/grad_feed/pallas_call | solution.py:252
  118.3 6.9 %attend_back.1 = (bf16[2,4,48,768]{3,2,1,0:T(8,128)(2,1)S(1)}, bf16[2,4,48,768]{3,2,1,0:T(8,128)(2,1)S(1)}, bf16[2,4,48,768]{3,2,1,0:T(8,128)(2,1)S(1)}, bf16[2,...) custom-call(s32[2]{0:T(128)S(1)} %pad_add_fusion.refs_0_, ...), custom_call_target="tpu_custom_call" | custom-call | flops 1048576 | bytes 1048576 | tf_op jit(solution)/shard_map/attend_back/pallas_call | solution.py:252
  127.2 2.8 %collective-permute-done.36 = f32[12,768]{1,0:T(8,128)S(1)} collective-permute-done((f32[12,768]{1,0:T(8,128)S(1)}, f32[12,768]{1,0:T(8,128)S(1)}, u32[]{:S(2)}, u32[]{:S(2)}) %collective-permute-start.36) | collective-permute-done | bytes 36896 | tf_op jit(solution)/shard_map/ppermute | solution.py:152
  131.9 5.5 %collective-permute-done.38 = bf16[4,192,768]{2,1,0:T(8,128)(2,1)} collective-permute-done((bf16[4,192,768]{2,1,0:T(8,128)(2,1)}, bf16[4,192,768]{2,1,0:T(8,128)(2,1)}, u32[]{:S(2)}, u32[]{:S(2)}) %collective-permute-start.38) | collective-permute-done | bytes 1179680 | tf_op jit(solution)/shard_map/ppermute | solution.py:148
  142.0 4.4 %collective-permute-done.30 = bf16[2,4,48,768]{3,2,1,0:T(8,128)(2,1)S(1)} collective-permute-done((bf16[2,4,48,768]{3,2,1,0:T(8,128)(2,1)S(1)}, bf16[2,4,48,768]{3,2,1,0:T(8,128)(2,1)S(1)}, u32[]{:S(2)}, u32[]{:S(2)}) %collective-permute-start.30) | collective-permute-done | bytes 589856 | tf_op jit(solution)/shard_map/ppermute | solution.py:140
  148.0 2.6 %collective-permute-done.34 = bf16[2,4,48,768]{3,2,1,0:T(8,128)(2,1)S(1)} collective-permute-done((bf16[2,4,48,768]{3,2,1,0:T(8,128)(2,1)S(1)}, bf16[2,4,48,768]{3,2,1,0:T(8,128)(2,1)S(1)}, u32[]{:S(2)}, u32[]{:S(2)}) %collective-permute-start.34) | collective-permute-done | bytes 589856 | tf_op jit(solution)/shard_map/ppermute | solution.py:148
  153.6 6.0 %collective-permute-done.41 = bf16[192,768]{1,0:T(8,128)(2,1)S(1)} collective-permute-done((bf16[192,768]{1,0:T(8,128)(2,1)S(1)}, bf16[192,768]{1,0:T(8,128)(2,1)S(1)}, u32[]{:S(2)}, u32[]{:S(2)}) %collective-permute-start.41) | collective-permute-done | bytes 294944 | tf_op jit(solution)/shard_map/ppermute | solution.py:152
  161.4 8.2 %collective-permute-start.42 = (bf16[96,768]{1,0:T(8,128)(2,1)S(1)}, bf16[96,768]{1,0:T(8,128)(2,1)S(1)}, u32[]{:S(2)}, u32[]{:S(2)}) collective-permute-start(bf16[96,768]{1,0:T(8,128)(2,1)S(1)} %get-tuple-element.148), channel_id=1, source_target_pairs={{0,2},{1,3},{2,0},{3,1},{4,6},{5,7},{6,4},{7,5},{8,10},{9,11},{10,... | collective-permute-start | bytes 442376 | tf_op jit(solution)/shard_map/ppermute | solution.py:152
  171.8 3.5 %collective-permute-start.46 = (f32[12,768]{1,0:T(8,128)S(1)}, f32[12,768]{1,0:T(8,128)S(1)}, u32[]{:S(2)}, u32[]{:S(2)}) collective-permute-start(f32[12,768]{1,0:T(8,128)S(1)} %add.111), channel_id=1, source_target_pairs={{0,8},{1,9},{2,10},{3,11},{4,12},{5,13},{6,14},{7,15},{8,0},{9,1},... | collective-permute-start | bytes 110600 | tf_op jit(solution)/shard_map/ppermute | solution.py:144
  176.3 3.1 %collective-permute-done.47 = f32[12,768]{1,0:T(8,128)S(1)} collective-permute-done((f32[12,768]{1,0:T(8,128)S(1)}, f32[12,768]{1,0:T(8,128)S(1)}, u32[]{:S(2)}, u32[]{:S(2)}) %collective-permute-start.47) | collective-permute-done | bytes 36896 | tf_op jit(solution)/shard_map/ppermute | solution.py:140
  179.5 2.5 %grad_tokens.1 = bf16[128,768]{1,0:T(8,128)(2,1)} custom-call(s32[2]{0:T(128)S(1)} %pad_add_fusion.refs_0_, f32[128,768]{1,0:T(8,128)S(1)} %get-tuple-element.130.refs_1_, bf16[128,2304]{1,0:T(8,128)(2,1)S(1)} %get-tuple-element.131.refs_2_, bf16[768,3072]{1,0:T(8,128)(2,1)S(1)} %bitcast.89), custom_call_target="tpu_custom_call" | custom-call | flops 1048576 | bytes 1048576 | tf_op jit(solution)/shard_map/grad_tokens/pallas_call | solution.py:252
  182.8 2.2 %collective-permute-start.51 = (bf16[2,192,768]{2,1,0:T(8,128)(2,1)S(1)}, bf16[2,192,768]{2,1,0:T(8,128)(2,1)S(1)}, u32[]{:S(2)}, u32[]{:S(2)}) collective-permute-start(bf16[2,192,768]{2,1,0:T(8,128)(2,1)S(1)} %pad_maximum_fusion.3), channel_id=1, source_target_pairs={{0,8},{1,9},{2,10},{3,11},{4,12},{5,13},{6,14},{7,15},{8,0},{9,1},... | collective-permute-start | bytes 1769480 | tf_op jit(solution)/shard_map/ppermute | solution.py:144
  185.3 5.3 %collective-permute-done.49.refs_2_ = bf16[96,768]{1,0:T(8,128)(2,1)S(1)} collective-permute-done((bf16[96,768]{1,0:T(8,128)(2,1)S(1)}, bf16[96,768]{1,0:T(8,128)(2,1)S(1)}, u32[]{:S(2)}, u32[]{:S(2)}) %collective-permute-start.49) | collective-permute-done | bytes 147488 | tf_op jit(solution)/shard_map/ppermute | solution.py:140
  195.2 2.4 %finish_feed.1 = (f32[96,3072]{1,0:T(8,128)}, f32[384,768]{1,0:T(8,128)}) custom-call(s32[2]{0:T(128)S(1)} %pad_add_fusion.refs_0_, bf16[192,768]{1,0:T(8,128)(2,1)S(1)} %fusion.2.refs_1_, bf16[192,768]{1,0:T(8,128)(2,1)S(1)} %collective-permute-done.45.refs_2_, bf16[2,192,768]{2,1,0:T(8,128)(2,1)S(1)} %collective-permute-done.51.refs_3_), custom_call_target="tpu_custom_call" | custom-call | flops 1048576 | bytes 1048576 | tf_op jit(solution)/shard_map/finish_feed/pallas_call | solution.py:252
  (173 shorter events, 61.7 us)
Async XLA Ops:
  1.7 17.6 %collective-permute-start = (bf16[96,768]{1,0:T(8,128)(2,1)S(1)}, bf16[96,768]{1,0:T(8,128)(2,1)S(1)}, u32[]{:S(2)}, u32[]{:S(2)}) collective-permute-start(bf16[96,768]{1,0:T(8,128)(2,1)S(1)} %dynamic-slice_select_fusion), channel_id=1, source_target_pairs={{0,2},{1,3},{2,0},{3,1},{4,6},{5,7},{6,4},{7,5},{8,10},{9,11},{10,... | collective-permute-start | bytes 442376 | tf_op jit(solution)/shard_map/ppermute | solution.py:152
  3.9 15.5 %collective-permute-start.1 = (bf16[96,768]{1,0:T(8,128)(2,1)S(1)}, bf16[96,768]{1,0:T(8,128)(2,1)S(1)}, u32[]{:S(2)}, u32[]{:S(2)}) collective-permute-start(bf16[96,768]{1,0:T(8,128)(2,1)S(1)} %dynamic-slice_select_fusion), channel_id=1, source_target_pairs={{0,4},{1,5},{2,6},{3,7},{4,0},{5,1},{6,2},{7,3},{8,12},{9,13},{10,... | collective-permute-start | bytes 442376 | tf_op jit(solution)/shard_map/ppermute | solution.py:152
  6.2 13.2 %collective-permute-start.2 = (bf16[96,768]{1,0:T(8,128)(2,1)S(1)}, bf16[96,768]{1,0:T(8,128)(2,1)S(1)}, u32[]{:S(2)}, u32[]{:S(2)}) collective-permute-start(bf16[96,768]{1,0:T(8,128)(2,1)S(1)} %dynamic-slice_select_fusion), channel_id=1, source_target_pairs={{0,6},{1,7},{2,4},{3,5},{4,2},{5,3},{6,0},{7,1},{8,14},{9,15},{10,... | collective-permute-start | bytes 442376 | tf_op jit(solution)/shard_map/ppermute | solution.py:152
  19.5 6.5 %collective-permute-start.3 = (bf16[4,48,768]{2,1,0:T(8,128)(2,1)S(1)}, bf16[4,48,768]{2,1,0:T(8,128)(2,1)S(1)}, u32[]{:S(2)}, u32[]{:S(2)}) collective-permute-start(bf16[4,48,768]{2,1,0:T(8,128)(2,1)S(1)} %get-tuple-element.157), channel_id=1, source_target_pairs={{0,1},{1,0},{2,3},{3,2},{4,5},{5,4},{6,7},{7,6},{8,9},{9,8},{10,11... | collective-permute-start | bytes 884744 | tf_op jit(solution)/shard_map/ppermute | solution.py:148
  20.0 7.3 %collective-permute-start.5 = (bf16[4,48,768]{2,1,0:T(8,128)(2,1)S(1)}, bf16[4,48,768]{2,1,0:T(8,128)(2,1)S(1)}, u32[]{:S(2)}, u32[]{:S(2)}) collective-permute-start(bf16[4,48,768]{2,1,0:T(8,128)(2,1)S(1)} %get-tuple-element.155), channel_id=1, source_target_pairs={{0,16},{1,17},{2,18},{3,19},{4,20},{5,21},{6,22},{7,23},{8,24},{9,... | collective-permute-start | bytes 884744 | tf_op jit(solution)/shard_map/ppermute | solution.py:140
  21.3 6.3 %collective-permute-start.9 = (bf16[4,1152]{1,0:T(4,128)(2,1)S(1)}, bf16[4,1152]{1,0:T(4,128)(2,1)S(1)}, u32[]{:S(2)}, u32[]{:S(2)}) collective-permute-start(bf16[4,1152]{1,0:T(4,128)(2,1)S(1)} %pad_maximum_fusion.11), channel_id=1, source_target_pairs={{0,4},{1,5},{2,6},{3,7},{4,0},{5,1},{6,2},{7,3},{8,12},{9,13},{10,... | collective-permute-start | bytes 27656 | tf_op jit(solution)/shard_map/ppermute | solution.py:152
  23.6 7.6 %collective-permute-start.16 = (bf16[192,768]{1,0:T(8,128)(2,1)S(1)}, bf16[192,768]{1,0:T(8,128)(2,1)S(1)}, u32[]{:S(2)}, u32[]{:S(2)}) collective-permute-start(bf16[192,768]{1,0:T(8,128)(2,1)S(1)} %pad_maximum_fusion.4), channel_id=1, source_target_pairs={{0,6},{1,7},{2,4},{3,5},{4,2},{5,3},{6,0},{7,1},{8,14},{9,15},{10,... | collective-permute-start | bytes 884744 | tf_op jit(solution)/shard_map/ppermute | solution.py:152
  24.6 26.9 %collective-permute-start.15 = (bf16[192,768]{1,0:T(8,128)(2,1)S(1)}, bf16[192,768]{1,0:T(8,128)(2,1)S(1)}, u32[]{:S(2)}, u32[]{:S(2)}) collective-permute-start(bf16[192,768]{1,0:T(8,128)(2,1)S(1)} %pad_maximum_fusion.4), channel_id=1, source_target_pairs={{0,4},{1,5},{2,6},{3,7},{4,0},{5,1},{6,2},{7,3},{8,12},{9,13},{10,... | collective-permute-start | bytes 884744 | tf_op jit(solution)/shard_map/ppermute | solution.py:152
  26.0 25.5 %collective-permute-start.14 = (bf16[192,768]{1,0:T(8,128)(2,1)S(1)}, bf16[192,768]{1,0:T(8,128)(2,1)S(1)}, u32[]{:S(2)}, u32[]{:S(2)}) collective-permute-start(bf16[192,768]{1,0:T(8,128)(2,1)S(1)} %pad_maximum_fusion.4), channel_id=1, source_target_pairs={{0,2},{1,3},{2,0},{3,1},{4,6},{5,7},{6,4},{7,5},{8,10},{9,11},{10,... | collective-permute-start | bytes 884744 | tf_op jit(solution)/shard_map/ppermute | solution.py:152
  27.2 26.0 %collective-permute-start.4 = (bf16[2,4,48,768]{3,2,1,0:T(8,128)(2,1)S(1)}, bf16[2,4,48,768]{3,2,1,0:T(8,128)(2,1)S(1)}, u32[]{:S(2)}, u32[]{:S(2)}) collective-permute-start(bf16[2,4,48,768]{3,2,1,0:T(8,128)(2,1)S(1)} %pad_maximum_fusion.1.refs_4_), channel_id=1, source_target_pairs={{0,16},{1,17},{2,18},{3,19},{4,20},{5,21},{6,22},{7,23},{8,24},{9,... | collective-permute-start | bytes 1769480 | tf_op jit(solution)/shard_map/ppermute | solution.py:140
  27.6 25.6 %collective-permute-start.6 = (bf16[2,4,48,768]{3,2,1,0:T(8,128)(2,1)S(1)}, bf16[2,4,48,768]{3,2,1,0:T(8,128)(2,1)S(1)}, u32[]{:S(2)}, u32[]{:S(2)}) collective-permute-start(bf16[2,4,48,768]{3,2,1,0:T(8,128)(2,1)S(1)} %pad_maximum_fusion.2.refs_8_), channel_id=1, source_target_pairs={{0,1},{1,0},{2,3},{3,2},{4,5},{5,4},{6,7},{7,6},{8,9},{9,8},{10,11... | collective-permute-start | bytes 1769480 | tf_op jit(solution)/shard_map/ppermute | solution.py:148
  51.7 25.9 %collective-permute-start.20 = (bf16[4,192,768]{2,1,0:T(8,128)(2,1)S(1)}, bf16[4,192,768]{2,1,0:T(8,128)(2,1)S(1)}, u32[]{:S(2)}, u32[]{:S(2)}) collective-permute-start(bf16[4,192,768]{2,1,0:T(8,128)(2,1)S(1)} %pad_maximum_fusion.refs_12_.refs_6_), channel_id=1, source_target_pairs={{0,1},{1,0},{2,3},{3,2},{4,5},{5,4},{6,7},{7,6},{8,9},{9,8},{10,11... | collective-permute-start | bytes 3538952 | tf_op jit(solution)/shard_map/ppermute | solution.py:148
  67.0 10.6 %collective-permute-start.17 = (bf16[128,768]{1,0:T(8,128)(2,1)S(1)}, bf16[128,768]{1,0:T(8,128)(2,1)S(1)}, u32[]{:S(2)}, u32[]{:S(2)}) collective-permute-start(bf16[128,768]{1,0:T(8,128)(2,1)S(1)} %get-tuple-element.89.refs_1_.refs_3_), channel_id=1, source_target_pairs={{0,8},{1,9},{2,10},{3,11},{4,12},{5,13},{6,14},{7,15},{8,0},{9,1},... | collective-permute-start | bytes 589832 | tf_op jit(solution)/shard_map/ppermute | solution.py:144
  84.4 6.2 %collective-permute-start.22 = (bf16[128,768]{1,0:T(8,128)(2,1)S(1)}, bf16[128,768]{1,0:T(8,128)(2,1)S(1)}, u32[]{:S(2)}, u32[]{:S(2)}) collective-permute-start(bf16[128,768]{1,0:T(8,128)(2,1)S(1)} %get-tuple-element.152), channel_id=1, source_target_pairs={{0,16},{1,17},{2,18},{3,19},{4,20},{5,21},{6,22},{7,23},{8,24},{9,... | collective-permute-start | bytes 589832 | tf_op jit(solution)/shard_map/ppermute | solution.py:140
  92.5 7.1 %collective-permute-start.23 = (bf16[128,768]{1,0:T(8,128)(2,1)S(1)}, bf16[128,768]{1,0:T(8,128)(2,1)S(1)}, u32[]{:S(2)}, u32[]{:S(2)}) collective-permute-start(bf16[128,768]{1,0:T(8,128)(2,1)S(1)} %get-tuple-element.96.refs_1_.refs_7_), channel_id=1, source_target_pairs={{0,8},{1,9},{2,10},{3,11},{4,12},{5,13},{6,14},{7,15},{8,0},{9,1},... | collective-permute-start | bytes 589832 | tf_op jit(solution)/shard_map/ppermute | solution.py:144
  106.7 6.4 %collective-permute-start.27 = (bf16[128,768]{1,0:T(8,128)(2,1)}, bf16[128,768]{1,0:T(8,128)(2,1)}, u32[]{:S(2)}, u32[]{:S(2)}) collective-permute-start(bf16[128,768]{1,0:T(8,128)(2,1)} %get-tuple-element.150), channel_id=1, source_target_pairs={{0,16},{1,17},{2,18},{3,19},{4,20},{5,21},{6,22},{7,23},{8,24},{9,... | collective-permute-start | bytes 589832 | tf_op jit(solution)/shard_map/ppermute | solution.py:140
  110.2 27.2 %collective-permute-start.38 = (bf16[4,192,768]{2,1,0:T(8,128)(2,1)}, bf16[4,192,768]{2,1,0:T(8,128)(2,1)}, u32[]{:S(2)}, u32[]{:S(2)}) collective-permute-start(bf16[4,192,768]{2,1,0:T(8,128)(2,1)} %get-tuple-element.111.refs_12_), channel_id=1, source_target_pairs={{0,1},{1,0},{2,3},{3,2},{4,5},{5,4},{6,7},{7,6},{8,9},{9,8},{10,11... | collective-permute-start | bytes 3538952 | tf_op jit(solution)/shard_map/ppermute | solution.py:148
  126.6 13.9 %collective-permute-start.28 = (bf16[2,4,48,768]{3,2,1,0:T(8,128)(2,1)S(1)}, bf16[2,4,48,768]{3,2,1,0:T(8,128)(2,1)S(1)}, u32[]{:S(2)}, u32[]{:S(2)}) collective-permute-start(bf16[2,4,48,768]{3,2,1,0:T(8,128)(2,1)S(1)} %get-tuple-element.113), channel_id=1, source_target_pairs={{0,8},{1,9},{2,10},{3,11},{4,12},{5,13},{6,14},{7,15},{8,0},{9,1},... | collective-permute-start | bytes 1769480 | tf_op jit(solution)/shard_map/ppermute | solution.py:144
  129.9 10.8 %collective-permute-start.32 = (bf16[2,4,48,768]{3,2,1,0:T(8,128)(2,1)S(1)}, bf16[2,4,48,768]{3,2,1,0:T(8,128)(2,1)S(1)}, u32[]{:S(2)}, u32[]{:S(2)}) collective-permute-start(bf16[2,4,48,768]{3,2,1,0:T(8,128)(2,1)S(1)} %get-tuple-element.117), channel_id=1, source_target_pairs={{0,8},{1,9},{2,10},{3,11},{4,12},{5,13},{6,14},{7,15},{8,0},{9,1},... | collective-permute-start | bytes 1769480 | tf_op jit(solution)/shard_map/ppermute | solution.py:144
  131.2 21.0 %collective-permute-start.37 = (f32[12,768]{1,0:T(8,128)S(1)}, f32[12,768]{1,0:T(8,128)S(1)}, u32[]{:S(2)}, u32[]{:S(2)}) collective-permute-start(f32[12,768]{1,0:T(8,128)S(1)} %fusion.20), channel_id=1, source_target_pairs={{0,4},{1,5},{2,6},{3,7},{4,0},{5,1},{6,2},{7,3},{8,12},{9,13},{10,... | collective-permute-start | bytes 110600 | tf_op jit(solution)/shard_map/ppermute | solution.py:152
  131.4 15.0 %collective-permute-start.30 = (bf16[2,4,48,768]{3,2,1,0:T(8,128)(2,1)S(1)}, bf16[2,4,48,768]{3,2,1,0:T(8,128)(2,1)S(1)}, u32[]{:S(2)}, u32[]{:S(2)}) collective-permute-start(bf16[2,4,48,768]{3,2,1,0:T(8,128)(2,1)S(1)} %add_convert_fusion.3), channel_id=1, source_target_pairs={{0,16},{1,17},{2,18},{3,19},{4,20},{5,21},{6,22},{7,23},{8,24},{9,... | collective-permute-start | bytes 1769480 | tf_op jit(solution)/shard_map/ppermute | solution.py:140
  137.4 13.3 %collective-permute-start.34 = (bf16[2,4,48,768]{3,2,1,0:T(8,128)(2,1)S(1)}, bf16[2,4,48,768]{3,2,1,0:T(8,128)(2,1)S(1)}, u32[]{:S(2)}, u32[]{:S(2)}) collective-permute-start(bf16[2,4,48,768]{3,2,1,0:T(8,128)(2,1)S(1)} %add_convert_fusion.1), channel_id=1, source_target_pairs={{0,1},{1,0},{2,3},{3,2},{4,5},{5,4},{6,7},{7,6},{8,9},{9,8},{10,11... | collective-permute-start | bytes 1769480 | tf_op jit(solution)/shard_map/ppermute | solution.py:148
  140.5 13.1 %collective-permute-start.39 = (bf16[192,768]{1,0:T(8,128)(2,1)S(1)}, bf16[192,768]{1,0:T(8,128)(2,1)S(1)}, u32[]{:S(2)}, u32[]{:S(2)}) collective-permute-start(bf16[192,768]{1,0:T(8,128)(2,1)S(1)} %get-tuple-element.146), channel_id=1, source_target_pairs={{0,2},{1,3},{2,0},{3,1},{4,6},{5,7},{6,4},{7,5},{8,10},{9,11},{10,... | collective-permute-start | bytes 884744 | tf_op jit(solution)/shard_map/ppermute | solution.py:152
  140.7 12.8 %collective-permute-start.40 = (bf16[192,768]{1,0:T(8,128)(2,1)S(1)}, bf16[192,768]{1,0:T(8,128)(2,1)S(1)}, u32[]{:S(2)}, u32[]{:S(2)}) collective-permute-start(bf16[192,768]{1,0:T(8,128)(2,1)S(1)} %get-tuple-element.145), channel_id=1, source_target_pairs={{0,4},{1,5},{2,6},{3,7},{4,0},{5,1},{6,2},{7,3},{8,12},{9,13},{10,... | collective-permute-start | bytes 884744 | tf_op jit(solution)/shard_map/ppermute | solution.py:152
  146.4 13.2 %collective-permute-start.41 = (bf16[192,768]{1,0:T(8,128)(2,1)S(1)}, bf16[192,768]{1,0:T(8,128)(2,1)S(1)}, u32[]{:S(2)}, u32[]{:S(2)}) collective-permute-start(bf16[192,768]{1,0:T(8,128)(2,1)S(1)} %get-tuple-element.144), channel_id=1, source_target_pairs={{0,6},{1,7},{2,4},{3,5},{4,2},{5,3},{6,0},{7,1},{8,14},{9,15},{10,... | collective-permute-start | bytes 884744 | tf_op jit(solution)/shard_map/ppermute | solution.py:152
  150.7 8.9 %collective-permute-start.31 = (bf16[4,48,768]{2,1,0:T(8,128)(2,1)S(1)}, bf16[4,48,768]{2,1,0:T(8,128)(2,1)S(1)}, u32[]{:S(2)}, u32[]{:S(2)}) collective-permute-start(bf16[4,48,768]{2,1,0:T(8,128)(2,1)S(1)} %fusion.6), channel_id=1, source_target_pairs={{0,1},{1,0},{2,3},{3,2},{4,5},{5,4},{6,7},{7,6},{8,9},{9,8},{10,11... | collective-permute-start | bytes 884744 | tf_op jit(solution)/shard_map/ppermute | solution.py:148
  152.2 7.4 %collective-permute-start.35 = (bf16[4,48,768]{2,1,0:T(8,128)(2,1)S(1)}, bf16[4,48,768]{2,1,0:T(8,128)(2,1)S(1)}, u32[]{:S(2)}, u32[]{:S(2)}) collective-permute-start(bf16[4,48,768]{2,1,0:T(8,128)(2,1)S(1)} %fusion.7), channel_id=1, source_target_pairs={{0,16},{1,17},{2,18},{3,19},{4,20},{5,21},{6,22},{7,23},{8,24},{9,... | collective-permute-start | bytes 884744 | tf_op jit(solution)/shard_map/ppermute | solution.py:140
  159.7 23.0 %collective-permute-start.45 = (bf16[192,768]{1,0:T(8,128)(2,1)S(1)}, bf16[192,768]{1,0:T(8,128)(2,1)S(1)}, u32[]{:S(2)}, u32[]{:S(2)}) collective-permute-start(bf16[192,768]{1,0:T(8,128)(2,1)S(1)} %fusion.2.refs_1_), channel_id=1, source_target_pairs={{0,16},{1,17},{2,18},{3,19},{4,20},{5,21},{6,22},{7,23},{8,24},{9,... | collective-permute-start | bytes 884744 | tf_op jit(solution)/shard_map/ppermute | solution.py:140
  161.4 21.4 %collective-permute-start.42 = (bf16[96,768]{1,0:T(8,128)(2,1)S(1)}, bf16[96,768]{1,0:T(8,128)(2,1)S(1)}, u32[]{:S(2)}, u32[]{:S(2)}) collective-permute-start(bf16[96,768]{1,0:T(8,128)(2,1)S(1)} %get-tuple-element.148), channel_id=1, source_target_pairs={{0,2},{1,3},{2,0},{3,1},{4,6},{5,7},{6,4},{7,5},{8,10},{9,11},{10,... | collective-permute-start | bytes 442376 | tf_op jit(solution)/shard_map/ppermute | solution.py:152
  169.6 13.1 %collective-permute-start.43 = (bf16[96,768]{1,0:T(8,128)(2,1)S(1)}, bf16[96,768]{1,0:T(8,128)(2,1)S(1)}, u32[]{:S(2)}, u32[]{:S(2)}) collective-permute-start(bf16[96,768]{1,0:T(8,128)(2,1)S(1)} %get-tuple-element.149), channel_id=1, source_target_pairs={{0,4},{1,5},{2,6},{3,7},{4,0},{5,1},{6,2},{7,3},{8,12},{9,13},{10,... | collective-permute-start | bytes 442376 | tf_op jit(solution)/shard_map/ppermute | solution.py:152
  170.3 12.5 %collective-permute-start.44 = (bf16[96,768]{1,0:T(8,128)(2,1)S(1)}, bf16[96,768]{1,0:T(8,128)(2,1)S(1)}, u32[]{:S(2)}, u32[]{:S(2)}) collective-permute-start(bf16[96,768]{1,0:T(8,128)(2,1)S(1)} %get-tuple-element.147), channel_id=1, source_target_pairs={{0,6},{1,7},{2,4},{3,5},{4,2},{5,3},{6,0},{7,1},{8,14},{9,15},{10,... | collective-permute-start | bytes 442376 | tf_op jit(solution)/shard_map/ppermute | solution.py:152
  182.8 12.4 %collective-permute-start.51 = (bf16[2,192,768]{2,1,0:T(8,128)(2,1)S(1)}, bf16[2,192,768]{2,1,0:T(8,128)(2,1)S(1)}, u32[]{:S(2)}, u32[]{:S(2)}) collective-permute-start(bf16[2,192,768]{2,1,0:T(8,128)(2,1)S(1)} %pad_maximum_fusion.3), channel_id=1, source_target_pairs={{0,8},{1,9},{2,10},{3,11},{4,12},{5,13},{6,14},{7,15},{8,0},{9,1},... | collective-permute-start | bytes 1769480 | tf_op jit(solution)/shard_map/ppermute | solution.py:144
  (37 other events, 270.8 us)

commit v5 on v4

--- a/solution.py
+++ b/solution.py
@@ -739,7 +739,7 @@
     half_attn = halves_of(z_attn)
     near_attn = near_of(half_attn, cross_first(half_attn))
     far_attn = cross_second(near_attn)
-    far_attn, near_attn, packed = together(far_attn, near_attn, packed)
+    far_attn, near_attn = together(far_attn, near_attn)
     core_attn = parts_of(near_attn, far_attn, swap_cores(near_attn), swap_cores(far_attn))
     near_feed = jnp.stack(z_feed)
     far_feed = swap_y(near_feed)
@@ -850,9 +850,10 @@
     )
     sums = sums + swap_z(sums, 1)
     sums = sums + swap_z(sums, 2)
-    come_attn = cross_second(far)
+    come_attn, across = together(cross_second(far), swap_core(sums))
     zs_feed = send_zs(last_feed)
     onward, stay_attn = sum_plane(near, come_attn)
+    sums = sums + across
     come_attn, sums, zs_feed, grad_first = together(
         cross_first(onward), sums, zs_feed, grad_first
     )
@@ -866,7 +867,6 @@
         (shaped(rows, 768),),
         [position, grad_first, grad_proj, w_attn],
     )
-    sums = sums + swap_core(sums)
     sums = sums + swap_x(sums)
     small_total = sums + swap_y(sums)
     zs_attn, far_feed, grad_tokens, small_total = together(
@@ -882,7 +882,9 @@
     )
     reduced_attn = sum_zs(last_attn, zs_attn)
     far_attn = swap_x(reduced_attn)
-    core_attn = swap_core(jnp.stack([reduced_attn, far_attn]))
+    core_attn, d_up, d_down = together(
+        swap_core(jnp.stack([reduced_attn, far_attn])), d_up, d_down
+    )
     d_qkv, d_out = kernel_call(
         finish_attend_kernel,
         "finish_attend",

time: 198 us -> 194 us (0.980)
  waiting for transfers between devices: 83.1 us -> 62 us
  starting transfers between devices: 59.1 us -> 73.7 us
    ppermute x16, waiting for transfers between devices: 33.7 us -> 19.5 us  [swap_z(): return lax.ppermute(value, AXES, swap_pairs(0, 0, distance, 0))]
    ppermute x16, starting transfers between devices: 24.1 us -> 37.9 us  [swap_z(): return lax.ppermute(value, AXES, swap_pairs(0, 0, distance, 0))]
    ppermute x8, waiting for transfers between devices: 12.3 us -> 0.77 us  [swap_y(): return lax.ppermute(value, AXES, swap_pairs(0, 0, 0, 1))]
    ppermute x11, waiting for transfers between devices: 28.9 us -> 33.6 us  [swap_x(): return lax.ppermute(value, AXES, swap_pairs(1, 0, 0, 0))]
    ppermute x17, starting transfers between devices: 20.4 us -> 24 us  [swap_core(): return lax.ppermute(value, AXES, swap_pairs(0, 1, 0, 0))]
    ppermute x8, starting transfers between devices: 8.7 us -> 5.38 us  [swap_y(): return lax.ppermute(value, AXES, swap_pairs(0, 0, 0, 1))]
    unnamed x34 -> x38, local copies, waits for them, and re-layouts: 7.34 us -> 8.35 us
  transfers between devices with their start and end apart: 52 -> 52, of which waited for: 24 -> 21; matrix products, arithmetic and copies ran while one was open for 7% -> 7% of each run, Pallas kernels for 10% -> 11%
where the time goes in v5:
time: 194 us; the launch traced here: 193 us
  starting transfers between devices  73.7 us (38%)
  waiting for transfers between devices  62 us (32%)
  Pallas kernels  31.4 us (16%)
  local copies, waits for them, and re-layouts  20.4 us (11%)
  other arithmetic  4.84 us (2%)
    ppermute x16, starting transfers between devices, swap_z(): return lax.ppermute(value, AXES, swap_pairs(0, 0, distance, 0))  37.9 us
    ppermute x11, waiting for transfers between devices, swap_x(): return lax.ppermute(value, AXES, swap_pairs(1, 0, 0, 0))  33.6 us
    pallas_call x9, Pallas kernels, kernel_call(): pl.pallas_call(body, out_shape=tuple(out_shapes), in_specs=[SMEM] * scala...  31.4 us
    ppermute x17, starting transfers between devices, swap_core(): return lax.ppermute(value, AXES, swap_pairs(0, 1, 0, 0))  24 us
    ppermute x16, waiting for transfers between devices, swap_z(): return lax.ppermute(value, AXES, swap_pairs(0, 0, distance, 0))  19.5 us
    unnamed x38, local copies, waits for them, and re-layouts  8.35 us
    ppermute x17, waiting for transfers between devices, swap_core(): return lax.ppermute(value, AXES, swap_pairs(0, 1, 0, 0))  8.06 us
    ppermute x11, starting transfers between devices, swap_x(): return lax.ppermute(value, AXES, swap_pairs(1, 0, 0, 0))  6.41 us
  transfers between devices with their start and end apart: 52, of which 21 were waited for; matrix products, arithmetic and copies ran while one was open for 7% of the time, Pallas kernels for 11%

profile of v5, /device:TPU:1, one launch (start us, length us, event | category | flops | bytes accessed | tf_op | source)
XLA Modules:
  0.0 193.5 jit_solution(15872598246968758324)
XLA Ops:
  1.7 2.2 %collective-permute-start.3 = (bf16[96,768]{1,0:T(8,128)(2,1)S(1)}, bf16[96,768]{1,0:T(8,128)(2,1)S(1)}, u32[]{:S(2)}, u32[]{:S(2)}) collective-permute-start(bf16[96,768]{1,0:T(8,128)(2,1)S(1)} %dynamic-slice_select_fusion), channel_id=1, source_target_pairs={{0,2},{1,3},{2,0},{3,1},{4,6},{5,7},{6,4},{7,5},{8,10},{9,11},{10,... | collective-permute-start | bytes 442376 | tf_op jit(solution)/shard_map/ppermute | solution.py:152
  3.9 2.3 %collective-permute-start.4 = (bf16[96,768]{1,0:T(8,128)(2,1)S(1)}, bf16[96,768]{1,0:T(8,128)(2,1)S(1)}, u32[]{:S(2)}, u32[]{:S(2)}) collective-permute-start(bf16[96,768]{1,0:T(8,128)(2,1)S(1)} %dynamic-slice_select_fusion), channel_id=1, source_target_pairs={{0,4},{1,5},{2,6},{3,7},{4,0},{5,1},{6,2},{7,3},{8,12},{9,13},{10,... | collective-permute-start | bytes 442376 | tf_op jit(solution)/shard_map/ppermute | solution.py:152
  6.2 5.4 %concatenate.21 = bf16[1152]{0:T(1024)(128)(2,1)S(1)} concatenate(bf16[192]{0:T(256)(128)(2,1)} %param.18, bf16[96]{0:T(256)(128)(2,1)} %param.20, bf16[96]{0:T(256)(128)(2,1)} %param.21, bf16[96]{0:T(256)(128)(2,1)} %param.22, bf16[384]{0:T(512)(128)(2,1)} %param.24, bf16[96]{0:T(256)(128)(2,1)} %param.26, bf16[96]{0:T(256)(128)(2,1)} %param.27, bf16[96]{0:T(256)(128)(2,1)} %param.28), dimensions={0} | concatenate | bytes 4608 | tf_op jit(solution)/shard_map/concatenate | solution.py:735
  12.9 2.3 %reshape.70 = bf16[96,8,4,96]{3,2,1,0:T(4,128)(2,1)S(1)} reshape(bf16[96,3072]{1,0:T(8,128)(2,1)} %param.23) | data formatting | bytes 1179648 | tf_op jit(solution)/shard_map/reshape | solution.py:731
  18.6 3.4 %collective-permute-start.1 = (bf16[2,1152]{1,0:T(2,128)(2,1)S(1)}, bf16[2,1152]{1,0:T(2,128)(2,1)S(1)}, u32[]{:S(2)}, u32[]{:S(2)}) collective-permute-start(bf16[2,1152]{1,0:T(2,128)(2,1)S(1)} %pad_maximum_fusion.12), channel_id=1, source_target_pairs={{0,2},{1,3},{2,0},{3,1},{4,6},{5,7},{6,4},{7,5},{8,10},{9,11},{10,... | collective-permute-start | bytes 13832 | tf_op jit(solution)/shard_map/ppermute | solution.py:152
  22.0 2.3 %collective-permute-start.16 = (bf16[192,768]{1,0:T(8,128)(2,1)S(1)}, bf16[192,768]{1,0:T(8,128)(2,1)S(1)}, u32[]{:S(2)}, u32[]{:S(2)}) collective-permute-start(bf16[192,768]{1,0:T(8,128)(2,1)S(1)} %pad_maximum_fusion.4), channel_id=1, source_target_pairs={{0,6},{1,7},{2,4},{3,5},{4,2},{5,3},{6,0},{7,1},{8,14},{9,15},{10,... | collective-permute-start | bytes 884744 | tf_op jit(solution)/shard_map/ppermute | solution.py:152
  29.9 12.1 %collective-permute-start.2 = (bf16[4,1152]{1,0:T(4,128)(2,1)S(1)}, bf16[4,1152]{1,0:T(4,128)(2,1)S(1)}, u32[]{:S(2)}, u32[]{:S(2)}) collective-permute-start(bf16[4,1152]{1,0:T(4,128)(2,1)S(1)} %pad_maximum_fusion.11), channel_id=1, source_target_pairs={{0,4},{1,5},{2,6},{3,7},{4,0},{5,1},{6,2},{7,3},{8,12},{9,13},{10,... | collective-permute-start | bytes 27656 | tf_op jit(solution)/shard_map/ppermute | solution.py:152
  42.0 5.7 %collective-permute-done.15 = bf16[192,768]{1,0:T(8,128)(2,1)S(1)} collective-permute-done((bf16[192,768]{1,0:T(8,128)(2,1)S(1)}, bf16[192,768]{1,0:T(8,128)(2,1)S(1)}, u32[]{:S(2)}, u32[]{:S(2)}) %collective-permute-start.15) | collective-permute-done | bytes 294944 | tf_op jit(solution)/shard_map/ppermute | solution.py:152
  48.3 3.0 %collective-permute-start.10 = (bf16[2,4,48,768]{3,2,1,0:T(8,128)(2,1)S(1)}, bf16[2,4,48,768]{3,2,1,0:T(8,128)(2,1)S(1)}, u32[]{:S(2)}, u32[]{:S(2)}) collective-permute-start(bf16[2,4,48,768]{3,2,1,0:T(8,128)(2,1)S(1)} %pad_maximum_fusion.1.refs_4_), channel_id=1, source_target_pairs={{0,8},{1,9},{2,10},{3,11},{4,12},{5,13},{6,14},{7,15},{8,0},{9,1},... | collective-permute-start | bytes 1769480 | tf_op jit(solution)/shard_map/ppermute | solution.py:144
  55.6 6.1 %attend.1 = (bf16[768,3072]{1,0:T(8,128)(2,1)S(1)}, bf16[768,768]{1,0:T(8,128)(2,1)S(1)}, bf16[128,2304]{1,0:T(8,128)(2,1)S(1)}, f32[12,128,128]{2,1,0:T(8,128)S...) custom-call(s32[2]{0:T(128)S(1)} %pad_add_fusion.refs_0_, ...), custom_call_target="tpu_custom_call" | custom-call | flops 1048576 | bytes 1048576 | tf_op jit(solution)/shard_map/attend/pallas_call | solution.py:252
  61.8 2.2 %copy-done.1 = bf16[768,3072]{1,0:T(8,128)(2,1)} copy-done((bf16[768,3072]{1,0:T(8,128)(2,1)}, bf16[768,3072]{1,0:T(8,128)(2,1)S(1)}, u32[]{:S(2)}) %copy-start.1) | copy-done | bytes 4718616
  65.8 5.4 %collective-permute-done.18.refs_3_.refs_5_ = bf16[128,768]{1,0:T(8,128)(2,1)S(1)} collective-permute-done((bf16[128,768]{1,0:T(8,128)(2,1)S(1)}, bf16[128,768]{1,0:T(8,128)(2,1)S(1)}, u32[]{:S(2)}, u32[]{:S(2)}) %collective-permute-start.18) | collective-permute-done | bytes 196640 | tf_op jit(solution)/shard_map/ppermute | solution.py:140
  73.4 3.4 %feed.1 = (bf16[768,768]{1,0:T(8,128)(2,1)S(1)}, bf16[768,768]{1,0:T(8,128)(2,1)S(1)}, bf16[512,768]{1,0:T(8,128)(2,1)S(1)}, f32[512,768]{1,0:T(8,128)S(1)}, bf1...) custom-call(s32[2]{0:T(128)S(1)} %pad_add_fusion.refs_0_, ...), custom_call_target="tpu_custom_call" | custom-call | flops 1048576 | bytes 1048576 | tf_op jit(solution)/shard_map/feed/pallas_call | solution.py:252
  76.8 3.1 %collective-permute-start.21 = (bf16[2,128,768]{2,1,0:T(8,128)(2,1)S(1)}, bf16[2,128,768]{2,1,0:T(8,128)(2,1)S(1)}, u32[]{:S(2)}, u32[]{:S(2)}) collective-permute-start(bf16[2,128,768]{2,1,0:T(8,128)(2,1)S(1)} %get-tuple-element.96), channel_id=1, source_target_pairs={{0,8},{1,9},{2,10},{3,11},{4,12},{5,13},{6,14},{7,15},{8,0},{9,1},... | collective-permute-start | bytes 1179656 | tf_op jit(solution)/shard_map/ppermute | solution.py:144
  81.7 6.0 %collective-permute-done.22.refs_2_ = bf16[128,768]{1,0:T(8,128)(2,1)S(1)} collective-permute-done((bf16[128,768]{1,0:T(8,128)(2,1)S(1)}, bf16[128,768]{1,0:T(8,128)(2,1)S(1)}, u32[]{:S(2)}, u32[]{:S(2)}) %collective-permute-start.22) | collective-permute-done | bytes 196640 | tf_op jit(solution)/shard_map/ppermute | solution.py:140
  91.0 3.6 %collective-permute-done.24.refs_3_.refs_9_ = bf16[128,768]{1,0:T(8,128)(2,1)S(1)} collective-permute-done((bf16[128,768]{1,0:T(8,128)(2,1)S(1)}, bf16[128,768]{1,0:T(8,128)(2,1)S(1)}, u32[]{:S(2)}, u32[]{:S(2)}) %collective-permute-start.24) | collective-permute-done | bytes 196640 | tf_op jit(solution)/shard_map/ppermute | solution.py:140
  94.6 2.1 %collective-permute-start.25 = (bf16[128,768]{1,0:T(8,128)(2,1)S(1)}, bf16[128,768]{1,0:T(8,128)(2,1)S(1)}, u32[]{:S(2)}, u32[]{:S(2)}) collective-permute-start(bf16[128,768]{1,0:T(8,128)(2,1)S(1)} %collective-permute-done.24.refs_3_.refs_9_), channel_id=1, source_target_pairs={{0,8},{1,9},{2,10},{3,11},{4,12},{5,13},{6,14},{7,15},{8,0},{9,1},... | collective-permute-start | bytes 589832 | tf_op jit(solution)/shard_map/ppermute | solution.py:144
  97.8 3.4 %back.1 = (bf16[512,768]{1,0:T(8,128)(2,1)S(1)}, bf16[2,128,768]{2,1,0:T(8,128)(2,1)S(1)}, bf16[2,128,768]{2,1,0:T(8,128)(2,1)S(1)}, f32[1,768]{1,0:T(1,128)S(1)}) custom-call(s32[2]{0:T(128)S(1)} %pad_add_fusion.refs_0_, bf16[128,768]{1,0:T(8,128)(2,1)S(1)} %get-tuple-element.100.refs_1_.refs_7_, ...), custom_call_target="tpu_custom_call" | custom-call | flops 1048576 | bytes 1048576 | tf_op jit(solution)/shard_map/back/pallas_call | solution.py:252
  103.9 3.3 %grad_feed.1 = (bf16[4,192,768]{2,1,0:T(8,128)(2,1)S(1)}, bf16[4,192,768]{2,1,0:T(8,128)(2,1)}) custom-call(s32[2]{0:T(128)S(1)} %pad_add_fusion.refs_0_, bf16[512,768]{1,0:T(8,128)(2,1)S(1)} %get-tuple-element.113.refs_1_, bf16[512,768]{1,0:T(8,128)(2,1)S(1)} %get-tuple-element.114.refs_2_, bf16[128,768]{1,0:T(8,128)(2,1)S(1)} %get-tuple-element.93.refs_1_.refs_3_, ...), custom_call_target="tpu_custom_call" | custom-call | flops 1048576 | bytes 1048576 | tf_op jit(solution)/shard_map/grad_feed/pallas_call | solution.py:252
  107.6 2.6 %collective-permute-done.27.refs_2_ = bf16[128,768]{1,0:T(8,128)(2,1)} collective-permute-done((bf16[128,768]{1,0:T(8,128)(2,1)}, bf16[128,768]{1,0:T(8,128)(2,1)}, u32[]{:S(2)}, u32[]{:S(2)}) %collective-permute-start.27) | collective-permute-done | bytes 196640 | tf_op jit(solution)/shard_map/ppermute | solution.py:140
  115.3 6.9 %attend_back.1 = (bf16[2,4,48,768]{3,2,1,0:T(8,128)(2,1)S(1)}, bf16[2,4,48,768]{3,2,1,0:T(8,128)(2,1)S(1)}, bf16[2,4,48,768]{3,2,1,0:T(8,128)(2,1)S(1)}, bf16[2,...) custom-call(s32[2]{0:T(128)S(1)} %pad_add_fusion.refs_0_, ...), custom_call_target="tpu_custom_call" | custom-call | flops 1048576 | bytes 1048576 | tf_op jit(solution)/shard_map/attend_back/pallas_call | solution.py:252
  123.7 3.3 %collective-permute-done.33 = f32[12,768]{1,0:T(8,128)S(1)} collective-permute-done((f32[12,768]{1,0:T(8,128)S(1)}, f32[12,768]{1,0:T(8,128)S(1)}, u32[]{:S(2)}, u32[]{:S(2)}) %collective-permute-start.33) | collective-permute-done | bytes 36896 | tf_op jit(solution)/shard_map/ppermute | solution.py:152
  131.4 2.1 %collective-permute-start.37 = (bf16[2,4,48,768]{3,2,1,0:T(8,128)(2,1)S(1)}, bf16[2,4,48,768]{3,2,1,0:T(8,128)(2,1)S(1)}, u32[]{:S(2)}, u32[]{:S(2)}) collective-permute-start(bf16[2,4,48,768]{3,2,1,0:T(8,128)(2,1)S(1)} %get-tuple-element.127), channel_id=1, source_target_pairs={{0,8},{1,9},{2,10},{3,11},{4,12},{5,13},{6,14},{7,15},{8,0},{9,1},... | collective-permute-start | bytes 1769480 | tf_op jit(solution)/shard_map/ppermute | solution.py:144
  136.7 2.7 %collective-permute-start.41 = (bf16[192,768]{1,0:T(8,128)(2,1)S(1)}, bf16[192,768]{1,0:T(8,128)(2,1)S(1)}, u32[]{:S(2)}, u32[]{:S(2)}) collective-permute-start(bf16[192,768]{1,0:T(8,128)(2,1)S(1)} %get-tuple-element.155), channel_id=1, source_target_pairs={{0,4},{1,5},{2,6},{3,7},{4,0},{5,1},{6,2},{7,3},{8,12},{9,13},{10,... | collective-permute-start | bytes 884744 | tf_op jit(solution)/shard_map/ppermute | solution.py:152
  140.5 7.8 %collective-permute-done.30 = bf16[2,4,48,768]{3,2,1,0:T(8,128)(2,1)S(1)} collective-permute-done((bf16[2,4,48,768]{3,2,1,0:T(8,128)(2,1)S(1)}, bf16[2,4,48,768]{3,2,1,0:T(8,128)(2,1)S(1)}, u32[]{:S(2)}, u32[]{:S(2)}) %collective-permute-start.30) | collective-permute-done | bytes 589856 | tf_op jit(solution)/shard_map/ppermute | solution.py:140
  149.6 7.5 %collective-permute-done.42 = bf16[192,768]{1,0:T(8,128)(2,1)S(1)} collective-permute-done((bf16[192,768]{1,0:T(8,128)(2,1)S(1)}, bf16[192,768]{1,0:T(8,128)(2,1)S(1)}, u32[]{:S(2)}, u32[]{:S(2)}) %collective-permute-start.42) | collective-permute-done | bytes 294944 | tf_op jit(solution)/shard_map/ppermute | solution.py:152
  158.8 6.9 %collective-permute-start.43 = (bf16[96,768]{1,0:T(8,128)(2,1)S(1)}, bf16[96,768]{1,0:T(8,128)(2,1)S(1)}, u32[]{:S(2)}, u32[]{:S(2)}) collective-permute-start(bf16[96,768]{1,0:T(8,128)(2,1)S(1)} %get-tuple-element.158), channel_id=1, source_target_pairs={{0,2},{1,3},{2,0},{3,1},{4,6},{5,7},{6,4},{7,5},{8,10},{9,11},{10,... | collective-permute-start | bytes 442376 | tf_op jit(solution)/shard_map/ppermute | solution.py:152
  168.1 3.0 %collective-permute-done.47 = f32[12,768]{1,0:T(8,128)S(1)} collective-permute-done((f32[12,768]{1,0:T(8,128)S(1)}, f32[12,768]{1,0:T(8,128)S(1)}, u32[]{:S(2)}, u32[]{:S(2)}) %collective-permute-start.47) | collective-permute-done | bytes 36896 | tf_op jit(solution)/shard_map/ppermute | solution.py:140
  172.4 2.5 %grad_tokens.1 = bf16[128,768]{1,0:T(8,128)(2,1)} custom-call(s32[2]{0:T(128)S(1)} %pad_add_fusion.refs_0_, f32[128,768]{1,0:T(8,128)S(1)} %get-tuple-element.137.refs_1_, bf16[128,2304]{1,0:T(8,128)(2,1)S(1)} %get-tuple-element.138.refs_2_, bf16[768,3072]{1,0:T(8,128)(2,1)S(1)} %bitcast.89), custom_call_target="tpu_custom_call" | custom-call | flops 1048576 | bytes 1048576 | tf_op jit(solution)/shard_map/grad_tokens/pallas_call | solution.py:252
  175.0 5.9 %collective-permute-start.51 = (bf16[2,192,768]{2,1,0:T(8,128)(2,1)S(1)}, bf16[2,192,768]{2,1,0:T(8,128)(2,1)S(1)}, u32[]{:S(2)}, u32[]{:S(2)}) collective-permute-start(bf16[2,192,768]{2,1,0:T(8,128)(2,1)S(1)} %pad_maximum_fusion.3), channel_id=1, source_target_pairs={{0,8},{1,9},{2,10},{3,11},{4,12},{5,13},{6,14},{7,15},{8,0},{9,1},... | collective-permute-start | bytes 1769480 | tf_op jit(solution)/shard_map/ppermute | solution.py:144
  181.3 5.2 %collective-permute-done.49.refs_2_ = bf16[96,768]{1,0:T(8,128)(2,1)S(1)} collective-permute-done((bf16[96,768]{1,0:T(8,128)(2,1)S(1)}, bf16[96,768]{1,0:T(8,128)(2,1)S(1)}, u32[]{:S(2)}, u32[]{:S(2)}) %collective-permute-start.49) | collective-permute-done | bytes 147488 | tf_op jit(solution)/shard_map/ppermute | solution.py:140
  189.5 2.4 %finish_feed.1 = (f32[96,3072]{1,0:T(8,128)}, f32[384,768]{1,0:T(8,128)}) custom-call(s32[2]{0:T(128)S(1)} %pad_add_fusion.refs_0_, bf16[192,768]{1,0:T(8,128)(2,1)S(1)} %fusion.2.refs_1_, bf16[192,768]{1,0:T(8,128)(2,1)S(1)} %collective-permute-done.46.refs_2_, bf16[2,192,768]{2,1,0:T(8,128)(2,1)S(1)} %collective-permute-done.51.refs_3_), custom_call_target="tpu_custom_call" | custom-call | flops 1048576 | bytes 1048576 | tf_op jit(solution)/shard_map/finish_feed/pallas_call | solution.py:252
  (177 shorter events, 56.2 us)
Async XLA Ops:
  1.7 15.1 %collective-permute-start.3 = (bf16[96,768]{1,0:T(8,128)(2,1)S(1)}, bf16[96,768]{1,0:T(8,128)(2,1)S(1)}, u32[]{:S(2)}, u32[]{:S(2)}) collective-permute-start(bf16[96,768]{1,0:T(8,128)(2,1)S(1)} %dynamic-slice_select_fusion), channel_id=1, source_target_pairs={{0,2},{1,3},{2,0},{3,1},{4,6},{5,7},{6,4},{7,5},{8,10},{9,11},{10,... | collective-permute-start | bytes 442376 | tf_op jit(solution)/shard_map/ppermute | solution.py:152
  3.9 12.9 %collective-permute-start.4 = (bf16[96,768]{1,0:T(8,128)(2,1)S(1)}, bf16[96,768]{1,0:T(8,128)(2,1)S(1)}, u32[]{:S(2)}, u32[]{:S(2)}) collective-permute-start(bf16[96,768]{1,0:T(8,128)(2,1)S(1)} %dynamic-slice_select_fusion), channel_id=1, source_target_pairs={{0,4},{1,5},{2,6},{3,7},{4,0},{5,1},{6,2},{7,3},{8,12},{9,13},{10,... | collective-permute-start | bytes 442376 | tf_op jit(solution)/shard_map/ppermute | solution.py:152
  6.2 10.6 %collective-permute-start.5 = (bf16[96,768]{1,0:T(8,128)(2,1)S(1)}, bf16[96,768]{1,0:T(8,128)(2,1)S(1)}, u32[]{:S(2)}, u32[]{:S(2)}) collective-permute-start(bf16[96,768]{1,0:T(8,128)(2,1)S(1)} %dynamic-slice_select_fusion), channel_id=1, source_target_pairs={{0,6},{1,7},{2,4},{3,5},{4,2},{5,3},{6,0},{7,1},{8,14},{9,15},{10,... | collective-permute-start | bytes 442376 | tf_op jit(solution)/shard_map/ppermute | solution.py:152
  16.9 7.4 %collective-permute-start.6 = (bf16[4,48,768]{2,1,0:T(8,128)(2,1)S(1)}, bf16[4,48,768]{2,1,0:T(8,128)(2,1)S(1)}, u32[]{:S(2)}, u32[]{:S(2)}) collective-permute-start(bf16[4,48,768]{2,1,0:T(8,128)(2,1)S(1)} %get-tuple-element.167), channel_id=1, source_target_pairs={{0,1},{1,0},{2,3},{3,2},{4,5},{5,4},{6,7},{7,6},{8,9},{9,8},{10,11... | collective-permute-start | bytes 884744 | tf_op jit(solution)/shard_map/ppermute | solution.py:148
  17.3 8.7 %collective-permute-start.8 = (bf16[4,48,768]{2,1,0:T(8,128)(2,1)S(1)}, bf16[4,48,768]{2,1,0:T(8,128)(2,1)S(1)}, u32[]{:S(2)}, u32[]{:S(2)}) collective-permute-start(bf16[4,48,768]{2,1,0:T(8,128)(2,1)S(1)} %get-tuple-element.165), channel_id=1, source_target_pairs={{0,16},{1,17},{2,18},{3,19},{4,20},{5,21},{6,22},{7,23},{8,24},{9,... | collective-permute-start | bytes 884744 | tf_op jit(solution)/shard_map/ppermute | solution.py:140
  18.6 8.9 %collective-permute-start.1 = (bf16[2,1152]{1,0:T(2,128)(2,1)S(1)}, bf16[2,1152]{1,0:T(2,128)(2,1)S(1)}, u32[]{:S(2)}, u32[]{:S(2)}) collective-permute-start(bf16[2,1152]{1,0:T(2,128)(2,1)S(1)} %pad_maximum_fusion.12), channel_id=1, source_target_pairs={{0,2},{1,3},{2,0},{3,1},{4,6},{5,7},{6,4},{7,5},{8,10},{9,11},{10,... | collective-permute-start | bytes 13832 | tf_op jit(solution)/shard_map/ppermute | solution.py:152
  22.0 7.9 %collective-permute-start.16 = (bf16[192,768]{1,0:T(8,128)(2,1)S(1)}, bf16[192,768]{1,0:T(8,128)(2,1)S(1)}, u32[]{:S(2)}, u32[]{:S(2)}) collective-permute-start(bf16[192,768]{1,0:T(8,128)(2,1)S(1)} %pad_maximum_fusion.4), channel_id=1, source_target_pairs={{0,6},{1,7},{2,4},{3,5},{4,2},{5,3},{6,0},{7,1},{8,14},{9,15},{10,... | collective-permute-start | bytes 884744 | tf_op jit(solution)/shard_map/ppermute | solution.py:152
  24.4 23.4 %collective-permute-start.15 = (bf16[192,768]{1,0:T(8,128)(2,1)S(1)}, bf16[192,768]{1,0:T(8,128)(2,1)S(1)}, u32[]{:S(2)}, u32[]{:S(2)}) collective-permute-start(bf16[192,768]{1,0:T(8,128)(2,1)S(1)} %pad_maximum_fusion.4), channel_id=1, source_target_pairs={{0,4},{1,5},{2,6},{3,7},{4,0},{5,1},{6,2},{7,3},{8,12},{9,13},{10,... | collective-permute-start | bytes 884744 | tf_op jit(solution)/shard_map/ppermute | solution.py:152
  24.4 23.4 %collective-permute-start.14 = (bf16[192,768]{1,0:T(8,128)(2,1)S(1)}, bf16[192,768]{1,0:T(8,128)(2,1)S(1)}, u32[]{:S(2)}, u32[]{:S(2)}) collective-permute-start(bf16[192,768]{1,0:T(8,128)(2,1)S(1)} %pad_maximum_fusion.4), channel_id=1, source_target_pairs={{0,2},{1,3},{2,0},{3,1},{4,6},{5,7},{6,4},{7,5},{8,10},{9,11},{10,... | collective-permute-start | bytes 884744 | tf_op jit(solution)/shard_map/ppermute | solution.py:152
  26.0 22.3 %collective-permute-start.7 = (bf16[2,4,48,768]{3,2,1,0:T(8,128)(2,1)S(1)}, bf16[2,4,48,768]{3,2,1,0:T(8,128)(2,1)}, u32[]{:S(2)}, u32[]{:S(2)}) collective-permute-start(bf16[2,4,48,768]{3,2,1,0:T(8,128)(2,1)S(1)} %pad_maximum_fusion.1.refs_4_), channel_id=1, source_target_pairs={{0,16},{1,17},{2,18},{3,19},{4,20},{5,21},{6,22},{7,23},{8,24},{9,... | collective-permute-start | bytes 1769480 | tf_op jit(solution)/shard_map/ppermute | solution.py:140
  27.5 20.7 %collective-permute-start.9 = (bf16[2,4,48,768]{3,2,1,0:T(8,128)(2,1)S(1)}, bf16[2,4,48,768]{3,2,1,0:T(8,128)(2,1)}, u32[]{:S(2)}, u32[]{:S(2)}) collective-permute-start(bf16[2,4,48,768]{3,2,1,0:T(8,128)(2,1)S(1)} %pad_maximum_fusion.2.refs_8_), channel_id=1, source_target_pairs={{0,1},{1,0},{2,3},{3,2},{4,5},{5,4},{6,7},{7,6},{8,9},{9,8},{10,11... | collective-permute-start | bytes 1769480 | tf_op jit(solution)/shard_map/ppermute | solution.py:148
  29.9 21.8 %collective-permute-start.2 = (bf16[4,1152]{1,0:T(4,128)(2,1)S(1)}, bf16[4,1152]{1,0:T(4,128)(2,1)S(1)}, u32[]{:S(2)}, u32[]{:S(2)}) collective-permute-start(bf16[4,1152]{1,0:T(4,128)(2,1)S(1)} %pad_maximum_fusion.11), channel_id=1, source_target_pairs={{0,4},{1,5},{2,6},{3,7},{4,0},{5,1},{6,2},{7,3},{8,12},{9,13},{10,... | collective-permute-start | bytes 27656 | tf_op jit(solution)/shard_map/ppermute | solution.py:152
  47.9 25.0 %collective-permute-start.20 = (bf16[4,192,768]{2,1,0:T(8,128)(2,1)S(1)}, bf16[4,192,768]{2,1,0:T(8,128)(2,1)}, u32[]{:S(2)}, u32[]{:S(2)}) collective-permute-start(bf16[4,192,768]{2,1,0:T(8,128)(2,1)S(1)} %pad_maximum_fusion.refs_12_.refs_6_), channel_id=1, source_target_pairs={{0,1},{1,0},{2,3},{3,2},{4,5},{5,4},{6,7},{7,6},{8,9},{9,8},{10,11... | collective-permute-start | bytes 3538952 | tf_op jit(solution)/shard_map/ppermute | solution.py:148
  65.2 7.7 %collective-permute-start.17 = (bf16[128,768]{1,0:T(8,128)(2,1)S(1)}, bf16[128,768]{1,0:T(8,128)(2,1)S(1)}, u32[]{:S(2)}, u32[]{:S(2)}) collective-permute-start(bf16[128,768]{1,0:T(8,128)(2,1)S(1)} %get-tuple-element.93.refs_1_.refs_3_), channel_id=1, source_target_pairs={{0,8},{1,9},{2,10},{3,11},{4,12},{5,13},{6,14},{7,15},{8,0},{9,1},... | collective-permute-start | bytes 589832 | tf_op jit(solution)/shard_map/ppermute | solution.py:144
  89.5 7.2 %collective-permute-start.23 = (bf16[128,768]{1,0:T(8,128)(2,1)S(1)}, bf16[128,768]{1,0:T(8,128)(2,1)S(1)}, u32[]{:S(2)}, u32[]{:S(2)}) collective-permute-start(bf16[128,768]{1,0:T(8,128)(2,1)S(1)} %get-tuple-element.100.refs_1_.refs_7_), channel_id=1, source_target_pairs={{0,8},{1,9},{2,10},{3,11},{4,12},{5,13},{6,14},{7,15},{8,0},{9,1},... | collective-permute-start | bytes 589832 | tf_op jit(solution)/shard_map/ppermute | solution.py:144
  103.8 6.4 %collective-permute-start.27 = (bf16[128,768]{1,0:T(8,128)(2,1)}, bf16[128,768]{1,0:T(8,128)(2,1)}, u32[]{:S(2)}, u32[]{:S(2)}) collective-permute-start(bf16[128,768]{1,0:T(8,128)(2,1)} %get-tuple-element.160), channel_id=1, source_target_pairs={{0,16},{1,17},{2,18},{3,19},{4,20},{5,21},{6,22},{7,23},{8,24},{9,... | collective-permute-start | bytes 589832 | tf_op jit(solution)/shard_map/ppermute | solution.py:140
  107.2 27.2 %collective-permute-start.39 = (bf16[4,192,768]{2,1,0:T(8,128)(2,1)}, bf16[4,192,768]{2,1,0:T(8,128)(2,1)}, u32[]{:S(2)}, u32[]{:S(2)}) collective-permute-start(bf16[4,192,768]{2,1,0:T(8,128)(2,1)} %get-tuple-element.115.refs_12_), channel_id=1, source_target_pairs={{0,1},{1,0},{2,3},{3,2},{4,5},{5,4},{6,7},{7,6},{8,9},{9,8},{10,11... | collective-permute-start | bytes 3538952 | tf_op jit(solution)/shard_map/ppermute | solution.py:148
  122.2 11.3 %collective-permute-start.29 = (bf16[2,4,48,768]{3,2,1,0:T(8,128)(2,1)S(1)}, bf16[2,4,48,768]{3,2,1,0:T(8,128)(2,1)S(1)}, u32[]{:S(2)}, u32[]{:S(2)}) collective-permute-start(bf16[2,4,48,768]{3,2,1,0:T(8,128)(2,1)S(1)} %get-tuple-element.119), channel_id=1, source_target_pairs={{0,8},{1,9},{2,10},{3,11},{4,12},{5,13},{6,14},{7,15},{8,0},{9,1},... | collective-permute-start | bytes 1769480 | tf_op jit(solution)/shard_map/ppermute | solution.py:144
  123.6 10.2 %collective-permute-start.31 = (bf16[2,4,48,768]{3,2,1,0:T(8,128)(2,1)S(1)}, bf16[2,4,48,768]{3,2,1,0:T(8,128)(2,1)S(1)}, u32[]{:S(2)}, u32[]{:S(2)}) collective-permute-start(bf16[2,4,48,768]{3,2,1,0:T(8,128)(2,1)S(1)} %get-tuple-element.121), channel_id=1, source_target_pairs={{0,8},{1,9},{2,10},{3,11},{4,12},{5,13},{6,14},{7,15},{8,0},{9,1},... | collective-permute-start | bytes 1769480 | tf_op jit(solution)/shard_map/ppermute | solution.py:144
  128.3 8.1 %collective-permute-start.28 = (bf16[2,4,48,768]{3,2,1,0:T(8,128)(2,1)S(1)}, bf16[2,4,48,768]{3,2,1,0:T(8,128)(2,1)S(1)}, u32[]{:S(2)}, u32[]{:S(2)}) collective-permute-start(bf16[2,4,48,768]{3,2,1,0:T(8,128)(2,1)S(1)} %get-tuple-element.117), channel_id=1, source_target_pairs={{0,8},{1,9},{2,10},{3,11},{4,12},{5,13},{6,14},{7,15},{8,0},{9,1},... | collective-permute-start | bytes 1769480 | tf_op jit(solution)/shard_map/ppermute | solution.py:144
  133.8 14.5 %collective-permute-start.30 = (bf16[2,4,48,768]{3,2,1,0:T(8,128)(2,1)S(1)}, bf16[2,4,48,768]{3,2,1,0:T(8,128)(2,1)S(1)}, u32[]{:S(2)}, u32[]{:S(2)}) collective-permute-start(bf16[2,4,48,768]{3,2,1,0:T(8,128)(2,1)S(1)} %add_convert_fusion.3), channel_id=1, source_target_pairs={{0,16},{1,17},{2,18},{3,19},{4,20},{5,21},{6,22},{7,23},{8,24},{9,... | collective-permute-start | bytes 1769480 | tf_op jit(solution)/shard_map/ppermute | solution.py:140
  134.4 13.9 %collective-permute-start.32 = (bf16[2,4,48,768]{3,2,1,0:T(8,128)(2,1)S(1)}, bf16[2,4,48,768]{3,2,1,0:T(8,128)(2,1)S(1)}, u32[]{:S(2)}, u32[]{:S(2)}) collective-permute-start(bf16[2,4,48,768]{3,2,1,0:T(8,128)(2,1)S(1)} %add_convert_fusion.2), channel_id=1, source_target_pairs={{0,1},{1,0},{2,3},{3,2},{4,5},{5,4},{6,7},{7,6},{8,9},{9,8},{10,11... | collective-permute-start | bytes 1769480 | tf_op jit(solution)/shard_map/ppermute | solution.py:148
  136.4 13.1 %collective-permute-start.40 = (bf16[192,768]{1,0:T(8,128)(2,1)S(1)}, bf16[192,768]{1,0:T(8,128)(2,1)S(1)}, u32[]{:S(2)}, u32[]{:S(2)}) collective-permute-start(bf16[192,768]{1,0:T(8,128)(2,1)S(1)} %get-tuple-element.156), channel_id=1, source_target_pairs={{0,2},{1,3},{2,0},{3,1},{4,6},{5,7},{6,4},{7,5},{8,10},{9,11},{10,... | collective-permute-start | bytes 884744 | tf_op jit(solution)/shard_map/ppermute | solution.py:152
  136.7 12.9 %collective-permute-start.41 = (bf16[192,768]{1,0:T(8,128)(2,1)S(1)}, bf16[192,768]{1,0:T(8,128)(2,1)S(1)}, u32[]{:S(2)}, u32[]{:S(2)}) collective-permute-start(bf16[192,768]{1,0:T(8,128)(2,1)S(1)} %get-tuple-element.155), channel_id=1, source_target_pairs={{0,4},{1,5},{2,6},{3,7},{4,0},{5,1},{6,2},{7,3},{8,12},{9,13},{10,... | collective-permute-start | bytes 884744 | tf_op jit(solution)/shard_map/ppermute | solution.py:152
  139.5 17.5 %collective-permute-start.42 = (bf16[192,768]{1,0:T(8,128)(2,1)S(1)}, bf16[192,768]{1,0:T(8,128)(2,1)S(1)}, u32[]{:S(2)}, u32[]{:S(2)}) collective-permute-start(bf16[192,768]{1,0:T(8,128)(2,1)S(1)} %get-tuple-element.154), channel_id=1, source_target_pairs={{0,6},{1,7},{2,4},{3,5},{4,2},{5,3},{6,0},{7,1},{8,14},{9,15},{10,... | collective-permute-start | bytes 884744 | tf_op jit(solution)/shard_map/ppermute | solution.py:152
  148.4 8.7 %collective-permute-start.36 = (bf16[4,48,768]{2,1,0:T(8,128)(2,1)S(1)}, bf16[4,48,768]{2,1,0:T(8,128)(2,1)S(1)}, u32[]{:S(2)}, u32[]{:S(2)}) collective-permute-start(bf16[4,48,768]{2,1,0:T(8,128)(2,1)S(1)} %fusion.6), channel_id=1, source_target_pairs={{0,1},{1,0},{2,3},{3,2},{4,5},{5,4},{6,7},{7,6},{8,9},{9,8},{10,11... | collective-permute-start | bytes 884744 | tf_op jit(solution)/shard_map/ppermute | solution.py:148
  148.7 8.3 %collective-permute-start.38 = (bf16[4,48,768]{2,1,0:T(8,128)(2,1)S(1)}, bf16[4,48,768]{2,1,0:T(8,128)(2,1)S(1)}, u32[]{:S(2)}, u32[]{:S(2)}) collective-permute-start(bf16[4,48,768]{2,1,0:T(8,128)(2,1)S(1)} %fusion.7), channel_id=1, source_target_pairs={{0,16},{1,17},{2,18},{3,19},{4,20},{5,21},{6,22},{7,23},{8,24},{9,... | collective-permute-start | bytes 884744 | tf_op jit(solution)/shard_map/ppermute | solution.py:140
  157.3 17.6 %collective-permute-start.46 = (bf16[192,768]{1,0:T(8,128)(2,1)S(1)}, bf16[192,768]{1,0:T(8,128)(2,1)S(1)}, u32[]{:S(2)}, u32[]{:S(2)}) collective-permute-start(bf16[192,768]{1,0:T(8,128)(2,1)S(1)} %fusion.2.refs_1_), channel_id=1, source_target_pairs={{0,16},{1,17},{2,18},{3,19},{4,20},{5,21},{6,22},{7,23},{8,24},{9,... | collective-permute-start | bytes 884744 | tf_op jit(solution)/shard_map/ppermute | solution.py:140
  158.8 16.1 %collective-permute-start.43 = (bf16[96,768]{1,0:T(8,128)(2,1)S(1)}, bf16[96,768]{1,0:T(8,128)(2,1)S(1)}, u32[]{:S(2)}, u32[]{:S(2)}) collective-permute-start(bf16[96,768]{1,0:T(8,128)(2,1)S(1)} %get-tuple-element.158), channel_id=1, source_target_pairs={{0,2},{1,3},{2,0},{3,1},{4,6},{5,7},{6,4},{7,5},{8,10},{9,11},{10,... | collective-permute-start | bytes 442376 | tf_op jit(solution)/shard_map/ppermute | solution.py:152
  165.7 9.2 %collective-permute-start.44 = (bf16[96,768]{1,0:T(8,128)(2,1)S(1)}, bf16[96,768]{1,0:T(8,128)(2,1)S(1)}, u32[]{:S(2)}, u32[]{:S(2)}) collective-permute-start(bf16[96,768]{1,0:T(8,128)(2,1)S(1)} %get-tuple-element.159), channel_id=1, source_target_pairs={{0,4},{1,5},{2,6},{3,7},{4,0},{5,1},{6,2},{7,3},{8,12},{9,13},{10,... | collective-permute-start | bytes 442376 | tf_op jit(solution)/shard_map/ppermute | solution.py:152
  166.7 8.2 %collective-permute-start.45 = (bf16[96,768]{1,0:T(8,128)(2,1)S(1)}, bf16[96,768]{1,0:T(8,128)(2,1)S(1)}, u32[]{:S(2)}, u32[]{:S(2)}) collective-permute-start(bf16[96,768]{1,0:T(8,128)(2,1)S(1)} %get-tuple-element.157), channel_id=1, source_target_pairs={{0,6},{1,7},{2,4},{3,5},{4,2},{5,3},{6,0},{7,1},{8,14},{9,15},{10,... | collective-permute-start | bytes 442376 | tf_op jit(solution)/shard_map/ppermute | solution.py:152
  175.0 14.4 %collective-permute-start.51 = (bf16[2,192,768]{2,1,0:T(8,128)(2,1)S(1)}, bf16[2,192,768]{2,1,0:T(8,128)(2,1)S(1)}, u32[]{:S(2)}, u32[]{:S(2)}) collective-permute-start(bf16[2,192,768]{2,1,0:T(8,128)(2,1)S(1)} %pad_maximum_fusion.3), channel_id=1, source_target_pairs={{0,8},{1,9},{2,10},{3,11},{4,12},{5,13},{6,14},{7,15},{8,0},{9,1},... | collective-permute-start | bytes 1769480 | tf_op jit(solution)/shard_map/ppermute | solution.py:144
  (39 other events, 273.6 us)
